TPU v7x, 32 devices: a whole 2x2x4 slice. The times are simulated.
32 devices in a mesh: chan: 8 (over z, y), row: 4 (over x, core).
Axes of the slice: x: 2, y: 2, z: 4, core: 2. Of those that a mesh axis runs over, the one named last changes fastest.
Arguments:
- voltages: bfloat16 [2, 2, 128, 256], P(None, None, None, 'chan'), may hold values from -6 to 6
- kernel_table: bfloat16 [4, 16, 16], replicated, may hold values from -6 to 6
- station_rows: int32 [256], replicated, may hold values from 0 to 752
- station_cols: int32 [256], replicated, may hold values from 0 to 752
- kernel_offset: int32 [256], replicated, may hold values from 0 to 3
Outputs:
- taylor_images: float32 [3, 768, 768], P(None, 'chan', 'row')
Inputs may be any that keep to these rules, and one draw needn't show every extreme that they name: `station_rows`: kernels lie inside the grid. `station_cols`: kernels lie inside the grid.
All inputs are finite; a program needn't handle non-finite values.
Results may differ from a plain program's by a relative error of at most 0.0013.
Values may be sent and summed in bfloat16 or wider, within the bound.
No kernel may reach another device: no remote copies, remote signals or barrier semaphores. Data moves between devices by JAX's collectives and lax.ppermute only.
A program may use at most 128 MiB of HBM per device.

v0:
```python
import math

import jax
import jax.numpy as jnp
from jax import lax
from jax.sharding import PartitionSpec as P

S = 256
F = 128
G = 768
K = 16
NOFF = 4
TT = 2


def twiddles(length):
    index = jnp.arange(length, dtype=jnp.int32)
    product = index[:, None] * index[None, :] % length
    angle = 2.0 * jnp.pi / length * product.astype(jnp.float32)
    return (jnp.cos(angle).astype(jnp.bfloat16), jnp.sin(angle).astype(jnp.bfloat16))


def taylor_weights(count):
    chans = jnp.arange(count, dtype=jnp.int32).astype(jnp.float32)
    coord = (2.0 * chans + 1.0 - count) / count
    stacked = jnp.stack([jnp.ones_like(coord), coord, coord * coord])
    return stacked / jnp.sqrt(jnp.sum(stacked * stacked, axis=1, keepdims=True))


def grid_rows(volt_rows, kernels, station_rows, col_select, first_row, row_count):
    block_rows = math.gcd(row_count, 64)
    width = kernels.shape[1]
    cells = col_select.shape[2]
    offsets = jnp.arange(width, dtype=jnp.int32)
    local_rows = jnp.arange(block_rows, dtype=jnp.int32)

    def one_block(block_index, accum_grid):
        start_row = first_row + block_index * block_rows
        row_select = (
            (start_row + local_rows)[None, :, None]
            == station_rows[:, None, None] + offsets[None, None, :]
        ).astype(jnp.bfloat16)
        placed = jnp.einsum(
            "sra,sab->srb", row_select, kernels, preferred_element_type=jnp.float32
        ).astype(jnp.bfloat16)
        footprint = jnp.einsum(
            "srb,sbc->src", placed, col_select, preferred_element_type=jnp.float32
        ).astype(jnp.bfloat16)
        block_grid = jnp.einsum(
            "qs,src->qrc", volt_rows, footprint, preferred_element_type=jnp.float32
        )
        return lax.dynamic_update_slice_in_dim(accum_grid, block_grid, block_index * block_rows, 1)

    empty = jnp.zeros((volt_rows.shape[0], row_count, cells), jnp.float32)
    return lax.fori_loop(0, row_count // block_rows, one_block, empty)


def section_one(aperture, planes, cosine_table, sine_table):
    rows_here = aperture.shape[1]
    cells = aperture.shape[2]
    real_grid = aperture[:planes].reshape(planes * rows_here, cells)
    imag_grid = aperture[planes:].reshape(planes * rows_here, cells)
    real_half = jnp.dot(real_grid, cosine_table, preferred_element_type=jnp.float32) + jnp.dot(
        imag_grid, sine_table, preferred_element_type=jnp.float32
    )
    imag_half = jnp.dot(imag_grid, cosine_table, preferred_element_type=jnp.float32) - jnp.dot(
        real_grid, sine_table, preferred_element_type=jnp.float32
    )
    stacked = jnp.stack([real_half, imag_half]).astype(jnp.bfloat16)
    return stacked.reshape(2, planes, rows_here, cells)


def section_two(half, cosine_table, sine_table):
    real_half = half[0]
    imag_half = half[1]
    real_field = jnp.einsum(
        "ru,nrk->nuk", cosine_table, real_half, preferred_element_type=jnp.float32
    ) + jnp.einsum("ru,nrk->nuk", sine_table, imag_half, preferred_element_type=jnp.float32)
    imag_field = jnp.einsum(
        "ru,nrk->nuk", cosine_table, imag_half, preferred_element_type=jnp.float32
    ) - jnp.einsum("ru,nrk->nuk", sine_table, real_half, preferred_element_type=jnp.float32)
    return real_field * real_field + imag_field * imag_field


def local(voltages, kernel_table, station_rows, station_cols, kernel_offset):
    high = lax.Precision.HIGHEST
    chan_count = lax.axis_size("chan")
    row_count = lax.axis_size("row")
    chan_index = lax.axis_index("chan")
    row_index = lax.axis_index("row")
    chan_local = F // chan_count
    planes = TT * chan_local
    turned = lax.all_to_all(voltages, "chan", split_axis=2, concat_axis=3, tiled=True)
    cosine_table, sine_table = twiddles(G)
    variant = (kernel_offset[:, None] == jnp.arange(NOFF, dtype=jnp.int32)[None, :]).astype(
        jnp.bfloat16
    )
    kernels = jnp.dot(
        variant, kernel_table.reshape(NOFF, K * K), preferred_element_type=jnp.float32
    )
    kernels = kernels.astype(jnp.bfloat16).reshape(S, K, K)
    col_select = (
        jnp.arange(G, dtype=jnp.int32)[None, None, :]
        == station_cols[:, None, None] + jnp.arange(K, dtype=jnp.int32)[None, :, None]
    ).astype(jnp.bfloat16)
    weights = lax.dynamic_slice_in_dim(taylor_weights(F), chan_index * chan_local, chan_local, 1)
    scale = 1.0 / (TT * S * K * K)
    rows_local = G // row_count
    volt_rows = turned.reshape(2 * planes, S)
    aperture = grid_rows(
        volt_rows, kernels, station_rows, col_select, row_index * rows_local, rows_local
    ).astype(jnp.bfloat16)
    half = section_one(aperture, planes, cosine_table, sine_table)
    power = section_two(
        lax.all_to_all(half, "row", split_axis=3, concat_axis=2, tiled=True),
        cosine_table,
        sine_table,
    )
    power = jnp.sum(power.reshape(TT, chan_local, G, power.shape[2]), axis=0)
    partial_images = jnp.einsum("kf,frc->krc", weights, power, precision=high) * scale
    summed = lax.psum(partial_images, "chan")
    rows_owned = G // chan_count
    taylor_images = lax.dynamic_slice_in_dim(summed, chan_index * rows_owned, rows_owned, 1)
    return taylor_images


def solution(mesh):
    placed = (P(None, None, None, "chan"), P(), P(), P(), P())
    return jax.shard_map(
        local, mesh=mesh, in_specs=placed, out_specs=P(None, "chan", "row"), check_vma=False
    )
```

profile of v0, /device:TPU:0, one launch (start us, length us, event | category | flops | bytes accessed | tf_op | source)
XLA Modules:
  0.0 957.8 jit_solution(12506384431562230192)
XLA Ops:
  8.2 7.3 all-to-all-start
  22.5 6.8 broadcast_in_dim.8.clone
  29.3 163.8 %while.14 = (s32[]{:T(128)}, bf16[64,192,768]{2,1,0:T(8,128)(2,1)}, s32[]{:T(128)}, s32[256]{0:T(256)S(1)}, bf16[256,16,16]{1,2,0:T(8,128)(2,1)}, /*index=5*/bf1...) while((s32[]{:T(128)}, bf16[64,192,768]{2,1,0:T(8,128)(2,1)}, ...), condition=%wide.region_2.3_spmd.clone, body=%wide.region_1.2_spmd.clone.sunk | while | flops 2041057280 | bytes 69420720 | solution.py:55
  29.5 12.7 %convolution_convert_fusion.3 = bf16[256,64,768]{2,1,0:T(8,128)(2,1)} fusion(s32[256,16]{1,0:T(8,128)S(1)} %get-tuple-element.284, bf16[256,16,16]{1,2,0:T(8,128)(2,1)} %get-tuple-element.282, s32[256,16]{1,0:T(8,128)S(1)} %iota_add_fusion.5, s32[64]{0:T(128)S(1)} %iota_add_fusion.6), kind=kOutput, calls=%fused_computation.5.clone.1 | convolution fusion | flops 430440448 | bytes 25329920 | tf_op jit(solution)/shard_map/while/body/eval_jaxpr/srb,sbc->src/dot_general | solution.py:46
  42.1 35.5 %fusion.98 = bf16[64,64,768]{2,0,1:T(8,128)(2,1)S(1)} fusion(bf16[256,64,768]{2,1,0:T(8,128)(2,1)} %convolution_convert_fusion.3, bf16[64,256]{1,0:T(8,128)(2,1)S(1)} %get-tuple-element.283), kind=kOutput, calls=%fused_computation.10.clone.1 | convolution fusion | flops 1610612736 | bytes 31490048 | tf_op jit(solution)/shard_map/while/body/eval_jaxpr/qs,src->qrc/dot_general | solution.py:49
  77.6 6.2 copy_dynamic-update-slice_fusion.2
  83.9 12.7 %convolution_convert_fusion.3 = bf16[256,64,768]{2,1,0:T(8,128)(2,1)} fusion(s32[256,16]{1,0:T(8,128)S(1)} %get-tuple-element.284, bf16[256,16,16]{1,2,0:T(8,128)(2,1)} %get-tuple-element.282, s32[256,16]{1,0:T(8,128)S(1)} %iota_add_fusion.5, s32[64]{0:T(128)S(1)} %iota_add_fusion.6), kind=kOutput, calls=%fused_computation.5.clone.1 | convolution fusion | flops 430440448 | bytes 25329920 | tf_op jit(solution)/shard_map/while/body/eval_jaxpr/srb,sbc->src/dot_general | solution.py:46
  96.6 35.5 %fusion.98 = bf16[64,64,768]{2,0,1:T(8,128)(2,1)S(1)} fusion(bf16[256,64,768]{2,1,0:T(8,128)(2,1)} %convolution_convert_fusion.3, bf16[64,256]{1,0:T(8,128)(2,1)S(1)} %get-tuple-element.283), kind=kOutput, calls=%fused_computation.10.clone.1 | convolution fusion | flops 1610612736 | bytes 31490048 | tf_op jit(solution)/shard_map/while/body/eval_jaxpr/qs,src->qrc/dot_general | solution.py:49
  138.4 12.7 %convolution_convert_fusion.3 = bf16[256,64,768]{2,1,0:T(8,128)(2,1)} fusion(s32[256,16]{1,0:T(8,128)S(1)} %get-tuple-element.284, bf16[256,16,16]{1,2,0:T(8,128)(2,1)} %get-tuple-element.282, s32[256,16]{1,0:T(8,128)S(1)} %iota_add_fusion.5, s32[64]{0:T(128)S(1)} %iota_add_fusion.6), kind=kOutput, calls=%fused_computation.5.clone.1 | convolution fusion | flops 430440448 | bytes 25329920 | tf_op jit(solution)/shard_map/while/body/eval_jaxpr/srb,sbc->src/dot_general | solution.py:46
  151.1 35.5 %fusion.98 = bf16[64,64,768]{2,0,1:T(8,128)(2,1)S(1)} fusion(bf16[256,64,768]{2,1,0:T(8,128)(2,1)} %convolution_convert_fusion.3, bf16[64,256]{1,0:T(8,128)(2,1)S(1)} %get-tuple-element.283), kind=kOutput, calls=%fused_computation.10.clone.1 | convolution fusion | flops 1610612736 | bytes 31490048 | tf_op jit(solution)/shard_map/while/body/eval_jaxpr/qs,src->qrc/dot_general | solution.py:49
  186.6 6.2 copy_dynamic-update-slice_fusion.2
  193.2 8.1 fusion.76
  201.3 18.2 %fusion.44 = f32[6144,768]{1,0:T(8,128)} fusion(bf16[6144,768]{1,0:T(8,128)(2,1)S(1)} %bitcast.60), kind=kOutput, calls=%fused_computation.44 | convolution fusion | flops 7253655552 | bytes 28311552 | tf_op jit(solution)/shard_map/dot_general | solution.py:63
  219.5 18.3 %fusion.43 = f32[6144,768]{1,0:T(8,128)} fusion(bf16[6144,768]{1,0:T(8,128)(2,1)S(1)} %bitcast.62), kind=kOutput, calls=%fused_computation.43 | convolution fusion | flops 7253655552 | bytes 28311552 | tf_op jit(solution)/shard_map/dot_general | solution.py:66
  237.8 20.7 %add_convert_fusion = bf16[6144,768]{1,0:T(8,128)(2,1)} fusion(f32[6144,768]{1,0:T(8,128)} %fusion.44, bf16[6144,768]{1,0:T(8,128)(2,1)S(1)} %bitcast.63), kind=kOutput, calls=%fused_computation.23 | convolution fusion | flops 7263092736 | bytes 37748736 | tf_op jit(solution)/shard_map/dot_general | solution.py:63
  258.6 17.4 %copy.28 = bf16[1,32,192,768]{2,1,0,3:T(8,128)(2,1)} copy(bf16[1,32,192,768]{3,2,1,0:T(8,128)(2,1)} %bitcast.64) | data formatting | bytes 18874368 | tf_op jit(solution)/shard_map/stack | solution.py:69
  276.0 22.4 %subtract_convert_fusion = bf16[6144,768]{1,0:T(8,128)(2,1)} fusion(f32[6144,768]{1,0:T(8,128)} %fusion.43, bf16[6144,768]{1,0:T(8,128)(2,1)} %bitcast.61), kind=kOutput, calls=%fused_computation.22 | convolution fusion | flops 7263092736 | bytes 37748736 | tf_op jit(solution)/shard_map/dot_general | solution.py:66
  298.4 17.5 %copy.29 = bf16[1,32,192,768]{2,1,0,3:T(8,128)(2,1)} copy(bf16[1,32,192,768]{3,2,1,0:T(8,128)(2,1)} %bitcast.65) | data formatting | bytes 18874368 | tf_op jit(solution)/shard_map/stack | solution.py:69
  315.9 21.2 %pad_maximum_fusion = bf16[2,32,192,768]{2,1,0,3:T(8,128)(2,1)} fusion(bf16[1,32,192,768]{2,1,0,3:T(8,128)(2,1)} %copy.29, bf16[1,32,192,768]{2,1,0,3:T(8,128)(2,1)} %copy.28), kind=kLoop, calls=%fused_computation.19 | loop fusion | flops 9437184 | bytes 37748736 | tf_op jit(solution)/shard_map/stack | solution.py:69
  337.1 8.5 all-to-all-start.1
  346.1 272.4 %all-to-all-done.1 = bf16[2,32,192,768]{2,1,0,3:T(8,128)(2,1)} async-done(((bf16[2,32,192,768]{2,1,0,3:T(8,128)(2,1)}), bf16[2,32,192,768]{2,1,0,3:T(8,128)(2,1)}, u32[]{:S(2)}, u32[]{:S(2)}) %all-to-all-start.1) | async-done | bytes 18874400 | tf_op jit(solution)/shard_map/all_to_all | solution.py:115
  618.5 32.4 %copy.47 = bf16[2,32,192,4,192]{2,3,4,1,0:T(4,128)(2,1)} copy(bf16[2,32,192,4,192]{2,1,0,4,3:T(8,128)(2,1)} %bitcast.8) | data formatting | bytes 37748736 | tf_op jit(solution)/shard_map/all_to_all | solution.py:115
  650.9 23.7 %fusion.75 = (bf16[1,32,4,192,192]{3,2,4,1,0:T(4,128)(2,1)}, bf16[1,32,4,192,192]{3,2,4,1,0:T(4,128)(2,1)}) fusion(bf16[2,32,4,192,192]{3,2,4,1,0:T(4,128)(2,1)} %bitcast.58), kind=kLoop, calls=%fused_computation.82 | loop fusion | bytes 37748736 | tf_op jit(solution)/shard_map/slice | solution.py:74
  674.6 21.8 %squeeze.7 = bf16[32,768,192]{1,2,0:T(8,128)(2,1)} reshape(bf16[1,32,4,192,192]{3,2,4,1,0:T(4,128)(2,1)} %get-tuple-element.208) | data formatting | bytes 18874368 | tf_op jit(solution)/shard_map/squeeze | solution.py:75
  696.4 21.6 %fusion.37 = f32[32,192,768]{2,1,0:T(8,128)} fusion(bf16[32,768,192]{1,2,0:T(8,128)(2,1)} %squeeze.7), kind=kOutput, calls=%fused_computation.37 | convolution fusion | flops 7253655552 | bytes 28311552 | tf_op jit(solution)/shard_map/ru,nrk->nuk/dot_general | solution.py:78
  718.0 18.7 %fusion.39 = f32[32,192,768]{2,1,0:T(8,128)} fusion(bf16[32,768,192]{1,2,0:T(8,128)(2,1)S(1)} %copy-done.1), kind=kOutput, calls=%fused_computation.39 | convolution fusion | flops 7253655552 | bytes 28311552 | tf_op jit(solution)/shard_map/ru,nrk->nuk/dot_general | solution.py:79
  736.7 21.8 %squeeze.6 = bf16[32,768,192]{1,2,0:T(8,128)(2,1)} reshape(bf16[1,32,4,192,192]{3,2,4,1,0:T(4,128)(2,1)} %get-tuple-element.207) | data formatting | bytes 18874368 | tf_op jit(solution)/shard_map/squeeze | solution.py:74
  758.5 21.3 %fusion.41 = f32[32,192,768]{2,1,0:T(8,128)} fusion(bf16[32,768,192]{1,2,0:T(8,128)(2,1)} %squeeze.6), kind=kOutput, calls=%fused_computation.41 | convolution fusion | flops 7253655552 | bytes 28311552 | tf_op jit(solution)/shard_map/ru,nrk->nuk/dot_general | solution.py:76
  779.8 34.8 %multiply_add_fusion = f32[32,192,768]{2,1,0:T(8,128)} fusion(f32[32,192,768]{2,1,0:T(8,128)} %fusion.39, f32[32,192,768]{2,1,0:T(8,128)} %fusion.41, f32[32,192,768]{2,1,0:T(8,128)} %fusion.37, bf16[32,768,192]{1,2,0:T(8,128)(2,1)} %squeeze.6), kind=kOutput, calls=%fused_computation.21 | convolution fusion | flops 7277248512 | bytes 84934656 | tf_op jit(solution)/shard_map/ru,nrk->nuk/dot_general | solution.py:81
  814.6 11.5 %reduce_sum.19 = f32[16,768,192]{1,2,0:T(8,128)} reduce(f32[2,16,768,192]{2,3,1,0:T(8,128)} %bitcast.59, f32[]{:T(128)} %constant.64.clone.1), dimensions={0}, to_apply=%region_3.4 | reduce | flops 2359296 | bytes 28311556 | tf_op jit(solution)/shard_map/reduce_sum | solution.py:119
  826.1 15.1 %fusion.33 = f32[3,768,192]{1,0,2:T(4,128)} fusion(f32[16,768,192]{1,2,0:T(8,128)} %reduce_sum.19, f32[3,128]{1,0:T(4,128)S(1)} %fusion.48, s32[]{:T(128)S(6)} %select_n.34), kind=kOutput, calls=%fused_computation.35 | convolution fusion | flops 85377024 | bytes 11208196 | tf_op jit(solution)/shard_map/kf,frc->krc/dot_general | solution.py:120
  841.2 107.1 %all-reduce.2.cloned.1.call-done = f32[3,768,192]{1,0,2:T(4,128)} async-done(((f32[3,768,192]{1,0,2:T(4,128)}), f32[3,768,192]{1,0,2:T(4,128)}) %all-reduce.2.cloned.1.call-update) | async-done | bytes 1769488 | tf_op jit(solution)/shard_map/psum | solution.py:121
  (33 shorter events, 18.0 us)
Async XLA Ops:
  8.2 14.0 %all-to-all-start = ((bf16[8,2,1024]{2,1,0:T(2,128)(2,1)}), bf16[8,2,1024]{2,1,0:T(2,128)(2,1)S(1)}, u32[]{:S(2)}, u32[]{:S(2)}) async-start(bf16[8,2,1024]{2,1,0:T(2,128)(2,1)} %reshape.124), calls=%async_computation | async-start | bytes 65536 | tf_op jit(solution)/shard_map/all_to_all | solution.py:93
  22.5 6.8 copy-start.2
  201.3 18.2 %copy-start = (bf16[32,192,768]{2,1,0:T(8,128)(2,1)}, bf16[32,192,768]{2,1,0:T(8,128)(2,1)S(1)}, u32[]{:S(2)}) copy-start(bf16[32,192,768]{2,1,0:T(8,128)(2,1)S(1)} %get-tuple-element.209) | copy-start | bytes 28311556
  337.1 281.4 %all-to-all-start.1 = ((bf16[2,32,192,768]{2,1,0,3:T(8,128)(2,1)}), bf16[2,32,192,768]{2,1,0,3:T(8,128)(2,1)}, u32[]{:S(2)}, u32[]{:S(2)}) async-start(bf16[2,32,192,768]{2,1,0,3:T(8,128)(2,1)} %pad_maximum_fusion), calls=%async_computation.1 | async-start | bytes 50331648 | tf_op jit(solution)/shard_map/all_to_all | solution.py:115
  345.6 602.8 %all-reduce.2.cloned.1.call-start = ((), (), s32[]{:S(2)}) async-start(), calls=%async_computation.2 | async-start | bytes 4718592 | tf_op jit(solution)/shard_map/psum | solution.py:121
  696.4 21.6 %copy-start.1 = (bf16[32,768,192]{1,2,0:T(8,128)(2,1)S(1)}, bf16[32,768,192]{1,2,0:T(8,128)(2,1)}, u32[]{:S(2)}) copy-start(bf16[32,768,192]{1,2,0:T(8,128)(2,1)} %squeeze.7) | copy-start | bytes 28311556
Sparse Core Ops, SparseCore 0:
  841.3 106.9 all-reduce.1
where the time goes:
time: 960 us; the launch traced here: 958 us
  waiting for transfers between devices  382 us (40%)
  matrix products  337 us (35%)
  local copies, waits for them, and re-layouts  175 us (18%)
  other arithmetic  34.1 us (4%)
  starting transfers between devices  16 us (2%)
  between operations  13.8 us (1%)
    all_to_all x1, waiting for transfers between devices, local(): lax.all_to_all(half, 'row', split_axis=3, concat_axis=2, tiled=True)  272 us
    psum x1, waiting for transfers between devices, local(): summed = lax.psum(partial_images, 'chan')  107 us
    dot_general x3, matrix products, one_block(): jnp.einsum('qs,src->qrc', volt_rows, footprint, preferred_element_type=jn...  107 us
    dot_general x3, matrix products, one_block(): jnp.einsum('srb,sbc->src', placed, col_select, preferred_element_type=jnp...  38 us
    another operation x2, local copies, waits for them, and re-layouts, section_one(): stacked = jnp.stack([real_half, imag_half]).astype(jnp.bfloat16)  34.9 us
    dot_general x1, matrix products, section_two(): jnp.einsum('ru,nrk->nuk', sine_table, real_half, preferred_element_type=j...  34.8 us
    all_to_all x1, local copies, waits for them, and re-layouts, local(): lax.all_to_all(half, 'row', split_axis=3, concat_axis=2, tiled=True)  32.4 us
    slice x1, local copies, waits for them, and re-layouts, section_two(): real_half = half[0]  23.7 us
  transfers between devices with their start and end apart: 3, of which 3 were waited for; matrix products, arithmetic and copies ran while one was open for 0% of the time, Pallas kernels for 0%

commit v1 on v0

v1 whole, which is shorter than its diff:
```python
import jax
import jax.numpy as jnp
import numpy as np
from jax import lax
from jax.experimental import pallas as pl
from jax.experimental.pallas import tpu as pltpu
from jax.sharding import PartitionSpec as P

TILE = 256
STEP = 4


def wave_fit(terms=8):
    nodes = 0.125 + 0.125 * np.cos(np.pi * (np.arange(200) + 0.5) / 200)
    root = np.sqrt(nodes)
    fit = np.polynomial.polynomial.polyfit
    cosine = fit(nodes, np.cos(2 * np.pi * root), terms - 1)
    sine = fit(nodes, np.sin(2 * np.pi * root) / root, terms - 1)
    return [float(c) for c in cosine], [float(c) for c in sine]


COS_FIT, SIN_FIT = wave_fit()


def horner(coefs, x):
    value = jnp.full_like(x, coefs[-1])
    for c in coefs[-2::-1]:
        value = value * x + c
    return value


def wave(product, cells):
    turns = product * (1.0 / cells)
    part = (product - cells * jnp.round(turns)) * (1.0 / cells)
    square = part * part
    return horner(COS_FIT, square), -part * horner(SIN_FIT, square)


def image_kernel(
    cells, width, volts, rows, cols, variant, first_col, phase_re, phase_im, spread_re, spread_im,
    coord, out, volt_re, volt_im, base_re, base_im, pick, x_a, x_b, h_a, h_b,
):
    stations = rows.shape[0]
    planes = volts.shape[0] // 2
    lanes = STEP * width
    steps = phase_re.shape[0]
    chans = coord.shape[0]
    volt_re[...] = volts[:planes, :].astype(jnp.float32)
    volt_im[...] = volts[planes:, :].astype(jnp.float32)
    pick[...] = jnp.broadcast_to(variant[...], (stations, 128))
    row_of = jnp.broadcast_to(rows[...].astype(jnp.float32), (stations, 128))
    col_of = jnp.broadcast_to(cols[...].astype(jnp.float32), (stations, 128))
    first = first_col[0].astype(jnp.float32)
    for tile in range(lanes // 128):
        place = lax.broadcasted_iota(jnp.int32, (stations, 128), 1) + tile * 128
        down = jnp.zeros((stations, 128), jnp.float32)
        for p in range(1, STEP):
            down = jnp.where(place >= p * width, float(p), down)
        across = place.astype(jnp.float32) - down * width + first
        real, imag = wave(row_of * down + col_of * across, cells)
        base_re[:, tile * 128:(tile + 1) * 128] = real
        base_im[:, tile * 128:(tile + 1) * 128] = imag

    def prepare(q, x_out, h_out):
        pr = phase_re[pl.ds(q, 1), :]
        pi = phase_im[pl.ds(q, 1), :]
        vr = volt_re[...]
        vi = volt_im[...]
        xr = (vr * pr - vi * pi).astype(jnp.bfloat16)
        xi = (vr * pi + vi * pr).astype(jnp.bfloat16)
        x_out[:planes, :stations] = xr
        x_out[:planes, stations:] = -xi
        x_out[planes:, :stations] = xi
        x_out[planes:, stations:] = xr
        for tile in range(lanes // 128):
            at = slice(tile * 128, (tile + 1) * 128)
            gr = spread_re[q, :, at]
            gi = spread_im[q, :, at]
            for group in range(stations // 16):
                parts_re = []
                parts_im = []
                for half in range(2):
                    sub = slice(group * 16 + half * 8, group * 16 + half * 8 + 8)
                    index = pick[sub, :]
                    sr = jnp.take_along_axis(gr, index, axis=0)
                    si = jnp.take_along_axis(gi, index, axis=0)
                    br = base_re[sub, at]
                    bi = base_im[sub, at]
                    parts_re.append(br * sr - bi * si)
                    parts_im.append(br * si + bi * sr)
                pair = slice(group * 16, group * 16 + 16)
                low = slice(stations + group * 16, stations + group * 16 + 16)
                h_out[pair, at] = jnp.concatenate(parts_re, axis=0).astype(jnp.bfloat16)
                h_out[low, at] = jnp.concatenate(parts_im, axis=0).astype(jnp.bfloat16)

    def finish(q, x_in, h_in):
        for tile in range(lanes // TILE):
            at = slice(tile * TILE, (tile + 1) * TILE)
            field = jnp.dot(x_in[...], h_in[:, at], preferred_element_type=jnp.float32)
            power = field * field
            total = power[:planes] + power[planes:]
            total = total[:chans] + total[chans:]
            x = jnp.concatenate([coord[...]] * (TILE // 128), axis=1)
            first_order = total * x
            second_order = first_order * x
            for k, value in enumerate((total, first_order, second_order)):
                out[q, k:k + 1, at] = jnp.sum(value, axis=0, keepdims=True)

    prepare(0, x_a, h_a)

    def two(i, carry):
        prepare(2 * i + 1, x_b, h_b)
        finish(2 * i, x_a, h_a)
        prepare(jnp.minimum(2 * i + 2, steps - 1), x_a, h_a)
        finish(2 * i + 1, x_b, h_b)
        return carry

    lax.fori_loop(0, steps // 2, two, 0)


def angle_of(product, cells):
    return (product % cells).astype(jnp.float32) * (2.0 * np.pi / cells)


def local(cells, voltages, kernel_table, station_rows, station_cols, kernel_offset):
    high = lax.Precision.HIGHEST
    times, chans = voltages.shape[1], voltages.shape[2]
    stations = station_rows.shape[0]
    variants, width_k = kernel_table.shape[0], kernel_table.shape[1]
    height = cells // lax.axis_size("chan")
    width = cells // lax.axis_size("row")
    first_row = lax.axis_index("chan") * height
    first_col = lax.axis_index("row") * width
    steps = height // STEP
    lanes = STEP * width

    planes = times * chans
    gathered = lax.all_gather(voltages.reshape(2 * planes, voltages.shape[3]), "chan", axis=1, tiled=True)

    start = first_row + STEP * jnp.arange(steps, dtype=jnp.int32)
    turn = angle_of(start[:, None] * station_rows[None, :], cells)
    phase_re, phase_im = jnp.cos(turn), -jnp.sin(turn)

    taps = jnp.arange(width_k, dtype=jnp.int32)
    turn_u = angle_of((first_row + jnp.arange(height, dtype=jnp.int32))[:, None] * taps[None, :], cells)
    turn_v = angle_of((first_col + jnp.arange(width, dtype=jnp.int32))[:, None] * taps[None, :], cells)
    table = kernel_table.astype(jnp.float32)
    half_re = jnp.einsum("oab,vb->oav", table, jnp.cos(turn_v), precision=high)
    half_im = -jnp.einsum("oab,vb->oav", table, jnp.sin(turn_v), precision=high)
    cu, su = jnp.cos(turn_u), jnp.sin(turn_u)
    spread_re = jnp.einsum("ua,oav->uov", cu, half_re, precision=high) + jnp.einsum(
        "ua,oav->uov", su, half_im, precision=high
    )
    spread_im = jnp.einsum("ua,oav->uov", cu, half_im, precision=high) - jnp.einsum(
        "ua,oav->uov", su, half_re, precision=high
    )

    def pack(s):
        s = s.reshape(steps, STEP, variants, width).transpose(0, 2, 1, 3).reshape(steps, variants, lanes)
        return jnp.pad(s, ((0, 0), (0, 8 - variants), (0, 0)))

    x = (2.0 * np.arange(chans) + 1.0 - chans) / chans
    coord = jnp.asarray(np.broadcast_to(x[:, None], (chans, 128)), jnp.float32)
    vmem = pl.BlockSpec(memory_space=pltpu.VMEM)
    smem = pl.BlockSpec(memory_space=pltpu.SMEM)
    raw = pl.pallas_call(
        lambda *refs: image_kernel(cells, width, *refs),
        out_shape=jax.ShapeDtypeStruct((steps, 3, lanes), jnp.float32),
        in_specs=[vmem, vmem, vmem, vmem, smem, vmem, vmem, vmem, vmem, vmem],
        out_specs=vmem,
        scratch_shapes=[
            pltpu.VMEM((planes, stations), jnp.float32),
            pltpu.VMEM((planes, stations), jnp.float32),
            pltpu.VMEM((stations, lanes), jnp.float32),
            pltpu.VMEM((stations, lanes), jnp.float32),
            pltpu.VMEM((stations, 128), jnp.int32),
            pltpu.VMEM((2 * planes, 2 * stations), jnp.bfloat16),
            pltpu.VMEM((2 * planes, 2 * stations), jnp.bfloat16),
            pltpu.VMEM((2 * stations, lanes), jnp.bfloat16),
            pltpu.VMEM((2 * stations, lanes), jnp.bfloat16),
        ],
        compiler_params=pltpu.CompilerParams(vmem_limit_bytes=40 * 1024 * 1024),
    )(
        gathered, station_rows[:, None], station_cols[:, None], kernel_offset[:, None],
        first_col.reshape(1).astype(jnp.int32), phase_re, phase_im, pack(spread_re), pack(spread_im), coord,
    )
    norm = np.array([1.0 / np.sqrt(np.sum(x ** (2 * k))) for k in range(3)]) / (times * stations * width_k * width_k)
    images = raw.reshape(steps, 3, STEP, width).transpose(1, 0, 2, 3).reshape(3, height, width)
    return images * jnp.asarray(norm, jnp.float32)[:, None, None]


def solution(mesh):
    cells = 768
    placed = (P(None, None, None, "chan"), P(), P(), P(), P())
    return jax.shard_map(
        lambda *args: local(cells, *args), mesh=mesh, in_specs=placed, out_specs=P(None, "chan", "row"), check_vma=False
    )
```

time: 960 us -> 63.5 us (0.07)
  waiting for transfers between devices: 382 us -> 0 us
  matrix products: 337 us -> 2.79 us
  local copies, waits for them, and re-layouts: 175 us -> 5.7 us
  other arithmetic: 34.1 us -> 1 us
  blocking collectives: 0 us -> 32.5 us
  Pallas kernels: 0 us -> 21 us
  starting transfers between devices: 16 us -> 0 us
  between operations: 13.8 us -> 0.23 us
    dot_general x16 -> x6, matrix products: 337 us -> 2.79 us  [the longest x1 0.57 us: local(): jnp.einsum('ua,oav->uov', su, half_re, precision=high)]
    all_to_all x2 -> x0, waiting for transfers between devices: 275 us -> none  [the longest x1 272 us: local(): lax.all_to_all(half, 'row', split_axis=3, concat_axis=2, tiled=True)]
    psum x1 -> x0, waiting for transfers between devices: 107 us -> none  [local(): summed = lax.psum(partial_images, 'chan')]
    squeeze x2 -> x0, local copies, waits for them, and re-layouts: 43.6 us -> none  [the longest x1 21.8 us: section_two(): real_half = half[0]]
    another operation x3 -> x0, local copies, waits for them, and re-layouts: 34.9 us -> none  [the longest x2 34.9 us: section_one(): stacked = jnp.stack([real_half, imag_half]).astype(jnp.bfloat16)]
    all_gather x0 -> x1, blocking collectives: none -> 32.5 us  [local(): lax.all_gather(voltages.reshape(2 * planes, voltages.shape[3]), 'chan', a...]
    all_to_all x3 -> x0, local copies, waits for them, and re-layouts: 32.4 us -> none  [the longest x1 32.4 us: local(): lax.all_to_all(half, 'row', split_axis=3, concat_axis=2, tiled=True)]
    slice x2 -> x0, local copies, waits for them, and re-layouts: 31.8 us -> none  [the longest x1 23.7 us: section_two(): real_half = half[0]]
  transfers between devices with their start and end apart: 3 -> 0, of which waited for: 3 -> 0; matrix products, arithmetic and copies ran while one was open for 0% -> 0% of each run, Pallas kernels for 0% -> 0%
where the time goes in v1:
time: 63.5 us; the launch traced here: 63.2 us
  blocking collectives  32.5 us (51%)
  Pallas kernels  21 us (33%)
  local copies, waits for them, and re-layouts  5.7 us (9%)
  matrix products  2.79 us (4%)
  other arithmetic  1 us (2%)
    all_gather x1, blocking collectives, local(): lax.all_gather(voltages.reshape(2 * planes, voltages.shape[3]), 'chan', a...  32.5 us
    pallas_call x1, Pallas kernels, local(): pl.pallas_call(lambda *refs: image_kernel(cells, width, *refs), out_shape...  21 us
    unnamed x13, local copies, waits for them, and re-layouts  3.72 us

profile of v1, /device:TPU:0, one launch (start us, length us, event | category | flops | bytes accessed | tf_op | source)
XLA Modules:
  0.0 63.2 jit_solution(13813775237052365066)
XLA Ops:
  0.0 0.0 copy-start
  0.0 0.8 %copy.19 = bf16[2,2,128,32]{2,1,0,3:T(2,128)(2,1)S(1)} copy(bf16[2,2,128,32]{2,3,1,0:T(8,128)(2,1)} %param.7) | data formatting | bytes 65536 | tf_op args[0]
  0.8 0.0 copy-start.2
  0.9 0.6 %copy-done.2 = s32[256]{0:T(256)S(1)} copy-done((s32[256]{0:T(256)S(1)}, s32[256]{0:T(256)}, u32[]{:S(2)}) %copy-start.2) | copy-done | bytes 1048
  1.5 0.2 sine_negate_fusion
  1.7 0.0 copy-done
  1.7 0.2 fusion
  1.9 0.0 copy-start.3
  2.0 0.2 convolution_bitcast_fusion
  2.2 0.4 copy-done.3
  2.6 0.1 copy.24.refs_2_
  2.8 0.5 copy-done.4
  3.3 0.1 copy.25.refs_3_
  3.5 0.1 copy.23.refs_1_
  3.6 32.5 %all_gather.3 = bf16[512,256]{0,1:T(8,128)(2,1)S(1)} all-gather(bf16[512,32]{0,1:T(8,128)(2,1)S(1)} %reshape.39), channel_id=1, replica_groups=mesh['chan'=8,'row'=4] {'chan'}, dimensions={1}, use_global_device_ids=true | all-gather | bytes 294912 | tf_op jit(solution)/shard_map/all_gather | solution.py:138
  36.1 0.1 copy.22.refs_0_
  36.3 0.6 fusion.24
  36.9 0.6 convolution_add_fusion
  37.4 0.1 reshape.41
  37.6 0.3 reshape.42
  38.0 0.6 fusion.22
  38.6 0.6 convolution_subtract_fusion
  39.2 0.1 reshape.43
  39.3 0.3 reshape.44
  39.7 0.0 copy-start.1
  39.7 0.8 %copy-done.1 = f32[128,128]{1,0:T(8,128)S(1)} copy-done((f32[128,128]{1,0:T(8,128)S(1)}, f32[128,128]{1,0:T(8,128)}, u32[]{:S(2)}) %copy-start.1) | copy-done | bytes 65560
  40.5 21.0 %shard_map.73 = f32[24,3,768]{2,1,0:T(4,128)S(1)} custom-call(bf16[512,256]{1,0:T(8,128)(2,1)S(1)} %copy.22.refs_0_, s32[256,1]{1,0:T(8,128)S(1)} %copy.23.refs_1_, s32[256,1]{1,0:T(8,128)S(1)} %copy.24.refs_2_, s32[256,1]{1,0:T(8,128)S(1)} %copy.25.refs_3_, s32[1]{0:T(128)} %bitcast.3.refs_4_, f32[24,256]{1,0:T(8,128)S(1)} %get-tuple-element.6.refs_5_, ...), custom_call_target="tpu_custom_call" | custom-call | tf_op jit(solution)/shard_map/pallas_call | solution.py:166
  61.5 0.2 reshape.45
  61.8 0.0 copy-start.5
  61.8 0.1 reshape.46
  61.9 0.5 copy-done.5
  62.4 0.8 %broadcast_multiply_fusion = f32[3,96,192]{2,1,0:T(8,128)} fusion(f32[3,96,192]{2,1,0:T(8,128)S(1)} %reshape.46, f32[3]{0:T(128)S(1)} %copy-done.5), kind=kLoop, calls=%fused_computation.7 | loop fusion | flops 55296 | bytes 442380 | tf_op jit(solution)/shard_map/mul | solution.py:189
  (10 shorter events, 0.2 us)
Async XLA Ops:
  0.0 1.7 %copy-start = (bf16[4,16,16]{2,1,0:T(8,128)(2,1)S(1)}, bf16[4,16,16]{2,1,0:T(8,128)(2,1)}, u32[]{:S(2)}) copy-start(bf16[4,16,16]{2,1,0:T(8,128)(2,1)} %param.8) | copy-start | bytes 6148
  0.8 0.7 %copy-start.2 = (s32[256]{0:T(256)S(1)}, s32[256]{0:T(256)}, u32[]{:S(2)}) copy-start(s32[256]{0:T(256)} %param.9) | copy-start | bytes 3076
  1.9 0.7 %copy-start.3 = (s32[256]{0:T(256)S(1)}, s32[256]{0:T(256)}, u32[]{:S(2)}) copy-start(s32[256]{0:T(256)} %param.10) | copy-start | bytes 3076
  2.6 0.7 %copy-start.4 = (s32[256]{0:T(256)S(1)}, s32[256]{0:T(256)}, u32[]{:S(2)}) copy-start(s32[256]{0:T(256)} %param.11) | copy-start | bytes 3076
  39.7 0.8 %copy-start.1 = (f32[128,128]{1,0:T(8,128)S(1)}, f32[128,128]{1,0:T(8,128)}, u32[]{:S(2)}) copy-start(f32[128,128]{1,0:T(8,128)} %constant.50.clone.refs_9_) | copy-start | bytes 196612
  61.8 0.7 %copy-start.5 = (f32[3]{0:T(128)S(1)}, f32[3]{0:T(128)}, u32[]{:S(2)}) copy-start(f32[3]{0:T(128)} %constant.51.clone) | copy-start | bytes 40

commit v2 on v1

v2 whole, which is shorter than its diff:
```python
import jax
import jax.numpy as jnp
import numpy as np
from jax import lax
from jax.experimental import pallas as pl
from jax.experimental.pallas import tpu as pltpu
from jax.sharding import PartitionSpec as P

TILE = 256
STEP = 4


def wave_fit(terms=8):
    nodes = 0.125 + 0.125 * np.cos(np.pi * (np.arange(200) + 0.5) / 200)
    root = np.sqrt(nodes)
    fit = np.polynomial.polynomial.polyfit
    cosine = fit(nodes, np.cos(2 * np.pi * root), terms - 1)
    sine = fit(nodes, np.sin(2 * np.pi * root) / root, terms - 1)
    return [float(c) for c in cosine], [float(c) for c in sine]


COS_FIT, SIN_FIT = wave_fit()


def horner(coefs, x):
    value = jnp.full_like(x, coefs[-1])
    for c in coefs[-2::-1]:
        value = value * x + c
    return value


def wave(product, cells):
    turns = product * (1.0 / cells)
    part = (product - cells * jnp.round(turns)) * (1.0 / cells)
    square = part * part
    return horner(COS_FIT, square), -part * horner(SIN_FIT, square)


def response_kernel(
    cells, width, rows, cols, variant, first_col, spread_re, spread_im, response, base_re, base_im, pick
):
    stations = rows.shape[0]
    lanes = STEP * width

    @pl.when(pl.program_id(0) == 0)
    def _():
        pick[...] = jnp.broadcast_to(variant[...], (stations, 128))
        row_of = jnp.broadcast_to(rows[...].astype(jnp.float32), (stations, 128))
        col_of = jnp.broadcast_to(cols[...].astype(jnp.float32), (stations, 128))
        first = first_col[0].astype(jnp.float32)
        for tile in range(lanes // 128):
            place = lax.broadcasted_iota(jnp.int32, (stations, 128), 1) + tile * 128
            down = jnp.zeros((stations, 128), jnp.float32)
            for p in range(1, STEP):
                down = jnp.where(place >= p * width, float(p), down)
            across = place.astype(jnp.float32) - down * width + first
            real, imag = wave(row_of * down + col_of * across, cells)
            base_re[:, tile * 128:(tile + 1) * 128] = real
            base_im[:, tile * 128:(tile + 1) * 128] = imag

    for tile in range(lanes // 128):
        at = slice(tile * 128, (tile + 1) * 128)
        gr = spread_re[0, :, at]
        gi = spread_im[0, :, at]
        for group in range(stations // 16):
            parts_re = []
            parts_im = []
            for half in range(2):
                sub = slice(group * 16 + half * 8, group * 16 + half * 8 + 8)
                index = pick[sub, :]
                sr = jnp.take_along_axis(gr, index, axis=0)
                si = jnp.take_along_axis(gi, index, axis=0)
                br = base_re[sub, at]
                bi = base_im[sub, at]
                parts_re.append(br * sr - bi * si)
                parts_im.append(br * si + bi * sr)
            pair = slice(group * 16, group * 16 + 16)
            low = slice(stations + group * 16, stations + group * 16 + 16)
            response[0, pair, at] = jnp.concatenate(parts_re, axis=0).astype(jnp.bfloat16)
            response[0, low, at] = jnp.concatenate(parts_im, axis=0).astype(jnp.bfloat16)


def image_kernel(chans, pieces, phase_re, phase_im, coord, response, out, volt_re, volt_im, x_a, x_b):
    planes, stations = volt_re.shape
    lanes = response.shape[2]
    steps = phase_re.shape[0]
    step = pl.program_id(0)

    def prepare(q, x_out):
        pr = phase_re[pl.ds(q, 1), :]
        pi = phase_im[pl.ds(q, 1), :]
        vr = volt_re[...]
        vi = volt_im[...]
        xr = (vr * pr - vi * pi).astype(jnp.bfloat16)
        xi = (vr * pi + vi * pr).astype(jnp.bfloat16)
        x_out[:planes, :stations] = xr
        x_out[:planes, stations:] = -xi
        x_out[planes:, :stations] = xi
        x_out[planes:, stations:] = xr

    def finish(part, x_in):
        for tile in range(lanes // TILE):
            at = slice(tile * TILE, (tile + 1) * TILE)
            field = jnp.dot(x_in[...], response[part, :, at], preferred_element_type=jnp.float32)
            power = field * field
            total = power[:planes] + power[planes:]
            total = total[:chans] + total[chans:]
            x = jnp.concatenate([coord[...]] * (TILE // 128), axis=1)
            first_order = total * x
            second_order = first_order * x
            for k, value in enumerate((total, first_order, second_order)):
                out[part, k:k + 1, at] = jnp.sum(value, axis=0, keepdims=True)

    @pl.when(step == 0)
    def _():
        blocks = [piece[...].astype(jnp.float32) for piece in pieces]
        count = blocks[0].shape[0] // (2 * planes // chans)
        for plane in range(2 * planes // chans):
            turned = jnp.concatenate([b[plane * count:(plane + 1) * count] for b in blocks], axis=0).T
            target = volt_re if plane < planes // chans else volt_im
            at = plane % (planes // chans) * chans
            target[at:at + chans, :] = turned
        prepare(0, x_a)

    prepare(2 * step + 1, x_b)
    finish(0, x_a)
    prepare(jnp.minimum(2 * step + 2, steps - 1), x_a)
    finish(1, x_b)


def angle_of(product, cells):
    return (product % cells).astype(jnp.float32) * (2.0 * np.pi / cells)


def local(cells, voltages, kernel_table, station_rows, station_cols, kernel_offset):
    high = lax.Precision.HIGHEST
    times, chans = voltages.shape[1], voltages.shape[2]
    stations = station_rows.shape[0]
    variants, width_k = kernel_table.shape[0], kernel_table.shape[1]
    height = cells // lax.axis_size("chan")
    width = cells // lax.axis_size("row")
    first_row = lax.axis_index("chan") * height
    first_col = lax.axis_index("row") * width
    steps = height // STEP
    lanes = STEP * width

    planes = times * chans
    count = lax.axis_size("chan")
    here = lax.axis_index("chan")
    own = voltages.transpose(0, 1, 3, 2).reshape(2 * times * voltages.shape[3], chans)
    pieces = [own] + [
        lax.ppermute(own, "chan", [(j, (j + k) % count) for j in range(count)]) for k in range(1, count)
    ]

    def arrival_order(values):
        turned = values.reshape(count, stations // count)[::-1]
        return lax.dynamic_slice_in_dim(jnp.concatenate([turned, turned]), count - 1 - here, count, 0).reshape(-1)

    station_rows = arrival_order(station_rows)
    station_cols = arrival_order(station_cols)
    kernel_offset = arrival_order(kernel_offset)

    start = first_row + STEP * jnp.arange(steps, dtype=jnp.int32)
    turn = angle_of(start[:, None] * station_rows[None, :], cells)
    phase_re, phase_im = jnp.cos(turn), -jnp.sin(turn)

    taps = jnp.arange(width_k, dtype=jnp.int32)
    turn_u = angle_of((first_row + jnp.arange(height, dtype=jnp.int32))[:, None] * taps[None, :], cells)
    turn_v = angle_of((first_col + jnp.arange(width, dtype=jnp.int32))[:, None] * taps[None, :], cells)
    table = kernel_table.astype(jnp.float32)
    half_re = jnp.einsum("oab,vb->oav", table, jnp.cos(turn_v), precision=high)
    half_im = -jnp.einsum("oab,vb->oav", table, jnp.sin(turn_v), precision=high)
    cu, su = jnp.cos(turn_u), jnp.sin(turn_u)
    spread_re = jnp.einsum("ua,oav->uov", cu, half_re, precision=high) + jnp.einsum(
        "ua,oav->uov", su, half_im, precision=high
    )
    spread_im = jnp.einsum("ua,oav->uov", cu, half_im, precision=high) - jnp.einsum(
        "ua,oav->uov", su, half_re, precision=high
    )

    def pack(s):
        s = s.reshape(steps, STEP, variants, width).transpose(0, 2, 1, 3).reshape(steps, variants, lanes)
        return jnp.pad(s, ((0, 0), (0, 8 - variants), (0, 0)))

    x = (2.0 * np.arange(chans) + 1.0 - chans) / chans
    coord = jnp.asarray(np.broadcast_to(x[:, None], (chans, 128)), jnp.float32)
    vmem = pl.BlockSpec(memory_space=pltpu.VMEM)
    smem = pl.BlockSpec(memory_space=pltpu.SMEM)
    spread = pl.BlockSpec((1, 8, lanes), lambda i: (i, 0, 0))
    response = pl.pallas_call(
        lambda *refs: response_kernel(cells, width, *refs),
        grid=(steps,),
        out_shape=jax.ShapeDtypeStruct((steps, 2 * stations, lanes), jnp.bfloat16),
        in_specs=[vmem, vmem, vmem, smem, spread, spread],
        out_specs=pl.BlockSpec((1, 2 * stations, lanes), lambda i: (i, 0, 0)),
        scratch_shapes=[
            pltpu.VMEM((stations, lanes), jnp.float32),
            pltpu.VMEM((stations, lanes), jnp.float32),
            pltpu.VMEM((stations, 128), jnp.int32),
        ],
        compiler_params=pltpu.CompilerParams(vmem_limit_bytes=16 * 1024 * 1024),
        cost_estimate=pl.CostEstimate(
            flops=16 * steps * stations * lanes, bytes_accessed=4 * steps * stations * lanes, transcendentals=0
        ),
    )(
        station_rows[:, None], station_cols[:, None], kernel_offset[:, None],
        first_col.reshape(1).astype(jnp.int32), pack(spread_re), pack(spread_im),
    )
    raw = pl.pallas_call(
        lambda *refs: image_kernel(chans, refs[:count], *refs[count:]),
        grid=(steps // 2,),
        out_shape=jax.ShapeDtypeStruct((steps, 3, lanes), jnp.float32),
        in_specs=[vmem] * (count + 3) + [pl.BlockSpec((2, 2 * stations, lanes), lambda i: (i, 0, 0))],
        out_specs=pl.BlockSpec((2, 3, lanes), lambda i: (i, 0, 0)),
        scratch_shapes=[
            pltpu.VMEM((planes, stations), jnp.float32),
            pltpu.VMEM((planes, stations), jnp.float32),
            pltpu.VMEM((2 * planes, 2 * stations), jnp.bfloat16),
            pltpu.VMEM((2 * planes, 2 * stations), jnp.bfloat16),
        ],
        compiler_params=pltpu.CompilerParams(vmem_limit_bytes=24 * 1024 * 1024),
        cost_estimate=pl.CostEstimate(
            flops=8 * steps * planes * stations * lanes, bytes_accessed=4 * steps * stations * lanes, transcendentals=0
        ),
    )(*pieces, phase_re, phase_im, coord, response)
    norm = np.array([1.0 / np.sqrt(np.sum(x ** (2 * k))) for k in range(3)]) / (times * stations * width_k * width_k)
    images = raw.reshape(steps, 3, STEP, width).transpose(1, 0, 2, 3).reshape(3, height, width)
    return images * jnp.asarray(norm, jnp.float32)[:, None, None]


def solution(mesh):
    cells = 768
    placed = (P(None, None, None, "chan"), P(), P(), P(), P())
    return jax.shard_map(
        lambda *args: local(cells, *args), mesh=mesh, in_specs=placed, out_specs=P(None, "chan", "row"), check_vma=False
    )
```

time: 63.5 us -> 46.4 us (0.73)
  blocking collectives: 32.5 us -> 0 us
  starting transfers between devices: 0 us -> 13.8 us
  Pallas kernels: 21 us -> 24.1 us
  local copies, waits for them, and re-layouts: 5.7 us -> 4.21 us
    all_gather x1 -> x0, blocking collectives: 32.5 us -> none  [local(): lax.all_gather(voltages.reshape(2 * planes, voltages.shape[3]), 'chan', a...]
    ppermute x0 -> x7, starting transfers between devices: none -> 13.8 us  [local(): lax.ppermute(own, 'chan', [(j, (j + k) % count) for j in range(count)])]
    unnamed x13 -> x8, local copies, waits for them, and re-layouts: 3.72 us -> 0.02 us
    pallas_call x1 -> x2, Pallas kernels: 21 us -> 24.1 us  [the longest x1 14.1 us: local(): pl.pallas_call(lambda *refs: image_kernel(chans, refs[:count], *refs[coun...]
    reshape x1 -> x3, local copies, waits for them, and re-layouts: 0.02 us -> 2.27 us  [arrival_order(): turned = values.reshape(count, stations // count)[::-1]]
  transfers between devices with their start and end apart: 0 -> 7, of which waited for: 0 -> 0; matrix products, arithmetic and copies ran while one was open for 0% -> 15% of each run, Pallas kernels for 0% -> 22%
where the time goes in v2:
time: 46.4 us; the launch traced here: 46.2 us
  Pallas kernels  24.1 us (52%)
  starting transfers between devices  13.8 us (30%)
  local copies, waits for them, and re-layouts  4.21 us (9%)
  matrix products  2.78 us (6%)
  other arithmetic  1.03 us (2%)
    pallas_call x1, Pallas kernels, local(): pl.pallas_call(lambda *refs: image_kernel(chans, refs[:count], *refs[coun...  14.1 us
    ppermute x7, starting transfers between devices, local(): lax.ppermute(own, 'chan', [(j, (j + k) % count) for j in range(count)])  13.8 us
    pallas_call x1, Pallas kernels, local(): pl.pallas_call(lambda *refs: response_kernel(cells, width, *refs), grid=(...  10 us
    reshape x3, local copies, waits for them, and re-layouts, arrival_order(): turned = values.reshape(count, stations // count)[::-1]  2.27 us
    reshape x6, local copies, waits for them, and re-layouts, pack(): s.reshape(steps, STEP, variants, width).transpose(0, 2, 1, 3)  0.97 us
  transfers between devices with their start and end apart: 7, of which 0 were waited for; matrix products, arithmetic and copies ran while one was open for 15% of the time, Pallas kernels for 22%

profile of v2, /device:TPU:0, one launch (start us, length us, event | category | flops | bytes accessed | tf_op | source)
XLA Modules:
  0.0 46.2 jit_solution(7315176465293680321)
XLA Ops:
  0.0 3.0 %collective-permute-start = (bf16[128,128]{1,0:T(8,128)(2,1)}, bf16[128,128]{1,0:T(8,128)(2,1)S(1)}, u32[]{:S(2)}, u32[]{:S(2)}) collective-permute-start(bf16[128,128]{1,0:T(8,128)(2,1)} %bitcast.43), channel_id=1, source_target_pairs={{0,4},{4,8},{8,12},{12,16},{16,20},{20,24},{24,28},{28,0},{1,5},{5... | collective-permute-start | bytes 98312 | tf_op jit(solution)/shard_map/ppermute | solution.py:152
  3.0 1.6 %collective-permute-start.1 = (bf16[128,128]{1,0:T(8,128)(2,1)}, bf16[128,128]{1,0:T(8,128)(2,1)S(1)}, u32[]{:S(2)}, u32[]{:S(2)}) collective-permute-start(bf16[128,128]{1,0:T(8,128)(2,1)} %bitcast.44), channel_id=1, source_target_pairs={{0,8},{4,12},{8,16},{12,20},{16,24},{20,28},{24,0},{28,4},{1,9},{5... | collective-permute-start | bytes 98312 | tf_op jit(solution)/shard_map/ppermute | solution.py:152
  4.6 2.5 %collective-permute-start.2 = (bf16[128,128]{1,0:T(8,128)(2,1)}, bf16[128,128]{1,0:T(8,128)(2,1)S(1)}, u32[]{:S(2)}, u32[]{:S(2)}) collective-permute-start(bf16[128,128]{1,0:T(8,128)(2,1)} %bitcast.45), channel_id=1, source_target_pairs={{0,12},{4,16},{8,20},{12,24},{16,28},{20,0},{24,4},{28,8},{1,13},{... | collective-permute-start | bytes 98312 | tf_op jit(solution)/shard_map/ppermute | solution.py:152
  7.1 1.2 %collective-permute-start.3 = (bf16[128,128]{1,0:T(8,128)(2,1)}, bf16[128,128]{1,0:T(8,128)(2,1)S(1)}, u32[]{:S(2)}, u32[]{:S(2)}) collective-permute-start(bf16[128,128]{1,0:T(8,128)(2,1)} %bitcast.46), channel_id=1, source_target_pairs={{0,16},{4,20},{8,24},{12,28},{16,0},{20,4},{24,8},{28,12},{1,17},{... | collective-permute-start | bytes 98312 | tf_op jit(solution)/shard_map/ppermute | solution.py:152
  8.4 2.6 %collective-permute-start.4 = (bf16[128,128]{1,0:T(8,128)(2,1)}, bf16[128,128]{1,0:T(8,128)(2,1)S(1)}, u32[]{:S(2)}, u32[]{:S(2)}) collective-permute-start(bf16[128,128]{1,0:T(8,128)(2,1)} %bitcast.47), channel_id=1, source_target_pairs={{0,20},{4,24},{8,28},{12,0},{16,4},{20,8},{24,12},{28,16},{1,21},{... | collective-permute-start | bytes 98312 | tf_op jit(solution)/shard_map/ppermute | solution.py:152
  11.0 0.2 convolution_bitcast_fusion
  11.3 0.2 fusion
  11.6 0.6 %fusion.24 = f32[96,4,192]{2,0,1:T(8,128)S(1)} fusion(f32[4,16,192]{2,1,0:T(8,128)S(1)} %convolution_bitcast_fusion, s32[96]{0:T(128)S(1)} %iota_add_fusion.1), kind=kOutput, calls=%fused_computation.41 | convolution fusion | flops 14169600 | bytes 344448 | tf_op jit(solution)/shard_map/ua,oav->uov/dot_general | solution.py:174
  12.1 0.6 %fusion.22 = f32[96,4,192]{2,0,1:T(8,128)S(1)} fusion(f32[4,16,192]{2,1,0:T(8,128)S(1)} %fusion, s32[96]{0:T(128)S(1)} %iota_add_fusion.1), kind=kOutput, calls=%fused_computation.39 | convolution fusion | flops 14169600 | bytes 344448 | tf_op jit(solution)/shard_map/ua,oav->uov/dot_general | solution.py:177
  12.7 0.6 %convolution_add_fusion = f32[96,4,192]{2,0,1:T(8,128)S(1)} fusion(f32[96,4,192]{2,0,1:T(8,128)S(1)} %fusion.24, f32[4,16,192]{2,1,0:T(8,128)S(1)} %fusion, s32[96]{0:T(128)S(1)} %iota_add_fusion.1), kind=kOutput, calls=%fused_computation.1 | convolution fusion | flops 14243328 | bytes 639360 | tf_op jit(solution)/shard_map/ua,oav->uov/dot_general | solution.py:174
  13.3 0.6 %convolution_subtract_fusion = f32[96,4,192]{2,0,1:T(8,128)S(1)} fusion(f32[96,4,192]{2,0,1:T(8,128)S(1)} %fusion.22, f32[4,16,192]{2,1,0:T(8,128)S(1)} %convolution_bitcast_fusion, s32[96]{0:T(128)S(1)} %iota_add_fusion.1), kind=kOutput, calls=%fused_computation | convolution fusion | flops 14243328 | bytes 639360 | tf_op jit(solution)/shard_map/ua,oav->uov/dot_general | solution.py:177
  13.9 0.8 %reshape.49 = s32[8,32]{1,0:T(8,128)S(1)} reshape(s32[256]{0:T(256)} %param.9) | data formatting | bytes 2048 | tf_op jit(solution)/shard_map/reshape | solution.py:156
  14.7 0.1 mul.83
  14.8 0.2 sine_negate_fusion
  14.9 0.8 %reshape.50 = s32[8,32]{1,0:T(8,128)S(1)} reshape(s32[256]{0:T(256)} %param.10) | data formatting | bytes 2048 | tf_op jit(solution)/shard_map/reshape | solution.py:156
  15.7 0.8 %reshape.51 = s32[8,32]{1,0:T(8,128)S(1)} reshape(s32[256]{0:T(256)} %param.11) | data formatting | bytes 2048 | tf_op jit(solution)/shard_map/reshape | solution.py:156
  16.5 0.0 collective-permute-done.refs_1_
  16.5 1.4 %collective-permute-start.5 = (bf16[128,128]{1,0:T(8,128)(2,1)}, bf16[128,128]{1,0:T(8,128)(2,1)S(1)}, u32[]{:S(2)}, u32[]{:S(2)}) collective-permute-start(bf16[128,128]{1,0:T(8,128)(2,1)} %bitcast.48), channel_id=1, source_target_pairs={{0,24},{4,28},{8,0},{12,4},{16,8},{20,12},{24,16},{28,20},{1,25},{... | collective-permute-start | bytes 98312 | tf_op jit(solution)/shard_map/ppermute | solution.py:152
  17.9 1.4 %collective-permute-start.6 = (bf16[128,128]{1,0:T(8,128)(2,1)}, bf16[128,128]{1,0:T(8,128)(2,1)S(1)}, u32[]{:S(2)}, u32[]{:S(2)}) collective-permute-start(bf16[128,128]{1,0:T(8,128)(2,1)} %bitcast.49), channel_id=1, source_target_pairs={{0,28},{4,0},{8,4},{12,8},{16,12},{20,16},{24,20},{28,24},{1,29},{... | collective-permute-start | bytes 98312 | tf_op jit(solution)/shard_map/ppermute | solution.py:152
  19.3 0.1 broadcast_in_dim_reshape.13.refs_0_
  19.4 0.1 reshape.53
  19.6 0.3 reshape.54
  19.9 0.1 reshape.55
  20.1 0.3 reshape.56
  20.5 0.1 broadcast_in_dim_reshape.14.refs_1_
  20.7 0.1 broadcast_in_dim_reshape.15.refs_2_
  20.8 10.0 %shard_map.73.refs_11_ = bf16[24,512,768]{2,1,0:T(8,128)(2,1)S(1)} custom-call(s32[256,1]{1,0:T(8,128)S(1)} %broadcast_in_dim_reshape.13.refs_0_, s32[256,1]{1,0:T(8,128)S(1)} %broadcast_in_dim_reshape.14.refs_1_, s32[256,1]{1,0:T(8,128)S(1)} %broadcast_in_dim_reshape.15.refs_2_, s32[1]{0:T(128)} %bitcast.3.refs_3_, f32[24,8,768]{2,1,0:T(8,128)S(1)} %pad.7.refs_4_, ...), custom_call_target="tpu_custom_call" | custom-call | flops 75497472 | bytes 18874368 | tf_op jit(solution)/shard_map/pallas_call | solution.py:190
  30.9 0.0 copy-start.3
  30.9 14.1 %shard_map.74 = f32[24,3,768]{2,1,0:T(4,128)S(1)} custom-call(bf16[128,128]{1,0:T(8,128)(2,1)S(1)} %bitcast.50, bf16[128,128]{1,0:T(8,128)(2,1)S(1)} %collective-permute-done.refs_1_, bf16[128,128]{1,0:T(8,128)(2,1)S(1)} %collective-permute-done.1.refs_2_, bf16[128,128]{1,0:T(8,128)(2,1)S(1)} %collective-permute-done.2.refs_3_, ...), custom_call_target="tpu_custom_call" | custom-call | flops 9663676416 | bytes 18874368 | tf_op jit(solution)/shard_map/pallas_call | solution.py:209
  45.1 0.2 reshape.57
  45.3 0.1 reshape.58
  45.4 0.8 %broadcast_multiply_fusion = f32[3,96,192]{2,1,0:T(8,128)} fusion(f32[3,96,192]{2,1,0:T(8,128)S(1)} %reshape.58, f32[3]{0:T(128)S(1)} %copy-done.3), kind=kLoop, calls=%fused_computation.7 | loop fusion | flops 55296 | bytes 442380 | tf_op jit(solution)/shard_map/mul | solution.py:228
  (26 shorter events, 0.3 us)
Async XLA Ops:
  0.0 11.0 %copy-start = (bf16[4,16,16]{2,1,0:T(8,128)(2,1)S(1)}, bf16[4,16,16]{2,1,0:T(8,128)(2,1)}, u32[]{:S(2)}) copy-start(bf16[4,16,16]{2,1,0:T(8,128)(2,1)} %param.8) | copy-start | bytes 6148
  0.0 30.9 %copy-start.2 = (f32[128,128]{1,0:T(8,128)S(1)}, f32[128,128]{1,0:T(8,128)}, u32[]{:S(2)}) copy-start(f32[128,128]{1,0:T(8,128)} %constant.55.clone.refs_10_) | copy-start | bytes 196612
  0.0 30.9 %copy-start.1 = (bf16[2,2,128,32]{2,3,1,0:T(8,128)(2,1)S(1)}, bf16[2,2,128,32]{2,3,1,0:T(8,128)(2,1)}, u32[]{:S(2)}) copy-start(bf16[2,2,128,32]{2,3,1,0:T(8,128)(2,1)} %param.7) | copy-start | bytes 98308
  0.0 16.5 %collective-permute-start = (bf16[128,128]{1,0:T(8,128)(2,1)}, bf16[128,128]{1,0:T(8,128)(2,1)S(1)}, u32[]{:S(2)}, u32[]{:S(2)}) collective-permute-start(bf16[128,128]{1,0:T(8,128)(2,1)} %bitcast.43), channel_id=1, source_target_pairs={{0,4},{4,8},{8,12},{12,16},{16,20},{20,24},{24,28},{28,0},{1,5},{5... | collective-permute-start | bytes 98312 | tf_op jit(solution)/shard_map/ppermute | solution.py:152
  3.0 14.8 %collective-permute-start.1 = (bf16[128,128]{1,0:T(8,128)(2,1)}, bf16[128,128]{1,0:T(8,128)(2,1)S(1)}, u32[]{:S(2)}, u32[]{:S(2)}) collective-permute-start(bf16[128,128]{1,0:T(8,128)(2,1)} %bitcast.44), channel_id=1, source_target_pairs={{0,8},{4,12},{8,16},{12,20},{16,24},{20,28},{24,0},{28,4},{1,9},{5... | collective-permute-start | bytes 98312 | tf_op jit(solution)/shard_map/ppermute | solution.py:152
  4.6 26.3 %collective-permute-start.2 = (bf16[128,128]{1,0:T(8,128)(2,1)}, bf16[128,128]{1,0:T(8,128)(2,1)S(1)}, u32[]{:S(2)}, u32[]{:S(2)}) collective-permute-start(bf16[128,128]{1,0:T(8,128)(2,1)} %bitcast.45), channel_id=1, source_target_pairs={{0,12},{4,16},{8,20},{12,24},{16,28},{20,0},{24,4},{28,8},{1,13},{... | collective-permute-start | bytes 98312 | tf_op jit(solution)/shard_map/ppermute | solution.py:152
  7.1 23.7 %collective-permute-start.3 = (bf16[128,128]{1,0:T(8,128)(2,1)}, bf16[128,128]{1,0:T(8,128)(2,1)S(1)}, u32[]{:S(2)}, u32[]{:S(2)}) collective-permute-start(bf16[128,128]{1,0:T(8,128)(2,1)} %bitcast.46), channel_id=1, source_target_pairs={{0,16},{4,20},{8,24},{12,28},{16,0},{20,4},{24,8},{28,12},{1,17},{... | collective-permute-start | bytes 98312 | tf_op jit(solution)/shard_map/ppermute | solution.py:152
  8.4 22.5 %collective-permute-start.4 = (bf16[128,128]{1,0:T(8,128)(2,1)}, bf16[128,128]{1,0:T(8,128)(2,1)S(1)}, u32[]{:S(2)}, u32[]{:S(2)}) collective-permute-start(bf16[128,128]{1,0:T(8,128)(2,1)} %bitcast.47), channel_id=1, source_target_pairs={{0,20},{4,24},{8,28},{12,0},{16,4},{20,8},{24,12},{28,16},{1,21},{... | collective-permute-start | bytes 98312 | tf_op jit(solution)/shard_map/ppermute | solution.py:152
  16.5 14.4 %collective-permute-start.5 = (bf16[128,128]{1,0:T(8,128)(2,1)}, bf16[128,128]{1,0:T(8,128)(2,1)S(1)}, u32[]{:S(2)}, u32[]{:S(2)}) collective-permute-start(bf16[128,128]{1,0:T(8,128)(2,1)} %bitcast.48), channel_id=1, source_target_pairs={{0,24},{4,28},{8,0},{12,4},{16,8},{20,12},{24,16},{28,20},{1,25},{... | collective-permute-start | bytes 98312 | tf_op jit(solution)/shard_map/ppermute | solution.py:152
  17.9 13.1 %collective-permute-start.6 = (bf16[128,128]{1,0:T(8,128)(2,1)}, bf16[128,128]{1,0:T(8,128)(2,1)S(1)}, u32[]{:S(2)}, u32[]{:S(2)}) collective-permute-start(bf16[128,128]{1,0:T(8,128)(2,1)} %bitcast.49), channel_id=1, source_target_pairs={{0,28},{4,0},{8,4},{12,8},{16,12},{20,16},{24,20},{28,24},{1,29},{... | collective-permute-start | bytes 98312 | tf_op jit(solution)/shard_map/ppermute | solution.py:152
  30.9 14.5 %copy-start.3 = (f32[3]{0:T(128)S(1)}, f32[3]{0:T(128)}, u32[]{:S(2)}) copy-start(f32[3]{0:T(128)} %constant.56.clone) | copy-start | bytes 40

commit v3 on v1

v3 whole, which is shorter than its diff:
```python
import jax
import jax.numpy as jnp
import numpy as np
from jax import lax
from jax.experimental import pallas as pl
from jax.experimental.pallas import tpu as pltpu
from jax.sharding import PartitionSpec as P

TILE = 256
STEP = 4


def wave_fit(terms=8):
    nodes = 0.125 + 0.125 * np.cos(np.pi * (np.arange(200) + 0.5) / 200)
    root = np.sqrt(nodes)
    fit = np.polynomial.polynomial.polyfit
    cosine = fit(nodes, np.cos(2 * np.pi * root), terms - 1)
    sine = fit(nodes, np.sin(2 * np.pi * root) / root, terms - 1)
    return [float(c) for c in cosine], [float(c) for c in sine]


COS_FIT, SIN_FIT = wave_fit()


def horner(coefs, x):
    value = jnp.full_like(x, coefs[-1])
    for c in coefs[-2::-1]:
        value = value * x + c
    return value


def wave(product, cells):
    turns = product * (1.0 / cells)
    part = (product - cells * jnp.round(turns)) * (1.0 / cells)
    square = part * part
    return horner(COS_FIT, square), -part * horner(SIN_FIT, square)


def whole_of(shape, axis):
    return lax.broadcasted_iota(jnp.int32, shape, axis)


def split(value):
    high = value.astype(jnp.bfloat16)
    return high, (value - high.astype(jnp.float32)).astype(jnp.bfloat16)


def station_column(values, stations):
    return jnp.broadcast_to(values.astype(jnp.float32), (128, stations)).T


def table_kernel(
    cells, width, held, place, rows, cols, variant, table, base_re, base_im, pick, spread_re, spread_im, kept
):
    kept[...] = held[...]
    stations = rows.shape[1]
    steps, lanes = spread_re.shape[0], spread_re.shape[2]
    taps = table.shape[1]
    variants = table.shape[0] // taps
    first_row = place[1].astype(jnp.float32)
    first_col = place[2].astype(jnp.float32)
    pick[...] = station_column(variant[...], stations).astype(jnp.int32)
    row_of = station_column(rows[...], stations)
    col_of = station_column(cols[...], stations)

    def down_across(shape, start):
        lane = whole_of(shape, 1) + start
        down = jnp.zeros(shape, jnp.float32)
        for p in range(1, STEP):
            down = jnp.where(lane >= p * width, float(p), down)
        return down, lane.astype(jnp.float32) - down * width + first_col

    for tile in range(lanes // 128):
        at = slice(tile * 128, (tile + 1) * 128)
        down, across = down_across((stations, 128), tile * 128)
        base_re[:, at], base_im[:, at] = wave(row_of * down + col_of * across, cells)

    down, across = down_across((taps, lanes), 0)
    tap = whole_of((taps, lanes), 0).astype(jnp.float32)
    kernels = table[...]

    def over_columns(value):
        high, low = split(value)
        return jnp.dot(kernels, high, preferred_element_type=jnp.float32) + jnp.dot(
            kernels, low, preferred_element_type=jnp.float32
        )

    half_re, half_im = [over_columns(value) for value in wave(tap * across, cells)]
    turn_re, turn_im = wave(tap * down, cells)
    tall = -(-steps // 16) * 16
    lane = whole_of((tall, 6 * taps), 1)
    start = first_row + float(STEP) * whole_of((tall, 6 * taps), 0).astype(jnp.float32)
    left_re, left_im = wave(start * (lane % taps).astype(jnp.float32), cells)
    value = jnp.where(lane // taps % 2 == 0, left_re, -left_im)
    high, low = split(value)
    left = jnp.where(lane // (2 * taps) == 1, low.astype(jnp.float32), high.astype(jnp.float32)).astype(jnp.bfloat16)
    for o in range(variants):
        rows_o = slice(o * taps, (o + 1) * taps)
        real = turn_re * half_re[rows_o] - turn_im * half_im[rows_o]
        imag = turn_re * half_im[rows_o] + turn_im * half_re[rows_o]
        for target, one, two in ((spread_re, real, imag), (spread_im, imag, -real)):
            one_high, one_low = split(one)
            two_high, two_low = split(two)
            right = jnp.concatenate([one_high, two_high, one_high, two_high, one_low, two_low], axis=0)
            target[:, o, :] = jnp.dot(left, right, preferred_element_type=jnp.float32)[:steps]


def response_kernel(first, held, base_re, base_im, pick, spread_re, spread_im, response, kept):
    kept[...] = held[...]
    parts, stations, lanes = response.shape[0], base_re.shape[0], base_re.shape[1]

    def two(i, carry):
        for tile in range(lanes // 128):
            at = slice(tile * 128, (tile + 1) * 128)
            tables = [(spread_re[first + 2 * i + j, :, at], spread_im[first + 2 * i + j, :, at]) for j in range(2)]
            for group in range(stations // 16):
                made = [([], []), ([], [])]
                for half in range(2):
                    sub = slice(group * 16 + half * 8, group * 16 + half * 8 + 8)
                    index = pick[sub, :]
                    br = base_re[sub, at]
                    bi = base_im[sub, at]
                    for j in range(2):
                        sr = jnp.take_along_axis(tables[j][0], index, axis=0)
                        si = jnp.take_along_axis(tables[j][1], index, axis=0)
                        made[j][0].append(br * sr - bi * si)
                        made[j][1].append(br * si + bi * sr)
                pair = slice(group * 16, group * 16 + 16)
                low = slice(stations + group * 16, stations + group * 16 + 16)
                for j in range(2):
                    response[2 * i + j, pair, at] = jnp.concatenate(made[j][0], axis=0).astype(jnp.bfloat16)
                    response[2 * i + j, low, at] = jnp.concatenate(made[j][1], axis=0).astype(jnp.bfloat16)
        return carry

    lax.fori_loop(0, parts // 2, two, 0)


def image_kernel(
    cells, chans, width, norm, masks, groups, place, rows, *refs
):
    blocks, responses = refs[:groups[0]], refs[groups[0]:sum(groups)]
    out, turned, volt_re, volt_im, phase_re, phase_im, x_a, x_b, f_a, f_b, sums, strips = refs[sum(groups):]
    planes, stations = volt_re.shape
    steps, lanes = phase_re.shape[0], responses[0].shape[2]
    sheets = turned.shape[0]
    each = stations // len(sum(masks, ()))

    for block, held in zip(blocks, masks):
        value = block[...].astype(jnp.float32)
        for n, mask in enumerate(held):
            at = pl.multiple_of((place[0] ^ mask) * each, 8)
            for sheet in range(sheets):
                line = (n * sheets + sheet) * each
                turned[sheet, pl.ds(at, each), :] = value[line:line + each]
    for sheet in range(sheets):
        target = volt_re if sheet < sheets // 2 else volt_im
        at = sheet % (sheets // 2) * chans
        target[at:at + chans, :] = turned[sheet].T
    start = place[1].astype(jnp.float32) + float(STEP) * whole_of((steps, stations), 0).astype(jnp.float32)
    phase_re[...], phase_im[...] = wave(start * rows[...].astype(jnp.float32), cells)

    def prepare(q, x_out):
        pr = phase_re[pl.ds(q, 1), :]
        pi = phase_im[pl.ds(q, 1), :]
        vr = volt_re[...]
        vi = volt_im[...]
        xr = (vr * pr - vi * pi).astype(jnp.bfloat16)
        xi = (vr * pi + vi * pr).astype(jnp.bfloat16)
        x_out[:planes, :stations] = xr
        x_out[:planes, stations:] = -xi
        x_out[planes:, :stations] = xi
        x_out[planes:, stations:] = xr

    step_of = (2.0 * whole_of((8, TILE), 0).astype(jnp.float32) + 1.0 - chans) * 0.0625

    def collect(q, tile, field):
        zero = jnp.zeros((8, TILE), jnp.float32)
        s0, s1, s2 = zero, zero, zero
        for g in range(chans // 8 - 1, -1, -1):
            for t in range(2 * planes // chans):
                line = t * chans + g * 8
                part = field[line:line + 8, :]
                total = part * part if t == 0 else total + part * part
            s0 = s0 + total
            s1 = s1 + s0
            s2 = s2 + s1
        g1 = s1 - s0
        g2 = 2.0 * s2 - 3.0 * s1 + s0
        first = g1 + step_of * s0
        second = g2 + step_of * (2.0 * g1 + step_of * s0)
        for k, value in enumerate((s0, first, second)):
            sums[k, pl.ds(q, 1), tile * TILE:(tile + 1) * TILE] = norm[k] * jnp.sum(value, axis=0, keepdims=True)

    tiles = lanes // TILE
    fields = (f_a, f_b)
    prepare(0, x_a)
    f_b[...] = jnp.zeros_like(f_b)
    for part, response in enumerate(responses):
        base = part * response.shape[0]

        def two(i, carry):
            q = base + 2 * i
            for n in range(2 * tiles):
                x = x_a if n < tiles else x_b
                at = slice(n % tiles * TILE, (n % tiles + 1) * TILE)
                fields[n % 2][...] = jnp.dot(
                    x[...], response[2 * i + n // tiles, :, at], preferred_element_type=jnp.float32
                )
                if n == 0:
                    collect(jnp.maximum(q - 1, 0), tiles - 1, fields[1])
                    prepare(q + 1, x_b)
                else:
                    collect(q + (n - 1) // tiles, (n - 1) % tiles, fields[1 - n % 2])
                if n == tiles:
                    prepare(jnp.minimum(q + 2, steps - 1), x_a)
            return carry

        lax.fori_loop(0, response.shape[0] // 2, two, 0)
    collect(steps - 1, tiles - 1, fields[1])
    for k in range(3):
        for p in range(STEP):
            for j in range(strips.shape[0]):
                at = p * width + j * 128
                strips[j, pl.ds(p, steps, stride=STEP), :] = sums[k, :, at:at + 128]
        for j in range(strips.shape[0]):
            left = min(128, width - j * 128)
            out[k, :, j * 128:j * 128 + left] = strips[j, :, :left]


def local(cells, voltages, kernel_table, station_rows, station_cols, kernel_offset):
    times, chans = voltages.shape[1], voltages.shape[2]
    stations = station_rows.shape[0]
    variants, taps = kernel_table.shape[0], kernel_table.shape[1]
    count = lax.axis_size("chan")
    height = cells // count
    width = cells // lax.axis_size("row")
    here = lax.axis_index("chan")
    steps = height // STEP
    lanes = STEP * width
    planes = times * chans
    place = jnp.stack([here, here * height, lax.axis_index("row") * width]).astype(jnp.int32)
    vmem = pl.BlockSpec(memory_space=pltpu.VMEM)
    smem = pl.BlockSpec(memory_space=pltpu.SMEM)
    f32, bf16 = jnp.float32, jnp.bfloat16
    mib = 1024 * 1024

    bits = []
    while (1 << len(bits)) < count:
        bits.append(count >> (len(bits) + 1))
    own = voltages.transpose(0, 1, 3, 2).reshape(2 * times * voltages.shape[3], chans)
    held, blocks, masks, reach = own, [own], [(0,)], (0,)

    lines = [v.reshape(1, stations) for v in (station_rows, station_cols, kernel_offset)]
    make_tables = lambda held: pl.pallas_call(
        lambda *refs: table_kernel(cells, width, *refs),
        out_shape=[
            jax.ShapeDtypeStruct((stations, lanes), f32),
            jax.ShapeDtypeStruct((stations, lanes), f32),
            jax.ShapeDtypeStruct((stations, 128), jnp.int32),
            jax.ShapeDtypeStruct((steps, 8, lanes), f32),
            jax.ShapeDtypeStruct((steps, 8, lanes), f32),
            jax.ShapeDtypeStruct(held.shape, bf16),
        ],
        in_specs=[vmem, smem, vmem, vmem, vmem, vmem],
        out_specs=[vmem] * 6,
        compiler_params=pltpu.CompilerParams(vmem_limit_bytes=16 * mib),
        cost_estimate=pl.CostEstimate(flops=100 * stations * lanes, bytes_accessed=16 * stations * lanes, transcendentals=0),
    )(held, place, *lines, kernel_table.reshape(variants * taps, taps))

    ahead = steps // 4 * 2
    shares = [(0, steps - ahead), (steps - ahead, ahead)]
    responses = []
    for cut, bit in enumerate(bits):
        came = lax.ppermute(held, "chan", [(j, j ^ bit) for j in range(count)])
        if cut == 0:
            *tables, held = make_tables(held)
        elif cut <= len(shares):
            first, part = shares[cut - 1]
            response, held = pl.pallas_call(
                lambda *refs, first=first: response_kernel(first, *refs),
                out_shape=[
                    jax.ShapeDtypeStruct((part, 2 * stations, lanes), bf16),
                    jax.ShapeDtypeStruct(held.shape, bf16),
                ],
                in_specs=[vmem] * 6,
                out_specs=[vmem] * 2,
                compiler_params=pltpu.CompilerParams(vmem_limit_bytes=16 * mib),
                cost_estimate=pl.CostEstimate(
                    flops=16 * part * stations * lanes, bytes_accessed=4 * part * stations * lanes, transcendentals=0
                ),
            )(held, *tables)
            responses.append(response)
        blocks.append(came)
        masks.append(tuple(m ^ bit for m in reach))
        reach = reach + masks[-1]
        held = jnp.concatenate([held, came])

    x = (2.0 * np.arange(chans) + 1.0 - chans) / chans
    norm = [
        float(1.0 / np.sqrt(np.sum(x ** (2 * k))) / (times * stations * taps * taps) * (16.0 / chans) ** k)
        for k in range(3)
    ]
    groups = (len(blocks), len(responses))
    return pl.pallas_call(
        lambda *refs: image_kernel(cells, chans, width, norm, masks, groups, *refs),
        out_shape=jax.ShapeDtypeStruct((3, height, width), f32),
        in_specs=[smem] + [vmem] * (1 + sum(groups)),
        out_specs=vmem,
        scratch_shapes=[
            pltpu.VMEM((2 * times, stations, chans), f32),
            pltpu.VMEM((planes, stations), f32),
            pltpu.VMEM((planes, stations), f32),
            pltpu.VMEM((steps, stations), f32),
            pltpu.VMEM((steps, stations), f32),
            pltpu.VMEM((2 * planes, 2 * stations), bf16),
            pltpu.VMEM((2 * planes, 2 * stations), bf16),
            pltpu.VMEM((2 * planes, TILE), f32),
            pltpu.VMEM((2 * planes, TILE), f32),
            pltpu.VMEM((3, steps, lanes + 128), f32),
            pltpu.VMEM((-(-width // 128), height, 128), f32),
        ],
        compiler_params=pltpu.CompilerParams(vmem_limit_bytes=32 * mib),
        cost_estimate=pl.CostEstimate(
            flops=8 * steps * planes * stations * lanes, bytes_accessed=4 * steps * stations * lanes, transcendentals=0
        ),
    )(place, lines[0], *blocks, *responses)


def solution(mesh):
    cells = 768
    placed = (P(None, None, None, "chan"), P(), P(), P(), P())
    return jax.shard_map(
        lambda *args: local(cells, *args), mesh=mesh, in_specs=placed, out_specs=P(None, "chan", "row"), check_vma=False
    )
```

time: 63.5 us -> 37.7 us (0.59)
  blocking collectives: 32.5 us -> 0 us
  starting transfers between devices: 0 us -> 7.26 us
  Pallas kernels: 21 us -> 25 us
  matrix products: 2.79 us -> 0 us
  other arithmetic: 1 us -> 0.08 us
  local copies, waits for them, and re-layouts: 5.7 us -> 4.98 us
    all_gather x1 -> x0, blocking collectives: 32.5 us -> none  [local(): lax.all_gather(voltages.reshape(2 * planes, voltages.shape[3]), 'chan', a...]
    ppermute x0 -> x3, starting transfers between devices: none -> 7.26 us  [local(): came = lax.ppermute(held, 'chan', [(j, j ^ bit) for j in range(count)])]
    pallas_call x1 -> x4, Pallas kernels: 21 us -> 25 us  [the longest x1 15.4 us: local(): pl.pallas_call(lambda *refs: image_kernel(cells, chans, width, norm, mask...]
    dot_general x6 -> x0, matrix products: 2.79 us -> none  [the longest x1 0.57 us: local(): jnp.einsum('ua,oav->uov', su, half_re, precision=high)]
    reshape x9 -> x0, local copies, waits for them, and re-layouts: 1.31 us -> none  [the longest x6 0.97 us: pack(): s.reshape(steps, STEP, variants, width).transpose(0, 2, 1, 3)]
    unnamed x13 -> x16, local copies, waits for them, and re-layouts: 3.72 us -> 4.96 us
    mul x1 -> x0, other arithmetic: 0.8 us -> none  [local(): return images * jnp.asarray(norm, jnp.float32)[:, None, None]]
  transfers between devices with their start and end apart: 0 -> 3, of which waited for: 0 -> 0; matrix products, arithmetic and copies ran while one was open for 0% -> 0% of each run, Pallas kernels for 0% -> 26%
where the time goes in v3:
time: 37.7 us; the launch traced here: 37.4 us
  Pallas kernels  25 us (66%)
  starting transfers between devices  7.26 us (19%)
  local copies, waits for them, and re-layouts  4.98 us (13%)
    pallas_call x1, Pallas kernels, local(): pl.pallas_call(lambda *refs: image_kernel(cells, chans, width, norm, mask...  15.4 us
    pallas_call x2, Pallas kernels, local(): pl.pallas_call(lambda *refs, first=first: response_kernel(first, *refs),...  7.38 us
    ppermute x3, starting transfers between devices, local(): came = lax.ppermute(held, 'chan', [(j, j ^ bit) for j in range(count)])  7.26 us
    unnamed x16, local copies, waits for them, and re-layouts  4.96 us
    pallas_call x1, Pallas kernels, local(): pl.pallas_call(lambda *refs: table_kernel(cells, width, *refs), out_shape...  2.2 us
  transfers between devices with their start and end apart: 3, of which 0 were waited for; matrix products, arithmetic and copies ran while one was open for 0% of the time, Pallas kernels for 26%

profile of v3, /device:TPU:0, one launch (start us, length us, event | category | flops | bytes accessed | tf_op | source)
XLA Modules:
  0.0 37.4 jit_solution(16281301790305020501)
XLA Ops:
  0.0 4.0 %collective-permute-start = (bf16[128,128]{1,0:T(8,128)(2,1)}, bf16[128,128]{1,0:T(8,128)(2,1)S(1)}, u32[]{:S(2)}, u32[]{:S(2)}) collective-permute-start(bf16[128,128]{1,0:T(8,128)(2,1)} %bitcast.10), channel_id=1, source_target_pairs={{0,16},{4,20},{8,24},{12,28},{16,0},{20,4},{24,8},{28,12},{1,17},{... | collective-permute-start | bytes 98312 | tf_op jit(solution)/shard_map/ppermute | solution.py:274
  4.0 0.1 pad_add_fusion.refs_1_.refs_0_
  4.1 0.0 copy-start
  4.1 0.8 %copy-done = bf16[2,2,128,32]{2,3,1,0:T(8,128)(2,1)S(1)} copy-done((bf16[2,2,128,32]{2,3,1,0:T(8,128)(2,1)S(1)}, bf16[2,2,128,32]{2,3,1,0:T(8,128)(2,1)}, u32[]{:S(2)}) %copy-start) | copy-done | bytes 32792
  4.9 0.0 copy-start.2
  4.9 0.7 %copy-done.2 = bf16[4,16,16]{2,1,0:T(8,128)(2,1)S(1)} copy-done((bf16[4,16,16]{2,1,0:T(8,128)(2,1)S(1)}, bf16[4,16,16]{2,1,0:T(8,128)(2,1)}, u32[]{:S(2)}) %copy-start.2) | copy-done | bytes 2072
  5.6 0.0 copy-start.3
  5.6 0.7 %copy-done.3 = s32[256]{0:T(256)S(1)} copy-done((s32[256]{0:T(256)S(1)}, s32[256]{0:T(256)}, u32[]{:S(2)}) %copy-start.3) | copy-done | bytes 1048
  6.3 0.0 copy-start.4
  6.3 0.7 %copy-done.4 = s32[256]{0:T(256)S(1)} copy-done((s32[256]{0:T(256)S(1)}, s32[256]{0:T(256)}, u32[]{:S(2)}) %copy-start.4) | copy-done | bytes 1048
  7.0 0.0 copy-start.5
  7.0 0.7 %copy-done.5 = s32[256]{0:T(256)S(1)} copy-done((s32[256]{0:T(256)S(1)}, s32[256]{0:T(256)}, u32[]{:S(2)}) %copy-start.5) | copy-done | bytes 1048
  7.6 2.2 %shard_map.55 = (f32[256,768]{1,0:T(8,128)S(1)}, f32[256,768]{1,0:T(8,128)S(1)}, s32[256,128]{1,0:T(8,128)S(1)}, f32[24,8,768]{2,1,0:T(8,128)S(1)}, f32[24,8,768...) custom-call(bf16[128,128]{1,0:T(8,128)(2,1)S(1)} %bitcast.11, s32[3]{0:T(128)S(1)} %pad_add_fusion.refs_1_.refs_0_, ...), custom_call_target="tpu_custom_call" | custom-call | flops 19660800 | bytes 3145728 | tf_op jit(solution)/shard_map/pallas_call | solution.py:254
  9.8 0.0 collective-permute-done.refs_3_
  9.9 1.6 %collective-permute-start.1 = (bf16[256,128]{1,0:T(8,128)(2,1)S(1)}, bf16[256,128]{1,0:T(8,128)(2,1)S(1)}, u32[]{:S(2)}, u32[]{:S(2)}) collective-permute-start(bf16[256,128]{1,0:T(8,128)(2,1)S(1)} %constant_dynamic-update-slice_fusion.refs_0_), channel_id=1, source_target_pairs={{0,8},{4,12},{8,0},{12,4},{16,24},{20,28},{24,16},{28,20},{1,9},{5... | collective-permute-start | bytes 196616 | tf_op jit(solution)/shard_map/ppermute | solution.py:274
  11.5 3.7 %shard_map.56 = (bf16[12,512,768]{2,1,0:T(8,128)(2,1)S(1)}, bf16[256,128]{1,0:T(8,128)(2,1)S(1)}) custom-call(bf16[256,128]{1,0:T(8,128)(2,1)S(1)} %constant_dynamic-update-slice_fusion.refs_0_, f32[256,768]{1,0:T(8,128)S(1)} %get-tuple-element.15.refs_1_, f32[256,768]{1,0:T(8,128)S(1)} %get-tuple-element.16.refs_2_, ...), custom_call_target="tpu_custom_call" | custom-call | flops 37748736 | bytes 9437184 | tf_op jit(solution)/shard_map/pallas_call | solution.py:279
  15.2 0.0 collective-permute-done.1.refs_4_
  15.2 1.6 %collective-permute-start.2 = (bf16[512,128]{1,0:T(8,128)(2,1)S(1)}, bf16[512,128]{1,0:T(8,128)(2,1)S(1)}, u32[]{:S(2)}, u32[]{:S(2)}) collective-permute-start(bf16[512,128]{1,0:T(8,128)(2,1)S(1)} %constant_dynamic-update-slice_fusion.2.refs_0_), channel_id=1, source_target_pairs={{0,4},{4,0},{8,12},{12,8},{16,20},{20,16},{24,28},{28,24},{1,5},{5... | collective-permute-start | bytes 393224 | tf_op jit(solution)/shard_map/ppermute | solution.py:274
  16.8 3.7 %shard_map.57 = (bf16[12,512,768]{2,1,0:T(8,128)(2,1)S(1)}, bf16[512,128]{1,0:T(8,128)(2,1)}) custom-call(bf16[512,128]{1,0:T(8,128)(2,1)S(1)} %constant_dynamic-update-slice_fusion.2.refs_0_, f32[256,768]{1,0:T(8,128)S(1)} %get-tuple-element.15.refs_1_, f32[256,768]{1,0:T(8,128)S(1)} %get-tuple-element.16.refs_2_, ...), custom_call_target="tpu_custom_call" | custom-call | flops 37748736 | bytes 9437184 | tf_op jit(solution)/shard_map/pallas_call | solution.py:279
  20.5 0.0 collective-permute-done.2.refs_5_
  20.5 0.0 copy-start.1
  20.5 0.8 %copy-done.1 = bf16[2,2,128,32]{2,3,1,0:T(8,128)(2,1)S(1)} copy-done((bf16[2,2,128,32]{2,3,1,0:T(8,128)(2,1)S(1)}, bf16[2,2,128,32]{2,3,1,0:T(8,128)(2,1)}, u32[]{:S(2)}) %copy-start.1) | copy-done | bytes 32792
  21.3 0.0 copy-start.6
  21.3 0.7 %copy-done.6 = s32[256]{0:T(256)S(1)} copy-done((s32[256]{0:T(256)S(1)}, s32[256]{0:T(256)}, u32[]{:S(2)}) %copy-start.6) | copy-done | bytes 1048
  22.0 15.4 %shard_map.58 = f32[3,96,192]{2,1,0:T(8,128)} custom-call(s32[3]{0:T(128)S(1)} %pad_add_fusion.refs_1_.refs_0_, s32[1,256]{1,0:T(1,128)S(1)} %bitcast.17, bf16[128,128]{1,0:T(8,128)(2,1)S(1)} %bitcast.12, bf16[128,128]{1,0:T(8,128)(2,1)S(1)} %collective-permute-done.refs_3_, bf16[256,128]{1,0:T(8,128)(2,1)S(1)} %collective-permute-done.1.refs_4_, ...), custom_call_target="tpu_custom_call" | custom-call | flops 9663676416 | bytes 18874368 | tf_op jit(solution)/shard_map/pallas_call | solution.py:304
  (4 shorter events, 0.0 us)
Async XLA Ops:
  0.0 9.8 %collective-permute-start = (bf16[128,128]{1,0:T(8,128)(2,1)}, bf16[128,128]{1,0:T(8,128)(2,1)S(1)}, u32[]{:S(2)}, u32[]{:S(2)}) collective-permute-start(bf16[128,128]{1,0:T(8,128)(2,1)} %bitcast.10), channel_id=1, source_target_pairs={{0,16},{4,20},{8,24},{12,28},{16,0},{20,4},{24,8},{28,12},{1,17},{... | collective-permute-start | bytes 98312 | tf_op jit(solution)/shard_map/ppermute | solution.py:274
  4.1 0.8 %copy-start = (bf16[2,2,128,32]{2,3,1,0:T(8,128)(2,1)S(1)}, bf16[2,2,128,32]{2,3,1,0:T(8,128)(2,1)}, u32[]{:S(2)}) copy-start(bf16[2,2,128,32]{2,3,1,0:T(8,128)(2,1)} %param.5) | copy-start | bytes 98308
  4.9 0.7 %copy-start.2 = (bf16[4,16,16]{2,1,0:T(8,128)(2,1)S(1)}, bf16[4,16,16]{2,1,0:T(8,128)(2,1)}, u32[]{:S(2)}) copy-start(bf16[4,16,16]{2,1,0:T(8,128)(2,1)} %param.6) | copy-start | bytes 6148
  5.6 0.7 %copy-start.3 = (s32[256]{0:T(256)S(1)}, s32[256]{0:T(256)}, u32[]{:S(2)}) copy-start(s32[256]{0:T(256)} %param.8) | copy-start | bytes 3076
  6.3 0.7 %copy-start.4 = (s32[256]{0:T(256)S(1)}, s32[256]{0:T(256)}, u32[]{:S(2)}) copy-start(s32[256]{0:T(256)} %param.9) | copy-start | bytes 3076
  7.0 0.7 %copy-start.5 = (s32[256]{0:T(256)S(1)}, s32[256]{0:T(256)}, u32[]{:S(2)}) copy-start(s32[256]{0:T(256)} %param.7) | copy-start | bytes 3076
  9.9 5.3 %collective-permute-start.1 = (bf16[256,128]{1,0:T(8,128)(2,1)S(1)}, bf16[256,128]{1,0:T(8,128)(2,1)S(1)}, u32[]{:S(2)}, u32[]{:S(2)}) collective-permute-start(bf16[256,128]{1,0:T(8,128)(2,1)S(1)} %constant_dynamic-update-slice_fusion.refs_0_), channel_id=1, source_target_pairs={{0,8},{4,12},{8,0},{12,4},{16,24},{20,28},{24,16},{28,20},{1,9},{5... | collective-permute-start | bytes 196616 | tf_op jit(solution)/shard_map/ppermute | solution.py:274
  15.2 5.3 %collective-permute-start.2 = (bf16[512,128]{1,0:T(8,128)(2,1)S(1)}, bf16[512,128]{1,0:T(8,128)(2,1)S(1)}, u32[]{:S(2)}, u32[]{:S(2)}) collective-permute-start(bf16[512,128]{1,0:T(8,128)(2,1)S(1)} %constant_dynamic-update-slice_fusion.2.refs_0_), channel_id=1, source_target_pairs={{0,4},{4,0},{8,12},{12,8},{16,20},{20,16},{24,28},{28,24},{1,5},{5... | collective-permute-start | bytes 393224 | tf_op jit(solution)/shard_map/ppermute | solution.py:274
  20.5 0.8 %copy-start.1 = (bf16[2,2,128,32]{2,3,1,0:T(8,128)(2,1)S(1)}, bf16[2,2,128,32]{2,3,1,0:T(8,128)(2,1)}, u32[]{:S(2)}) copy-start(bf16[2,2,128,32]{2,3,1,0:T(8,128)(2,1)} %param.5) | copy-start | bytes 98308
  21.3 0.7 %copy-start.6 = (s32[256]{0:T(256)S(1)}, s32[256]{0:T(256)}, u32[]{:S(2)}) copy-start(s32[256]{0:T(256)} %param.7) | copy-start | bytes 3076

commit v4 on v3

--- a/solution.py
+++ b/solution.py
@@ -6,11 +6,11 @@
 from jax.experimental.pallas import tpu as pltpu
 from jax.sharding import PartitionSpec as P
 
-TILE = 256
-STEP = 4
-
-
-def wave_fit(terms=8):
+TILE = 512
+STEP = 8
+
+
+def wave_fit(terms=7):
     nodes = 0.125 + 0.125 * np.cos(np.pi * (np.arange(200) + 0.5) / 200)
     root = np.sqrt(nodes)
     fit = np.polynomial.polynomial.polyfit
@@ -46,22 +46,38 @@
 
 
 def station_column(values, stations):
-    return jnp.broadcast_to(values.astype(jnp.float32), (128, stations)).T
+    return jnp.broadcast_to(values, (128, stations)).T
 
 
 def table_kernel(
-    cells, width, held, place, rows, cols, variant, table, base_re, base_im, pick, spread_re, spread_im, kept
+    cells, width, place, held_in, joined_in, table_in,
+    base_re, base_im, pick, spread_re, spread_im, phase_re, phase_im, held, joined, table, arrived
 ):
-    kept[...] = held[...]
-    stations = rows.shape[1]
+    copies = [
+        pltpu.make_async_copy(source, target, arrived.at[n])
+        for n, (source, target) in enumerate((
+            (joined_in, joined), (table_in, table), (held_in, held),
+        ))
+    ]
+    for copy in copies:
+        copy.start()
+    for copy in copies:
+        copy.wait()
+    stations = joined.shape[1]
     steps, lanes = spread_re.shape[0], spread_re.shape[2]
     taps = table.shape[1]
     variants = table.shape[0] // taps
     first_row = place[1].astype(jnp.float32)
     first_col = place[2].astype(jnp.float32)
-    pick[...] = station_column(variant[...], stations).astype(jnp.int32)
-    row_of = station_column(rows[...], stations)
-    col_of = station_column(cols[...], stations)
+    code = joined[...].astype(jnp.float32)
+    rows = jnp.floor((code + 0.5) * (1.0 / (cells * variants)))
+    code = code - rows * float(cells * variants)
+    cols = jnp.floor((code + 0.5) * (1.0 / variants))
+    pick[...] = station_column(code - cols * float(variants), stations).astype(jnp.int32)
+    row_of = station_column(rows, stations)
+    col_of = station_column(cols, stations)
+    start = first_row + float(STEP) * whole_of((steps, stations), 0).astype(jnp.float32)
+    phase_re[...], phase_im[...] = wave(start * rows, cells)
 
     def down_across(shape, start):
         lane = whole_of(shape, 1) + start
@@ -70,10 +86,16 @@
             down = jnp.where(lane >= p * width, float(p), down)
         return down, lane.astype(jnp.float32) - down * width + first_col
 
-    for tile in range(lanes // 128):
+    half = lanes // 2
+    leap_re, leap_im = wave(row_of * float(STEP // 2), cells)
+    for tile in range(half // 128):
         at = slice(tile * 128, (tile + 1) * 128)
+        later = slice(half + tile * 128, half + (tile + 1) * 128)
         down, across = down_across((stations, 128), tile * 128)
-        base_re[:, at], base_im[:, at] = wave(row_of * down + col_of * across, cells)
+        real, imag = wave(row_of * down + col_of * across, cells)
+        base_re[:, at], base_im[:, at] = real, imag
+        base_re[:, later] = real * leap_re - imag * leap_im
+        base_im[:, later] = real * leap_im + imag * leap_re
 
     down, across = down_across((taps, lanes), 0)
     tap = whole_of((taps, lanes), 0).astype(jnp.float32)
@@ -108,38 +130,41 @@
 def response_kernel(first, held, base_re, base_im, pick, spread_re, spread_im, response, kept):
     kept[...] = held[...]
     parts, stations, lanes = response.shape[0], base_re.shape[0], base_re.shape[1]
-
-    def two(i, carry):
+    joint = 2 if parts % 2 == 0 else 1
+
+    def some(i, carry):
         for tile in range(lanes // 128):
             at = slice(tile * 128, (tile + 1) * 128)
-            tables = [(spread_re[first + 2 * i + j, :, at], spread_im[first + 2 * i + j, :, at]) for j in range(2)]
+            tables = [
+                (spread_re[first + joint * i + j, :, at], spread_im[first + joint * i + j, :, at]) for j in range(joint)
+            ]
             for group in range(stations // 16):
-                made = [([], []), ([], [])]
+                made = [([], []) for j in range(joint)]
                 for half in range(2):
                     sub = slice(group * 16 + half * 8, group * 16 + half * 8 + 8)
                     index = pick[sub, :]
                     br = base_re[sub, at]
                     bi = base_im[sub, at]
-                    for j in range(2):
+                    for j in range(joint):
                         sr = jnp.take_along_axis(tables[j][0], index, axis=0)
                         si = jnp.take_along_axis(tables[j][1], index, axis=0)
                         made[j][0].append(br * sr - bi * si)
                         made[j][1].append(br * si + bi * sr)
                 pair = slice(group * 16, group * 16 + 16)
                 low = slice(stations + group * 16, stations + group * 16 + 16)
-                for j in range(2):
-                    response[2 * i + j, pair, at] = jnp.concatenate(made[j][0], axis=0).astype(jnp.bfloat16)
-                    response[2 * i + j, low, at] = jnp.concatenate(made[j][1], axis=0).astype(jnp.bfloat16)
+                for j in range(joint):
+                    response[joint * i + j, pair, at] = jnp.concatenate(made[j][0], axis=0).astype(jnp.bfloat16)
+                    response[joint * i + j, low, at] = jnp.concatenate(made[j][1], axis=0).astype(jnp.bfloat16)
         return carry
 
-    lax.fori_loop(0, parts // 2, two, 0)
+    lax.fori_loop(0, parts // joint, some, 0)
 
 
 def image_kernel(
-    cells, chans, width, norm, masks, groups, place, rows, *refs
+    chans, width, norm, masks, groups, place, phase_re, phase_im, *refs
 ):
     blocks, responses = refs[:groups[0]], refs[groups[0]:sum(groups)]
-    out, turned, volt_re, volt_im, phase_re, phase_im, x_a, x_b, f_a, f_b, sums, strips = refs[sum(groups):]
+    out, turned, volt_re, volt_im, x_a, x_b, f_a, f_b, sums, strips = refs[sum(groups):]
     planes, stations = volt_re.shape
     steps, lanes = phase_re.shape[0], responses[0].shape[2]
     sheets = turned.shape[0]
@@ -156,9 +181,6 @@
         target = volt_re if sheet < sheets // 2 else volt_im
         at = sheet % (sheets // 2) * chans
         target[at:at + chans, :] = turned[sheet].T
-    start = place[1].astype(jnp.float32) + float(STEP) * whole_of((steps, stations), 0).astype(jnp.float32)
-    phase_re[...], phase_im[...] = wave(start * rows[...].astype(jnp.float32), cells)
-
     def prepare(q, x_out):
         pr = phase_re[pl.ds(q, 1), :]
         pi = phase_im[pl.ds(q, 1), :]
@@ -193,30 +215,36 @@
 
     tiles = lanes // TILE
     fields = (f_a, f_b)
+    xs = (x_a, x_b)
     prepare(0, x_a)
     f_b[...] = jnp.zeros_like(f_b)
-    for part, response in enumerate(responses):
-        base = part * response.shape[0]
+
+    def chunk(q, turn, response, index):
+        for n in range(tiles):
+            side = (turn * tiles + n) % 2
+            fields[side][...] = jnp.dot(
+                xs[turn][...], response[index, :, n * TILE:(n + 1) * TILE], preferred_element_type=jnp.float32
+            )
+            if n == 0:
+                collect(jnp.maximum(q - 1, 0), tiles - 1, fields[1 - side])
+                prepare(jnp.minimum(q + 1, steps - 1), xs[1 - turn])
+            else:
+                collect(q, n - 1, fields[1 - side])
+
+    base, turn = 0, 0
+    for response in responses:
+        here = response.shape[0]
 
         def two(i, carry):
-            q = base + 2 * i
-            for n in range(2 * tiles):
-                x = x_a if n < tiles else x_b
-                at = slice(n % tiles * TILE, (n % tiles + 1) * TILE)
-                fields[n % 2][...] = jnp.dot(
-                    x[...], response[2 * i + n // tiles, :, at], preferred_element_type=jnp.float32
-                )
-                if n == 0:
-                    collect(jnp.maximum(q - 1, 0), tiles - 1, fields[1])
-                    prepare(q + 1, x_b)
-                else:
-                    collect(q + (n - 1) // tiles, (n - 1) % tiles, fields[1 - n % 2])
-                if n == tiles:
-                    prepare(jnp.minimum(q + 2, steps - 1), x_a)
+            for j in range(2):
+                chunk(base + 2 * i + j, (turn + j) % 2, response, 2 * i + j)
             return carry
 
-        lax.fori_loop(0, response.shape[0] // 2, two, 0)
-    collect(steps - 1, tiles - 1, fields[1])
+        lax.fori_loop(0, here // 2, two, 0)
+        if here % 2:
+            chunk(base + here - 1, turn, response, here - 1)
+        base, turn = base + here, (turn + here) % 2
+    collect(steps - 1, tiles - 1, fields[(steps * tiles - 1) % 2])
     for k in range(3):
         for p in range(STEP):
             for j in range(strips.shape[0]):
@@ -247,11 +275,10 @@
     bits = []
     while (1 << len(bits)) < count:
         bits.append(count >> (len(bits) + 1))
+    hbm = pl.BlockSpec(memory_space=pltpu.HBM)
+    joined = ((station_rows * cells + station_cols) * variants + kernel_offset).reshape(1, stations)
     own = voltages.transpose(0, 1, 3, 2).reshape(2 * times * voltages.shape[3], chans)
-    held, blocks, masks, reach = own, [own], [(0,)], (0,)
-
-    lines = [v.reshape(1, stations) for v in (station_rows, station_cols, kernel_offset)]
-    make_tables = lambda held: pl.pallas_call(
+    *tables, phase_re, phase_im, held = pl.pallas_call(
         lambda *refs: table_kernel(cells, width, *refs),
         out_shape=[
             jax.ShapeDtypeStruct((stations, lanes), f32),
@@ -259,23 +286,29 @@
             jax.ShapeDtypeStruct((stations, 128), jnp.int32),
             jax.ShapeDtypeStruct((steps, 8, lanes), f32),
             jax.ShapeDtypeStruct((steps, 8, lanes), f32),
-            jax.ShapeDtypeStruct(held.shape, bf16),
+            jax.ShapeDtypeStruct((steps, stations), f32),
+            jax.ShapeDtypeStruct((steps, stations), f32),
+            jax.ShapeDtypeStruct(own.shape, bf16),
         ],
-        in_specs=[vmem, smem, vmem, vmem, vmem, vmem],
-        out_specs=[vmem] * 6,
+        in_specs=[smem] + [hbm] * 3,
+        out_specs=[vmem] * 8,
+        scratch_shapes=[
+            pltpu.VMEM((1, stations), jnp.int32),
+            pltpu.VMEM((variants * taps, taps), bf16),
+            pltpu.SemaphoreType.DMA((3,)),
+        ],
         compiler_params=pltpu.CompilerParams(vmem_limit_bytes=16 * mib),
         cost_estimate=pl.CostEstimate(flops=100 * stations * lanes, bytes_accessed=16 * stations * lanes, transcendentals=0),
-    )(held, place, *lines, kernel_table.reshape(variants * taps, taps))
-
-    ahead = steps // 4 * 2
-    shares = [(0, steps - ahead), (steps - ahead, ahead)]
+    )(place, own, joined, kernel_table.reshape(variants * taps, taps))
+
+    blocks, masks, reach = [held], [(0,)], (0,)
+    shares = [(k * (steps // 3), steps // 3) for k in range(2)]
+    shares.append((steps // 3 * 2, steps - steps // 3 * 2))
     responses = []
     for cut, bit in enumerate(bits):
         came = lax.ppermute(held, "chan", [(j, j ^ bit) for j in range(count)])
-        if cut == 0:
-            *tables, held = make_tables(held)
-        elif cut <= len(shares):
-            first, part = shares[cut - 1]
+        if cut < len(shares):
+            first, part = shares[cut]
             response, held = pl.pallas_call(
                 lambda *refs, first=first: response_kernel(first, *refs),
                 out_shape=[
@@ -302,16 +335,14 @@
     ]
     groups = (len(blocks), len(responses))
     return pl.pallas_call(
-        lambda *refs: image_kernel(cells, chans, width, norm, masks, groups, *refs),
+        lambda *refs: image_kernel(chans, width, norm, masks, groups, *refs),
         out_shape=jax.ShapeDtypeStruct((3, height, width), f32),
-        in_specs=[smem] + [vmem] * (1 + sum(groups)),
+        in_specs=[smem] + [vmem] * (2 + sum(groups)),
         out_specs=vmem,
         scratch_shapes=[
             pltpu.VMEM((2 * times, stations, chans), f32),
             pltpu.VMEM((planes, stations), f32),
             pltpu.VMEM((planes, stations), f32),
-            pltpu.VMEM((steps, stations), f32),
-            pltpu.VMEM((steps, stations), f32),
             pltpu.VMEM((2 * planes, 2 * stations), bf16),
             pltpu.VMEM((2 * planes, 2 * stations), bf16),
             pltpu.VMEM((2 * planes, TILE), f32),
@@ -323,7 +354,7 @@
         cost_estimate=pl.CostEstimate(
             flops=8 * steps * planes * stations * lanes, bytes_accessed=4 * steps * stations * lanes, transcendentals=0
         ),
-    )(place, lines[0], *blocks, *responses)
+    )(place, phase_re, phase_im, *blocks, *responses)
 
 
 def solution(mesh):

time: 37.7 us -> 37.4 us (level)
  waiting for transfers between devices: 0.01 us -> 3.68 us
  local copies, waits for them, and re-layouts: 4.98 us -> 1.51 us
  Pallas kernels: 25 us -> 23.8 us
  other arithmetic: 0.08 us -> 0.79 us
    ppermute x3, waiting for transfers between devices: 0.01 us -> 3.68 us  [local(): came = lax.ppermute(held, 'chan', [(j, j ^ bit) for j in range(count)])]
    unnamed x16 -> x6, local copies, waits for them, and re-layouts: 4.96 us -> 1.48 us
    pallas_call x1, Pallas kernels: 15.4 us -> 13.7 us  [local(): pl.pallas_call(lambda *refs: image_kernel(chans, width, norm, masks, grou...]
    add x0 -> x1, other arithmetic: none -> 0.72 us  [local(): (station_rows * cells + station_cols) * variants + kernel_offset]
    pallas_call x1, Pallas kernels: 2.2 us -> 2.73 us  [local(): pl.pallas_call(lambda *refs: table_kernel(cells, width, *refs), out_shape...]
    pallas_call x2 -> x3, Pallas kernels: 7.38 us -> 7.35 us  [local(): pl.pallas_call(lambda *refs, first=first: response_kernel(first, *refs),...]
  transfers between devices with their start and end apart: 3 -> 3, of which waited for: 0 -> 2; matrix products, arithmetic and copies ran while one was open for 0% -> 0% of each run, Pallas kernels for 26% -> 13%
where the time goes in v4:
time: 37.4 us; the launch traced here: 37.1 us
  Pallas kernels  23.8 us (64%)
  starting transfers between devices  7.33 us (20%)
  waiting for transfers between devices  3.68 us (10%)
  local copies, waits for them, and re-layouts  1.51 us (4%)
  other arithmetic  0.79 us (2%)
    pallas_call x1, Pallas kernels, local(): pl.pallas_call(lambda *refs: image_kernel(chans, width, norm, masks, grou...  13.7 us
    pallas_call x3, Pallas kernels, local(): pl.pallas_call(lambda *refs, first=first: response_kernel(first, *refs),...  7.35 us
    ppermute x3, starting transfers between devices, local(): came = lax.ppermute(held, 'chan', [(j, j ^ bit) for j in range(count)])  7.33 us
    ppermute x3, waiting for transfers between devices, local(): came = lax.ppermute(held, 'chan', [(j, j ^ bit) for j in range(count)])  3.68 us
    pallas_call x1, Pallas kernels, local(): pl.pallas_call(lambda *refs: table_kernel(cells, width, *refs), out_shape...  2.73 us
    unnamed x6, local copies, waits for them, and re-layouts  1.48 us
  transfers between devices with their start and end apart: 3, of which 2 were waited for; matrix products, arithmetic and copies ran while one was open for 0% of the time, Pallas kernels for 13%

profile of v4, /device:TPU:0, one launch (start us, length us, event | category | flops | bytes accessed | tf_op | source)
XLA Modules:
  0.0 37.1 jit_solution(13493256847099772299)
XLA Ops:
  0.0 0.1 pad_add_fusion.refs_0_
  0.1 0.7 %multiply_add_fusion = s32[256]{0:T(256)S(1)} fusion(s32[256]{0:T(256)} %param.9, s32[256]{0:T(256)} %param.8, s32[256]{0:T(256)} %param.7), kind=kLoop, calls=%fused_computation.4 | loop fusion | flops 1024 | bytes 4096 | tf_op jit(solution)/shard_map/add | solution.py:279
  0.8 0.0 copy-start
  0.8 0.8 %copy-done = bf16[2,2,128,32]{2,3,1,0:T(8,128)(2,1)S(1)} copy-done((bf16[2,2,128,32]{2,3,1,0:T(8,128)(2,1)S(1)}, bf16[2,2,128,32]{2,3,1,0:T(8,128)(2,1)}, u32[]{:S(2)}) %copy-start) | copy-done | bytes 32792
  1.6 0.0 copy-start.1
  1.6 0.7 %copy-done.1 = bf16[4,16,16]{2,1,0:T(8,128)(2,1)S(1)} copy-done((bf16[4,16,16]{2,1,0:T(8,128)(2,1)S(1)}, bf16[4,16,16]{2,1,0:T(8,128)(2,1)}, u32[]{:S(2)}) %copy-start.1) | copy-done | bytes 2072
  2.3 2.7 %shard_map.55 = (f32[256,1536]{1,0:T(8,128)S(1)}, f32[256,1536]{1,0:T(8,128)S(1)}, s32[256,128]{1,0:T(8,128)S(1)}, f32[12,8,1536]{2,1,0:T(8,128)S(1)}, f32[12,8,...) custom-call(s32[3]{0:T(128)S(1)} %pad_add_fusion.refs_0_, ...), custom_call_target="tpu_custom_call" | custom-call | flops 39321600 | bytes 6291456 | tf_op jit(solution)/shard_map/pallas_call | solution.py:281
  5.0 4.1 %collective-permute-start = (bf16[128,128]{1,0:T(8,128)(2,1)S(1)}, bf16[128,128]{1,0:T(8,128)(2,1)S(1)}, u32[]{:S(2)}, u32[]{:S(2)}) collective-permute-start(bf16[128,128]{1,0:T(8,128)(2,1)S(1)} %get-tuple-element.20.refs_0_.refs_3_), channel_id=1, source_target_pairs={{0,16},{4,20},{8,24},{12,28},{16,0},{20,4},{24,8},{28,12},{1,17},{... | collective-permute-start | bytes 98312 | tf_op jit(solution)/shard_map/ppermute | solution.py:309
  9.1 2.4 %shard_map.56 = (bf16[4,512,1536]{2,1,0:T(8,128)(2,1)S(1)}, bf16[128,128]{1,0:T(8,128)(2,1)S(1)}) custom-call(bf16[128,128]{1,0:T(8,128)(2,1)S(1)} %get-tuple-element.20.refs_0_.refs_3_, f32[256,1536]{1,0:T(8,128)S(1)} %get-tuple-element.21.refs_1_, f32[256,1536]{1,0:T(8,128)S(1)} %get-tuple-element.22.refs_2_, s32[256,128]{1,0:T(8,128)S(1)} %get-tuple-element.23.refs_3_, ...), custom_call_target="tpu_custom_call" | custom-call | flops 25165824 | bytes 6291456 | tf_op jit(solution)/shard_map/pallas_call | solution.py:312
  11.6 0.0 collective-permute-done.refs_4_
  11.6 2.4 %shard_map.57 = (bf16[4,512,1536]{2,1,0:T(8,128)(2,1)S(1)}, bf16[256,128]{1,0:T(8,128)(2,1)S(1)}) custom-call(bf16[256,128]{1,0:T(8,128)(2,1)S(1)} %constant_dynamic-update-slice_fusion.refs_0_, f32[256,1536]{1,0:T(8,128)S(1)} %get-tuple-element.21.refs_1_, f32[256,1536]{1,0:T(8,128)S(1)} %get-tuple-element.22.refs_2_, ...), custom_call_target="tpu_custom_call" | custom-call | flops 25165824 | bytes 6291456 | tf_op jit(solution)/shard_map/pallas_call | solution.py:312
  14.0 1.6 %collective-permute-start.1 = (bf16[256,128]{1,0:T(8,128)(2,1)S(1)}, bf16[256,128]{1,0:T(8,128)(2,1)S(1)}, u32[]{:S(2)}, u32[]{:S(2)}) collective-permute-start(bf16[256,128]{1,0:T(8,128)(2,1)S(1)} %constant_dynamic-update-slice_fusion.refs_0_), channel_id=1, source_target_pairs={{0,8},{4,12},{8,0},{12,4},{16,24},{20,28},{24,16},{28,20},{1,9},{5... | collective-permute-start | bytes 196616 | tf_op jit(solution)/shard_map/ppermute | solution.py:309
  15.7 2.7 %collective-permute-done.1.refs_5_ = bf16[256,128]{1,0:T(8,128)(2,1)S(1)} collective-permute-done((bf16[256,128]{1,0:T(8,128)(2,1)S(1)}, bf16[256,128]{1,0:T(8,128)(2,1)S(1)}, u32[]{:S(2)}, u32[]{:S(2)}) %collective-permute-start.1) | collective-permute-done | bytes 65568 | tf_op jit(solution)/shard_map/ppermute | solution.py:309
  18.4 1.6 %collective-permute-start.2 = (bf16[512,128]{1,0:T(8,128)(2,1)S(1)}, bf16[512,128]{1,0:T(8,128)(2,1)S(1)}, u32[]{:S(2)}, u32[]{:S(2)}) collective-permute-start(bf16[512,128]{1,0:T(8,128)(2,1)S(1)} %constant_dynamic-update-slice_fusion.2.refs_0_), channel_id=1, source_target_pairs={{0,4},{4,0},{8,12},{12,8},{16,20},{20,16},{24,28},{28,24},{1,5},{5... | collective-permute-start | bytes 393224 | tf_op jit(solution)/shard_map/ppermute | solution.py:309
  20.0 2.5 %shard_map.58 = (bf16[4,512,1536]{2,1,0:T(8,128)(2,1)S(1)}, bf16[512,128]{1,0:T(8,128)(2,1)}) custom-call(bf16[512,128]{1,0:T(8,128)(2,1)S(1)} %constant_dynamic-update-slice_fusion.2.refs_0_, f32[256,1536]{1,0:T(8,128)S(1)} %get-tuple-element.21.refs_1_, f32[256,1536]{1,0:T(8,128)S(1)} %get-tuple-element.22.refs_2_, ...), custom_call_target="tpu_custom_call" | custom-call | flops 25165824 | bytes 6291456 | tf_op jit(solution)/shard_map/pallas_call | solution.py:312
  22.4 1.0 %collective-permute-done.2.refs_6_ = bf16[512,128]{1,0:T(8,128)(2,1)S(1)} collective-permute-done((bf16[512,128]{1,0:T(8,128)(2,1)S(1)}, bf16[512,128]{1,0:T(8,128)(2,1)S(1)}, u32[]{:S(2)}, u32[]{:S(2)}) %collective-permute-start.2) | collective-permute-done | bytes 131104 | tf_op jit(solution)/shard_map/ppermute | solution.py:309
  23.4 13.7 %shard_map.59 = f32[3,96,192]{2,1,0:T(8,128)} custom-call(s32[3]{0:T(128)S(1)} %pad_add_fusion.refs_0_, f32[12,256]{1,0:T(8,128)S(1)} %get-tuple-element.18.refs_1_, f32[12,256]{1,0:T(8,128)S(1)} %get-tuple-element.19.refs_2_, bf16[128,128]{1,0:T(8,128)(2,1)S(1)} %get-tuple-element.20.refs_0_.refs_3_, bf16[128,128]{1,0:T(8,128)(2,1)S(1)} %collective-permute-done.refs_4_, ...), custom_call_target="tpu_custom_call" | custom-call | flops 9663676416 | bytes 18874368 | tf_op jit(solution)/shard_map/pallas_call | solution.py:337
  (4 shorter events, 0.0 us)
Async XLA Ops:
  0.8 0.8 %copy-start = (bf16[2,2,128,32]{2,3,1,0:T(8,128)(2,1)S(1)}, bf16[2,2,128,32]{2,3,1,0:T(8,128)(2,1)}, u32[]{:S(2)}) copy-start(bf16[2,2,128,32]{2,3,1,0:T(8,128)(2,1)} %param.5) | copy-start | bytes 98308
  1.6 0.7 %copy-start.1 = (bf16[4,16,16]{2,1,0:T(8,128)(2,1)S(1)}, bf16[4,16,16]{2,1,0:T(8,128)(2,1)}, u32[]{:S(2)}) copy-start(bf16[4,16,16]{2,1,0:T(8,128)(2,1)} %param.6) | copy-start | bytes 6148
  5.0 6.6 %collective-permute-start = (bf16[128,128]{1,0:T(8,128)(2,1)S(1)}, bf16[128,128]{1,0:T(8,128)(2,1)S(1)}, u32[]{:S(2)}, u32[]{:S(2)}) collective-permute-start(bf16[128,128]{1,0:T(8,128)(2,1)S(1)} %get-tuple-element.20.refs_0_.refs_3_), channel_id=1, source_target_pairs={{0,16},{4,20},{8,24},{12,28},{16,0},{20,4},{24,8},{28,12},{1,17},{... | collective-permute-start | bytes 98312 | tf_op jit(solution)/shard_map/ppermute | solution.py:309
  14.0 4.3 %collective-permute-start.1 = (bf16[256,128]{1,0:T(8,128)(2,1)S(1)}, bf16[256,128]{1,0:T(8,128)(2,1)S(1)}, u32[]{:S(2)}, u32[]{:S(2)}) collective-permute-start(bf16[256,128]{1,0:T(8,128)(2,1)S(1)} %constant_dynamic-update-slice_fusion.refs_0_), channel_id=1, source_target_pairs={{0,8},{4,12},{8,0},{12,4},{16,24},{20,28},{24,16},{28,20},{1,9},{5... | collective-permute-start | bytes 196616 | tf_op jit(solution)/shard_map/ppermute | solution.py:309
  18.4 5.0 %collective-permute-start.2 = (bf16[512,128]{1,0:T(8,128)(2,1)S(1)}, bf16[512,128]{1,0:T(8,128)(2,1)S(1)}, u32[]{:S(2)}, u32[]{:S(2)}) collective-permute-start(bf16[512,128]{1,0:T(8,128)(2,1)S(1)} %constant_dynamic-update-slice_fusion.2.refs_0_), channel_id=1, source_target_pairs={{0,4},{4,0},{8,12},{12,8},{16,20},{20,16},{24,28},{28,24},{1,5},{5... | collective-permute-start | bytes 393224 | tf_op jit(solution)/shard_map/ppermute | solution.py:309

commit v5 on v4

--- a/solution.py
+++ b/solution.py
@@ -6,7 +6,7 @@
 from jax.experimental.pallas import tpu as pltpu
 from jax.sharding import PartitionSpec as P
 
-TILE = 512
+TILE = 256
 STEP = 8
 
 
@@ -164,7 +164,7 @@
     chans, width, norm, masks, groups, place, phase_re, phase_im, *refs
 ):
     blocks, responses = refs[:groups[0]], refs[groups[0]:sum(groups)]
-    out, turned, volt_re, volt_im, x_a, x_b, f_a, f_b, sums, strips = refs[sum(groups):]
+    out, turned, volt_re, volt_im, x_a, x_b, sums, strips = refs[sum(groups):]
     planes, stations = volt_re.shape
     steps, lanes = phase_re.shape[0], responses[0].shape[2]
     sheets = turned.shape[0]
@@ -177,59 +177,60 @@
             for sheet in range(sheets):
                 line = (n * sheets + sheet) * each
                 turned[sheet, pl.ds(at, each), :] = value[line:line + each]
+    times = sheets // 2
     for sheet in range(sheets):
-        target = volt_re if sheet < sheets // 2 else volt_im
-        at = sheet % (sheets // 2) * chans
-        target[at:at + chans, :] = turned[sheet].T
+        target = volt_re if sheet < times else volt_im
+        facing = turned[sheet].T
+        for g in range(chans // 8):
+            at = (g * times + sheet % times) * 8
+            target[at:at + 8, :] = facing[g * 8:g * 8 + 8]
+    span = 8 * times
+
     def prepare(q, x_out):
         pr = phase_re[pl.ds(q, 1), :]
         pi = phase_im[pl.ds(q, 1), :]
-        vr = volt_re[...]
-        vi = volt_im[...]
-        xr = (vr * pr - vi * pi).astype(jnp.bfloat16)
-        xi = (vr * pi + vi * pr).astype(jnp.bfloat16)
-        x_out[:planes, :stations] = xr
-        x_out[:planes, stations:] = -xi
-        x_out[planes:, :stations] = xi
-        x_out[planes:, stations:] = xr
-
-    step_of = (2.0 * whole_of((8, TILE), 0).astype(jnp.float32) + 1.0 - chans) * 0.0625
+        for g in range(chans // 8):
+            vr = volt_re[g * span:(g + 1) * span, :]
+            vi = volt_im[g * span:(g + 1) * span, :]
+            xr = (vr * pr - vi * pi).astype(jnp.bfloat16)
+            xi = (vr * pi + vi * pr).astype(jnp.bfloat16)
+            real = slice(2 * g * span, (2 * g + 1) * span)
+            imag = slice((2 * g + 1) * span, (2 * g + 2) * span)
+            x_out[real, :stations] = xr
+            x_out[real, stations:] = -xi
+            x_out[imag, :stations] = xi
+            x_out[imag, stations:] = xr
+
+    top = chans // 8
+    step_of = top + (2.0 * whole_of((8, TILE), 0).astype(jnp.float32) + 1.0 - chans) * 0.0625
 
     def collect(q, tile, field):
-        zero = jnp.zeros((8, TILE), jnp.float32)
-        s0, s1, s2 = zero, zero, zero
-        for g in range(chans // 8 - 1, -1, -1):
-            for t in range(2 * planes // chans):
-                line = t * chans + g * 8
+        s0, s1, s2 = None, None, None
+        for g in range(top):
+            for t in range(2 * times):
+                line = (g * 2 * times + t) * 8
                 part = field[line:line + 8, :]
                 total = part * part if t == 0 else total + part * part
-            s0 = s0 + total
-            s1 = s1 + s0
-            s2 = s2 + s1
-        g1 = s1 - s0
-        g2 = 2.0 * s2 - 3.0 * s1 + s0
-        first = g1 + step_of * s0
-        second = g2 + step_of * (2.0 * g1 + step_of * s0)
+            s0 = total if g == 0 else s0 + total
+            s1 = s0 if g == 0 else s1 + s0
+            s2 = s1 if g == 0 else s2 + s1
+        first = step_of * s0 - s1
+        second = step_of * (step_of * s0 - 2.0 * s1) + (2.0 * s2 - s1)
         for k, value in enumerate((s0, first, second)):
             sums[k, pl.ds(q, 1), tile * TILE:(tile + 1) * TILE] = norm[k] * jnp.sum(value, axis=0, keepdims=True)
 
     tiles = lanes // TILE
-    fields = (f_a, f_b)
     xs = (x_a, x_b)
     prepare(0, x_a)
-    f_b[...] = jnp.zeros_like(f_b)
 
     def chunk(q, turn, response, index):
         for n in range(tiles):
-            side = (turn * tiles + n) % 2
-            fields[side][...] = jnp.dot(
+            field = jnp.dot(
                 xs[turn][...], response[index, :, n * TILE:(n + 1) * TILE], preferred_element_type=jnp.float32
             )
             if n == 0:
-                collect(jnp.maximum(q - 1, 0), tiles - 1, fields[1 - side])
                 prepare(jnp.minimum(q + 1, steps - 1), xs[1 - turn])
-            else:
-                collect(q, n - 1, fields[1 - side])
+            collect(q, n, field)
 
     base, turn = 0, 0
     for response in responses:
@@ -244,7 +245,6 @@
         if here % 2:
             chunk(base + here - 1, turn, response, here - 1)
         base, turn = base + here, (turn + here) % 2
-    collect(steps - 1, tiles - 1, fields[(steps * tiles - 1) % 2])
     for k in range(3):
         for p in range(STEP):
             for j in range(strips.shape[0]):
@@ -278,7 +278,7 @@
     hbm = pl.BlockSpec(memory_space=pltpu.HBM)
     joined = ((station_rows * cells + station_cols) * variants + kernel_offset).reshape(1, stations)
     own = voltages.transpose(0, 1, 3, 2).reshape(2 * times * voltages.shape[3], chans)
-    *tables, phase_re, phase_im, held = pl.pallas_call(
+    make_tables = lambda: pl.pallas_call(
         lambda *refs: table_kernel(cells, width, *refs),
         out_shape=[
             jax.ShapeDtypeStruct((stations, lanes), f32),
@@ -301,14 +301,15 @@
         cost_estimate=pl.CostEstimate(flops=100 * stations * lanes, bytes_accessed=16 * stations * lanes, transcendentals=0),
     )(place, own, joined, kernel_table.reshape(variants * taps, taps))
 
-    blocks, masks, reach = [held], [(0,)], (0,)
-    shares = [(k * (steps // 3), steps // 3) for k in range(2)]
-    shares.append((steps // 3 * 2, steps - steps // 3 * 2))
-    responses = []
+    ahead = steps // 2
+    shares = [(0, steps - ahead), (steps - ahead, ahead)]
+    held, reach, responses = own, (0,), []
     for cut, bit in enumerate(bits):
         came = lax.ppermute(held, "chan", [(j, j ^ bit) for j in range(count)])
-        if cut < len(shares):
-            first, part = shares[cut]
+        if cut == 0:
+            *tables, phase_re, phase_im, held = make_tables()
+        elif cut <= len(shares):
+            first, part = shares[cut - 1]
             response, held = pl.pallas_call(
                 lambda *refs, first=first: response_kernel(first, *refs),
                 out_shape=[
@@ -323,10 +324,10 @@
                 ),
             )(held, *tables)
             responses.append(response)
-        blocks.append(came)
-        masks.append(tuple(m ^ bit for m in reach))
-        reach = reach + masks[-1]
-        held = jnp.concatenate([held, came])
+        masks = [reach, tuple(m ^ bit for m in reach)]
+        reach = sum(masks, ())
+        blocks = [held, came]
+        held = jnp.concatenate(blocks)
 
     x = (2.0 * np.arange(chans) + 1.0 - chans) / chans
     norm = [
@@ -345,8 +346,6 @@
             pltpu.VMEM((planes, stations), f32),
             pltpu.VMEM((2 * planes, 2 * stations), bf16),
             pltpu.VMEM((2 * planes, 2 * stations), bf16),
-            pltpu.VMEM((2 * planes, TILE), f32),
-            pltpu.VMEM((2 * planes, TILE), f32),
             pltpu.VMEM((3, steps, lanes + 128), f32),
             pltpu.VMEM((-(-width // 128), height, 128), f32),
         ],

time: 37.4 us -> 32.7 us (0.87)
  waiting for transfers between devices: 3.68 us -> 0.01 us
  Pallas kernels: 23.8 us -> 22.8 us
    ppermute x3, waiting for transfers between devices: 3.68 us -> 0.01 us  [local(): came = lax.ppermute(held, 'chan', [(j, j ^ bit) for j in range(count)])]
    pallas_call x1, Pallas kernels: 13.7 us -> 12.7 us  [local(): pl.pallas_call(lambda *refs: image_kernel(chans, width, norm, masks, grou...]
    pallas_call x3 -> x2, Pallas kernels: 7.35 us -> 7.34 us  [local(): pl.pallas_call(lambda *refs, first=first: response_kernel(first, *refs),...]
  transfers between devices with their start and end apart: 3 -> 3, of which waited for: 2 -> 0; matrix products, arithmetic and copies ran while one was open for 0% -> 2% of each run, Pallas kernels for 13% -> 31%
where the time goes in v5:
time: 32.7 us; the launch traced here: 32.4 us
  Pallas kernels  22.8 us (70%)
  starting transfers between devices  7.26 us (22%)
  local copies, waits for them, and re-layouts  1.51 us (5%)
  other arithmetic  0.79 us (2%)
    pallas_call x1, Pallas kernels, local(): pl.pallas_call(lambda *refs: image_kernel(chans, width, norm, masks, grou...  12.7 us
    pallas_call x2, Pallas kernels, local(): pl.pallas_call(lambda *refs, first=first: response_kernel(first, *refs),...  7.34 us
    ppermute x3, starting transfers between devices, local(): came = lax.ppermute(held, 'chan', [(j, j ^ bit) for j in range(count)])  7.26 us
    pallas_call x1, Pallas kernels, local(): pl.pallas_call(lambda *refs: table_kernel(cells, width, *refs), out_shape...  2.73 us
    unnamed x6, local copies, waits for them, and re-layouts  1.48 us
    add x1, other arithmetic, local(): (station_rows * cells + station_cols) * variants + kernel_offset  0.72 us
  transfers between devices with their start and end apart: 3, of which 0 were waited for; matrix products, arithmetic and copies ran while one was open for 2% of the time, Pallas kernels for 31%

profile of v5, /device:TPU:0, one launch (start us, length us, event | category | flops | bytes accessed | tf_op | source)
XLA Modules:
  0.0 32.4 jit_solution(15509953299651304639)
XLA Ops:
  0.0 4.0 %collective-permute-start = (bf16[128,128]{1,0:T(8,128)(2,1)}, bf16[128,128]{1,0:T(8,128)(2,1)S(1)}, u32[]{:S(2)}, u32[]{:S(2)}) collective-permute-start(bf16[128,128]{1,0:T(8,128)(2,1)} %bitcast.9), channel_id=1, source_target_pairs={{0,16},{4,20},{8,24},{12,28},{16,0},{20,4},{24,8},{28,12},{1,17},{... | collective-permute-start | bytes 98312 | tf_op jit(solution)/shard_map/ppermute | solution.py:308
  4.0 0.1 pad_add_fusion.refs_0_
  4.1 0.7 %multiply_add_fusion = s32[256]{0:T(256)S(1)} fusion(s32[256]{0:T(256)} %param.9, s32[256]{0:T(256)} %param.8, s32[256]{0:T(256)} %param.7), kind=kLoop, calls=%fused_computation.4 | loop fusion | flops 1024 | bytes 4096 | tf_op jit(solution)/shard_map/add | solution.py:279
  4.8 0.0 copy-start
  4.8 0.8 %copy-done = bf16[2,2,128,32]{2,3,1,0:T(8,128)(2,1)S(1)} copy-done((bf16[2,2,128,32]{2,3,1,0:T(8,128)(2,1)S(1)}, bf16[2,2,128,32]{2,3,1,0:T(8,128)(2,1)}, u32[]{:S(2)}) %copy-start) | copy-done | bytes 32792
  5.6 0.0 copy-start.1
  5.6 0.7 %copy-done.1 = bf16[4,16,16]{2,1,0:T(8,128)(2,1)S(1)} copy-done((bf16[4,16,16]{2,1,0:T(8,128)(2,1)S(1)}, bf16[4,16,16]{2,1,0:T(8,128)(2,1)}, u32[]{:S(2)}) %copy-start.1) | copy-done | bytes 2072
  6.3 2.7 %shard_map.55 = (f32[256,1536]{1,0:T(8,128)S(1)}, f32[256,1536]{1,0:T(8,128)S(1)}, s32[256,128]{1,0:T(8,128)S(1)}, f32[12,8,1536]{2,1,0:T(8,128)S(1)}, f32[12,8,...) custom-call(s32[3]{0:T(128)S(1)} %pad_add_fusion.refs_0_, ...), custom_call_target="tpu_custom_call" | custom-call | flops 39321600 | bytes 6291456 | tf_op jit(solution)/shard_map/pallas_call | solution.py:281
  9.1 0.0 collective-permute-done
  9.1 1.6 %collective-permute-start.1 = (bf16[256,128]{1,0:T(8,128)(2,1)S(1)}, bf16[256,128]{1,0:T(8,128)(2,1)S(1)}, u32[]{:S(2)}, u32[]{:S(2)}) collective-permute-start(bf16[256,128]{1,0:T(8,128)(2,1)S(1)} %constant_dynamic-update-slice_fusion.refs_0_), channel_id=1, source_target_pairs={{0,8},{4,12},{8,0},{12,4},{16,24},{20,28},{24,16},{28,20},{1,9},{5... | collective-permute-start | bytes 196616 | tf_op jit(solution)/shard_map/ppermute | solution.py:308
  10.7 3.7 %shard_map.56 = (bf16[6,512,1536]{2,1,0:T(8,128)(2,1)S(1)}, bf16[256,128]{1,0:T(8,128)(2,1)S(1)}) custom-call(bf16[256,128]{1,0:T(8,128)(2,1)S(1)} %constant_dynamic-update-slice_fusion.refs_0_, f32[256,1536]{1,0:T(8,128)S(1)} %get-tuple-element.20.refs_1_, f32[256,1536]{1,0:T(8,128)S(1)} %get-tuple-element.21.refs_2_, ...), custom_call_target="tpu_custom_call" | custom-call | flops 37748736 | bytes 9437184 | tf_op jit(solution)/shard_map/pallas_call | solution.py:313
  14.4 0.0 collective-permute-done.1
  14.4 1.6 %collective-permute-start.2 = (bf16[512,128]{1,0:T(8,128)(2,1)S(1)}, bf16[512,128]{1,0:T(8,128)(2,1)S(1)}, u32[]{:S(2)}, u32[]{:S(2)}) collective-permute-start(bf16[512,128]{1,0:T(8,128)(2,1)S(1)} %constant_dynamic-update-slice_fusion.2.refs_0_), channel_id=1, source_target_pairs={{0,4},{4,0},{8,12},{12,8},{16,20},{20,16},{24,28},{28,24},{1,5},{5... | collective-permute-start | bytes 393224 | tf_op jit(solution)/shard_map/ppermute | solution.py:308
  16.0 3.7 %shard_map.57 = (bf16[6,512,1536]{2,1,0:T(8,128)(2,1)S(1)}, bf16[512,128]{1,0:T(8,128)(2,1)S(1)}) custom-call(bf16[512,128]{1,0:T(8,128)(2,1)S(1)} %constant_dynamic-update-slice_fusion.2.refs_0_, f32[256,1536]{1,0:T(8,128)S(1)} %get-tuple-element.20.refs_1_, f32[256,1536]{1,0:T(8,128)S(1)} %get-tuple-element.21.refs_2_, ...), custom_call_target="tpu_custom_call" | custom-call | flops 37748736 | bytes 9437184 | tf_op jit(solution)/shard_map/pallas_call | solution.py:313
  19.7 0.0 collective-permute-done.2.refs_4_
  19.7 12.7 %shard_map.58 = f32[3,96,192]{2,1,0:T(8,128)} custom-call(s32[3]{0:T(128)S(1)} %pad_add_fusion.refs_0_, f32[12,256]{1,0:T(8,128)S(1)} %get-tuple-element.17.refs_1_, f32[12,256]{1,0:T(8,128)S(1)} %get-tuple-element.18.refs_2_, bf16[512,128]{1,0:T(8,128)(2,1)S(1)} %get-tuple-element.26.refs_3_, bf16[512,128]{1,0:T(8,128)(2,1)S(1)} %collective-permute-done.2.refs_4_, ...), custom_call_target="tpu_custom_call" | custom-call | flops 9663676416 | bytes 18874368 | tf_op jit(solution)/shard_map/pallas_call | solution.py:338
  (4 shorter events, 0.0 us)
Async XLA Ops:
  0.0 9.1 %collective-permute-start = (bf16[128,128]{1,0:T(8,128)(2,1)}, bf16[128,128]{1,0:T(8,128)(2,1)S(1)}, u32[]{:S(2)}, u32[]{:S(2)}) collective-permute-start(bf16[128,128]{1,0:T(8,128)(2,1)} %bitcast.9), channel_id=1, source_target_pairs={{0,16},{4,20},{8,24},{12,28},{16,0},{20,4},{24,8},{28,12},{1,17},{... | collective-permute-start | bytes 98312 | tf_op jit(solution)/shard_map/ppermute | solution.py:308
  4.8 0.8 %copy-start = (bf16[2,2,128,32]{2,3,1,0:T(8,128)(2,1)S(1)}, bf16[2,2,128,32]{2,3,1,0:T(8,128)(2,1)}, u32[]{:S(2)}) copy-start(bf16[2,2,128,32]{2,3,1,0:T(8,128)(2,1)} %param.5) | copy-start | bytes 98308
  5.6 0.7 %copy-start.1 = (bf16[4,16,16]{2,1,0:T(8,128)(2,1)S(1)}, bf16[4,16,16]{2,1,0:T(8,128)(2,1)}, u32[]{:S(2)}) copy-start(bf16[4,16,16]{2,1,0:T(8,128)(2,1)} %param.6) | copy-start | bytes 6148
  9.1 5.3 %collective-permute-start.1 = (bf16[256,128]{1,0:T(8,128)(2,1)S(1)}, bf16[256,128]{1,0:T(8,128)(2,1)S(1)}, u32[]{:S(2)}, u32[]{:S(2)}) collective-permute-start(bf16[256,128]{1,0:T(8,128)(2,1)S(1)} %constant_dynamic-update-slice_fusion.refs_0_), channel_id=1, source_target_pairs={{0,8},{4,12},{8,0},{12,4},{16,24},{20,28},{24,16},{28,20},{1,9},{5... | collective-permute-start | bytes 196616 | tf_op jit(solution)/shard_map/ppermute | solution.py:308
  14.4 5.3 %collective-permute-start.2 = (bf16[512,128]{1,0:T(8,128)(2,1)S(1)}, bf16[512,128]{1,0:T(8,128)(2,1)S(1)}, u32[]{:S(2)}, u32[]{:S(2)}) collective-permute-start(bf16[512,128]{1,0:T(8,128)(2,1)S(1)} %constant_dynamic-update-slice_fusion.2.refs_0_), channel_id=1, source_target_pairs={{0,4},{4,0},{8,12},{12,8},{16,20},{20,16},{24,28},{28,24},{1,5},{5... | collective-permute-start | bytes 393224 | tf_op jit(solution)/shard_map/ppermute | solution.py:308

commit v6 on v5

--- a/solution.py
+++ b/solution.py
@@ -6,7 +6,7 @@
 from jax.experimental.pallas import tpu as pltpu
 from jax.sharding import PartitionSpec as P
 
-TILE = 256
+TILE = 512
 STEP = 8
 
 

time: 32.7 us -> 32.7 us (level)
  no operation moved by 1% of the time
where the time goes in v6:
time: 32.7 us; the launch traced here: 32.4 us
  Pallas kernels  22.8 us (70%)
  starting transfers between devices  7.26 us (22%)
  local copies, waits for them, and re-layouts  1.51 us (5%)
  other arithmetic  0.79 us (2%)
    pallas_call x1, Pallas kernels, local(): pl.pallas_call(lambda *refs: image_kernel(chans, width, norm, masks, grou...  12.7 us
    pallas_call x2, Pallas kernels, local(): pl.pallas_call(lambda *refs, first=first: response_kernel(first, *refs),...  7.34 us
    ppermute x3, starting transfers between devices, local(): came = lax.ppermute(held, 'chan', [(j, j ^ bit) for j in range(count)])  7.26 us
    pallas_call x1, Pallas kernels, local(): pl.pallas_call(lambda *refs: table_kernel(cells, width, *refs), out_shape...  2.73 us
    unnamed x6, local copies, waits for them, and re-layouts  1.48 us
    add x1, other arithmetic, local(): (station_rows * cells + station_cols) * variants + kernel_offset  0.72 us
  transfers between devices with their start and end apart: 3, of which 0 were waited for; matrix products, arithmetic and copies ran while one was open for 2% of the time, Pallas kernels for 31%

profile of v6, /device:TPU:0, one launch (start us, length us, event | category | flops | bytes accessed | tf_op | source)
XLA Modules:
  0.0 32.4 jit_solution(15800649499088175973)
XLA Ops:
  0.0 4.0 %collective-permute-start = (bf16[128,128]{1,0:T(8,128)(2,1)}, bf16[128,128]{1,0:T(8,128)(2,1)S(1)}, u32[]{:S(2)}, u32[]{:S(2)}) collective-permute-start(bf16[128,128]{1,0:T(8,128)(2,1)} %bitcast.9), channel_id=1, source_target_pairs={{0,16},{4,20},{8,24},{12,28},{16,0},{20,4},{24,8},{28,12},{1,17},{... | collective-permute-start | bytes 98312 | tf_op jit(solution)/shard_map/ppermute | solution.py:308
  4.0 0.1 pad_add_fusion.refs_0_
  4.1 0.7 %multiply_add_fusion = s32[256]{0:T(256)S(1)} fusion(s32[256]{0:T(256)} %param.9, s32[256]{0:T(256)} %param.8, s32[256]{0:T(256)} %param.7), kind=kLoop, calls=%fused_computation.4 | loop fusion | flops 1024 | bytes 4096 | tf_op jit(solution)/shard_map/add | solution.py:279
  4.8 0.0 copy-start
  4.8 0.8 %copy-done = bf16[2,2,128,32]{2,3,1,0:T(8,128)(2,1)S(1)} copy-done((bf16[2,2,128,32]{2,3,1,0:T(8,128)(2,1)S(1)}, bf16[2,2,128,32]{2,3,1,0:T(8,128)(2,1)}, u32[]{:S(2)}) %copy-start) | copy-done | bytes 32792
  5.6 0.0 copy-start.1
  5.6 0.7 %copy-done.1 = bf16[4,16,16]{2,1,0:T(8,128)(2,1)S(1)} copy-done((bf16[4,16,16]{2,1,0:T(8,128)(2,1)S(1)}, bf16[4,16,16]{2,1,0:T(8,128)(2,1)}, u32[]{:S(2)}) %copy-start.1) | copy-done | bytes 2072
  6.3 2.7 %shard_map.55 = (f32[256,1536]{1,0:T(8,128)S(1)}, f32[256,1536]{1,0:T(8,128)S(1)}, s32[256,128]{1,0:T(8,128)S(1)}, f32[12,8,1536]{2,1,0:T(8,128)S(1)}, f32[12,8,...) custom-call(s32[3]{0:T(128)S(1)} %pad_add_fusion.refs_0_, ...), custom_call_target="tpu_custom_call" | custom-call | flops 39321600 | bytes 6291456 | tf_op jit(solution)/shard_map/pallas_call | solution.py:281
  9.1 0.0 collective-permute-done
  9.1 1.6 %collective-permute-start.1 = (bf16[256,128]{1,0:T(8,128)(2,1)S(1)}, bf16[256,128]{1,0:T(8,128)(2,1)S(1)}, u32[]{:S(2)}, u32[]{:S(2)}) collective-permute-start(bf16[256,128]{1,0:T(8,128)(2,1)S(1)} %constant_dynamic-update-slice_fusion.refs_0_), channel_id=1, source_target_pairs={{0,8},{4,12},{8,0},{12,4},{16,24},{20,28},{24,16},{28,20},{1,9},{5... | collective-permute-start | bytes 196616 | tf_op jit(solution)/shard_map/ppermute | solution.py:308
  10.7 3.7 %shard_map.56 = (bf16[6,512,1536]{2,1,0:T(8,128)(2,1)S(1)}, bf16[256,128]{1,0:T(8,128)(2,1)S(1)}) custom-call(bf16[256,128]{1,0:T(8,128)(2,1)S(1)} %constant_dynamic-update-slice_fusion.refs_0_, f32[256,1536]{1,0:T(8,128)S(1)} %get-tuple-element.20.refs_1_, f32[256,1536]{1,0:T(8,128)S(1)} %get-tuple-element.21.refs_2_, ...), custom_call_target="tpu_custom_call" | custom-call | flops 37748736 | bytes 9437184 | tf_op jit(solution)/shard_map/pallas_call | solution.py:313
  14.4 0.0 collective-permute-done.1
  14.4 1.6 %collective-permute-start.2 = (bf16[512,128]{1,0:T(8,128)(2,1)S(1)}, bf16[512,128]{1,0:T(8,128)(2,1)S(1)}, u32[]{:S(2)}, u32[]{:S(2)}) collective-permute-start(bf16[512,128]{1,0:T(8,128)(2,1)S(1)} %constant_dynamic-update-slice_fusion.2.refs_0_), channel_id=1, source_target_pairs={{0,4},{4,0},{8,12},{12,8},{16,20},{20,16},{24,28},{28,24},{1,5},{5... | collective-permute-start | bytes 393224 | tf_op jit(solution)/shard_map/ppermute | solution.py:308
  16.0 3.7 %shard_map.57 = (bf16[6,512,1536]{2,1,0:T(8,128)(2,1)S(1)}, bf16[512,128]{1,0:T(8,128)(2,1)S(1)}) custom-call(bf16[512,128]{1,0:T(8,128)(2,1)S(1)} %constant_dynamic-update-slice_fusion.2.refs_0_, f32[256,1536]{1,0:T(8,128)S(1)} %get-tuple-element.20.refs_1_, f32[256,1536]{1,0:T(8,128)S(1)} %get-tuple-element.21.refs_2_, ...), custom_call_target="tpu_custom_call" | custom-call | flops 37748736 | bytes 9437184 | tf_op jit(solution)/shard_map/pallas_call | solution.py:313
  19.7 0.0 collective-permute-done.2.refs_4_
  19.7 12.7 %shard_map.58 = f32[3,96,192]{2,1,0:T(8,128)} custom-call(s32[3]{0:T(128)S(1)} %pad_add_fusion.refs_0_, f32[12,256]{1,0:T(8,128)S(1)} %get-tuple-element.17.refs_1_, f32[12,256]{1,0:T(8,128)S(1)} %get-tuple-element.18.refs_2_, bf16[512,128]{1,0:T(8,128)(2,1)S(1)} %get-tuple-element.26.refs_3_, bf16[512,128]{1,0:T(8,128)(2,1)S(1)} %collective-permute-done.2.refs_4_, ...), custom_call_target="tpu_custom_call" | custom-call | flops 9663676416 | bytes 18874368 | tf_op jit(solution)/shard_map/pallas_call | solution.py:338
  (4 shorter events, 0.0 us)
Async XLA Ops:
  0.0 9.1 %collective-permute-start = (bf16[128,128]{1,0:T(8,128)(2,1)}, bf16[128,128]{1,0:T(8,128)(2,1)S(1)}, u32[]{:S(2)}, u32[]{:S(2)}) collective-permute-start(bf16[128,128]{1,0:T(8,128)(2,1)} %bitcast.9), channel_id=1, source_target_pairs={{0,16},{4,20},{8,24},{12,28},{16,0},{20,4},{24,8},{28,12},{1,17},{... | collective-permute-start | bytes 98312 | tf_op jit(solution)/shard_map/ppermute | solution.py:308
  4.8 0.8 %copy-start = (bf16[2,2,128,32]{2,3,1,0:T(8,128)(2,1)S(1)}, bf16[2,2,128,32]{2,3,1,0:T(8,128)(2,1)}, u32[]{:S(2)}) copy-start(bf16[2,2,128,32]{2,3,1,0:T(8,128)(2,1)} %param.5) | copy-start | bytes 98308
  5.6 0.7 %copy-start.1 = (bf16[4,16,16]{2,1,0:T(8,128)(2,1)S(1)}, bf16[4,16,16]{2,1,0:T(8,128)(2,1)}, u32[]{:S(2)}) copy-start(bf16[4,16,16]{2,1,0:T(8,128)(2,1)} %param.6) | copy-start | bytes 6148
  9.1 5.3 %collective-permute-start.1 = (bf16[256,128]{1,0:T(8,128)(2,1)S(1)}, bf16[256,128]{1,0:T(8,128)(2,1)S(1)}, u32[]{:S(2)}, u32[]{:S(2)}) collective-permute-start(bf16[256,128]{1,0:T(8,128)(2,1)S(1)} %constant_dynamic-update-slice_fusion.refs_0_), channel_id=1, source_target_pairs={{0,8},{4,12},{8,0},{12,4},{16,24},{20,28},{24,16},{28,20},{1,9},{5... | collective-permute-start | bytes 196616 | tf_op jit(solution)/shard_map/ppermute | solution.py:308
  14.4 5.3 %collective-permute-start.2 = (bf16[512,128]{1,0:T(8,128)(2,1)S(1)}, bf16[512,128]{1,0:T(8,128)(2,1)S(1)}, u32[]{:S(2)}, u32[]{:S(2)}) collective-permute-start(bf16[512,128]{1,0:T(8,128)(2,1)S(1)} %constant_dynamic-update-slice_fusion.2.refs_0_), channel_id=1, source_target_pairs={{0,4},{4,0},{8,12},{12,8},{16,20},{20,16},{24,28},{28,24},{1,5},{5... | collective-permute-start | bytes 393224 | tf_op jit(solution)/shard_map/ppermute | solution.py:308

commit v7 on v6

--- a/solution.py
+++ b/solution.py
@@ -50,13 +50,13 @@
 
 
 def table_kernel(
-    cells, width, place, held_in, joined_in, table_in,
-    base_re, base_im, pick, spread_re, spread_im, phase_re, phase_im, held, joined, table, arrived
+    cells, width, place, joined_in, table_in,
+    base_re, base_im, pick, spread_re, spread_im, phase_re, phase_im, joined, table, arrived
 ):
     copies = [
         pltpu.make_async_copy(source, target, arrived.at[n])
         for n, (source, target) in enumerate((
-            (joined_in, joined), (table_in, table), (held_in, held),
+            (joined_in, joined), (table_in, table),
         ))
     ]
     for copy in copies:
@@ -127,8 +127,7 @@
             target[:, o, :] = jnp.dot(left, right, preferred_element_type=jnp.float32)[:steps]
 
 
-def response_kernel(first, held, base_re, base_im, pick, spread_re, spread_im, response, kept):
-    kept[...] = held[...]
+def response_kernel(first, base_re, base_im, pick, spread_re, spread_im, response):
     parts, stations, lanes = response.shape[0], base_re.shape[0], base_re.shape[1]
     joint = 2 if parts % 2 == 0 else 1
 
@@ -266,15 +265,12 @@
     steps = height // STEP
     lanes = STEP * width
     planes = times * chans
-    place = jnp.stack([here, here * height, lax.axis_index("row") * width]).astype(jnp.int32)
+    place = jnp.stack([here * 0, here * height, lax.axis_index("row") * width]).astype(jnp.int32)
     vmem = pl.BlockSpec(memory_space=pltpu.VMEM)
     smem = pl.BlockSpec(memory_space=pltpu.SMEM)
     f32, bf16 = jnp.float32, jnp.bfloat16
     mib = 1024 * 1024
 
-    bits = []
-    while (1 << len(bits)) < count:
-        bits.append(count >> (len(bits) + 1))
     hbm = pl.BlockSpec(memory_space=pltpu.HBM)
     joined = ((station_rows * cells + station_cols) * variants + kernel_offset).reshape(1, stations)
     own = voltages.transpose(0, 1, 3, 2).reshape(2 * times * voltages.shape[3], chans)
@@ -288,46 +284,31 @@
             jax.ShapeDtypeStruct((steps, 8, lanes), f32),
             jax.ShapeDtypeStruct((steps, stations), f32),
             jax.ShapeDtypeStruct((steps, stations), f32),
-            jax.ShapeDtypeStruct(own.shape, bf16),
         ],
-        in_specs=[smem] + [hbm] * 3,
-        out_specs=[vmem] * 8,
+        in_specs=[smem] + [hbm] * 2,
+        out_specs=[vmem] * 7,
         scratch_shapes=[
             pltpu.VMEM((1, stations), jnp.int32),
             pltpu.VMEM((variants * taps, taps), bf16),
-            pltpu.SemaphoreType.DMA((3,)),
+            pltpu.SemaphoreType.DMA((2,)),
         ],
         compiler_params=pltpu.CompilerParams(vmem_limit_bytes=16 * mib),
         cost_estimate=pl.CostEstimate(flops=100 * stations * lanes, bytes_accessed=16 * stations * lanes, transcendentals=0),
-    )(place, own, joined, kernel_table.reshape(variants * taps, taps))
-
-    ahead = steps // 2
-    shares = [(0, steps - ahead), (steps - ahead, ahead)]
-    held, reach, responses = own, (0,), []
-    for cut, bit in enumerate(bits):
-        came = lax.ppermute(held, "chan", [(j, j ^ bit) for j in range(count)])
-        if cut == 0:
-            *tables, phase_re, phase_im, held = make_tables()
-        elif cut <= len(shares):
-            first, part = shares[cut - 1]
-            response, held = pl.pallas_call(
-                lambda *refs, first=first: response_kernel(first, *refs),
-                out_shape=[
-                    jax.ShapeDtypeStruct((part, 2 * stations, lanes), bf16),
-                    jax.ShapeDtypeStruct(held.shape, bf16),
-                ],
-                in_specs=[vmem] * 6,
-                out_specs=[vmem] * 2,
-                compiler_params=pltpu.CompilerParams(vmem_limit_bytes=16 * mib),
-                cost_estimate=pl.CostEstimate(
-                    flops=16 * part * stations * lanes, bytes_accessed=4 * part * stations * lanes, transcendentals=0
-                ),
-            )(held, *tables)
-            responses.append(response)
-        masks = [reach, tuple(m ^ bit for m in reach)]
-        reach = sum(masks, ())
-        blocks = [held, came]
-        held = jnp.concatenate(blocks)
+    )(place, joined, kernel_table.reshape(variants * taps, taps))
+
+    gathered = lax.all_gather(own, "chan", axis=0, tiled=True)
+    *tables, phase_re, phase_im = make_tables()
+    responses = [pl.pallas_call(
+        lambda *refs: response_kernel(0, *refs),
+        out_shape=jax.ShapeDtypeStruct((steps, 2 * stations, lanes), bf16),
+        in_specs=[vmem] * 5,
+        out_specs=vmem,
+        compiler_params=pltpu.CompilerParams(vmem_limit_bytes=16 * mib),
+        cost_estimate=pl.CostEstimate(
+            flops=16 * steps * stations * lanes, bytes_accessed=4 * steps * stations * lanes, transcendentals=0
+        ),
+    )(*tables)]
+    blocks, masks = [gathered], [tuple(range(count))]
 
     x = (2.0 * np.arange(chans) + 1.0 - chans) / chans
     norm = [

time: 32.7 us -> 57.3 us (1.75)
  blocking collectives: 0 us -> 32.5 us
  starting transfers between devices: 7.26 us -> 0 us
  local copies, waits for them, and re-layouts: 1.51 us -> 0.72 us
    all_gather x0 -> x1, blocking collectives: none -> 32.5 us  [local(): gathered = lax.all_gather(own, 'chan', axis=0, tiled=True)]
    ppermute x3 -> x0, starting transfers between devices: 7.26 us -> none  [local(): came = lax.ppermute(held, 'chan', [(j, j ^ bit) for j in range(count)])]
    unnamed x6 -> x4, local copies, waits for them, and re-layouts: 1.48 us -> 0.72 us
    pallas_call x2 -> x1, Pallas kernels: 7.34 us -> 7.3 us  [local(): pl.pallas_call(lambda *refs: response_kernel(0, *refs), out_shape=jax.Sha...]
  transfers between devices with their start and end apart: 3 -> 0, of which waited for: 0 -> 0; matrix products, arithmetic and copies ran while one was open for 2% -> 0% of each run, Pallas kernels for 31% -> 0%
where the time goes in v7:
time: 57.3 us; the launch traced here: 57 us
  blocking collectives  32.5 us (57%)
  Pallas kernels  22.9 us (40%)
  other arithmetic  0.79 us (1%)
  local copies, waits for them, and re-layouts  0.72 us (1%)
    all_gather x1, blocking collectives, local(): gathered = lax.all_gather(own, 'chan', axis=0, tiled=True)  32.5 us
    pallas_call x1, Pallas kernels, local(): pl.pallas_call(lambda *refs: image_kernel(chans, width, norm, masks, grou...  12.9 us
    pallas_call x1, Pallas kernels, local(): pl.pallas_call(lambda *refs: response_kernel(0, *refs), out_shape=jax.Sha...  7.3 us
    pallas_call x1, Pallas kernels, local(): pl.pallas_call(lambda *refs: table_kernel(cells, width, *refs), out_shape...  2.68 us

profile of v7, /device:TPU:0, one launch (start us, length us, event | category | flops | bytes accessed | tf_op | source)
XLA Modules:
  0.0 57.0 jit_solution(9745244271867716437)
XLA Ops:
  0.0 0.1 pad_add_fusion.refs_0_
  0.1 0.7 %multiply_add_fusion = s32[256]{0:T(256)S(1)} fusion(s32[256]{0:T(256)} %param.9, s32[256]{0:T(256)} %param.8, s32[256]{0:T(256)} %param.7), kind=kLoop, calls=%fused_computation | loop fusion | flops 1024 | bytes 4096 | tf_op jit(solution)/shard_map/add | solution.py:275
  0.8 0.0 copy-start
  0.8 0.7 %copy-done = bf16[4,16,16]{2,1,0:T(8,128)(2,1)S(1)} copy-done((bf16[4,16,16]{2,1,0:T(8,128)(2,1)S(1)}, bf16[4,16,16]{2,1,0:T(8,128)(2,1)}, u32[]{:S(2)}) %copy-start) | copy-done | bytes 2072
  1.5 2.7 %shard_map.55 = (f32[256,1536]{1,0:T(8,128)S(1)}, f32[256,1536]{1,0:T(8,128)S(1)}, s32[256,128]{1,0:T(8,128)S(1)}, f32[12,8,1536]{2,1,0:T(8,128)S(1)}, f32[12,8,...) custom-call(s32[3]{0:T(128)S(1)} %pad_add_fusion.refs_0_, s32[1,256]{1,0:T(1,128)S(1)} %bitcast.7, ...), custom_call_target="tpu_custom_call" | custom-call | flops 39321600 | bytes 6291456 | tf_op jit(solution)/shard_map/pallas_call | solution.py:277
  4.2 0.0 copy-start.1
  4.2 7.3 %shard_map.56.refs_4_ = bf16[12,512,1536]{2,1,0:T(8,128)(2,1)S(1)} custom-call(f32[256,1536]{1,0:T(8,128)S(1)} %get-tuple-element.14.refs_0_, f32[256,1536]{1,0:T(8,128)S(1)} %get-tuple-element.15.refs_1_, s32[256,128]{1,0:T(8,128)S(1)} %get-tuple-element.16.refs_2_, f32[12,8,1536]{2,1,0:T(8,128)S(1)} %get-tuple-element.17.refs_3_, ...), custom_call_target="tpu_custom_call" | custom-call | flops 75497472 | bytes 18874368 | tf_op jit(solution)/shard_map/pallas_call | solution.py:301
  11.5 0.0 copy-done.1
  11.5 32.5 %all_gather.3.refs_3_ = bf16[1024,128]{1,0:T(8,128)(2,1)S(1)} all-gather(bf16[128,128]{1,0:T(8,128)(2,1)S(1)} %bitcast.9), channel_id=1, replica_groups=mesh['chan'=8,'row'=4] {'chan'}, dimensions={0}, use_global_device_ids=true | all-gather | bytes 294912 | tf_op jit(solution)/shard_map/all_gather | solution.py:299
  44.1 12.9 %shard_map.57 = f32[3,96,192]{2,1,0:T(8,128)} custom-call(s32[3]{0:T(128)S(1)} %pad_add_fusion.refs_0_, f32[12,256]{1,0:T(8,128)S(1)} %get-tuple-element.12.refs_1_, f32[12,256]{1,0:T(8,128)S(1)} %get-tuple-element.13.refs_2_, bf16[1024,128]{1,0:T(8,128)(2,1)S(1)} %all_gather.3.refs_3_, bf16[12,512,1536]{2,1,0:T(8,128)(2,1)S(1)} %shard_map.56.refs_4_), custom_call_target="tpu_custom_call" | custom-call | flops 9663676416 | bytes 18874368 | tf_op jit(solution)/shard_map/pallas_call | solution.py:319
Async XLA Ops:
  0.8 0.7 %copy-start = (bf16[4,16,16]{2,1,0:T(8,128)(2,1)S(1)}, bf16[4,16,16]{2,1,0:T(8,128)(2,1)}, u32[]{:S(2)}) copy-start(bf16[4,16,16]{2,1,0:T(8,128)(2,1)} %param.6) | copy-start | bytes 6148
  4.2 7.3 %copy-start.1 = (bf16[2,2,128,32]{2,3,1,0:T(8,128)(2,1)S(1)}, bf16[2,2,128,32]{2,3,1,0:T(8,128)(2,1)}, u32[]{:S(2)}) copy-start(bf16[2,2,128,32]{2,3,1,0:T(8,128)(2,1)} %param.5) | copy-start | bytes 98308

commit v8 on v6

--- a/solution.py
+++ b/solution.py
@@ -7,6 +7,7 @@
 from jax.sharding import PartitionSpec as P
 
 TILE = 512
+ROWS = 256
 STEP = 8
 
 
@@ -50,26 +51,26 @@
 
 
 def table_kernel(
-    cells, width, place, held_in, joined_in, table_in,
-    base_re, base_im, pick, spread_re, spread_im, phase_re, phase_im, held, joined, table, arrived
+    cells, taps, variants, width, place, held_in, joined_in,
+    base_re, base_im, pick, spread_re, spread_im, phase_re, phase_im, held, joined, right_re, right_im, arrived
 ):
     copies = [
         pltpu.make_async_copy(source, target, arrived.at[n])
         for n, (source, target) in enumerate((
-            (joined_in, joined), (table_in, table), (held_in, held),
+            (joined_in, joined), (held_in, held),
         ))
     ]
     for copy in copies:
         copy.start()
     for copy in copies:
         copy.wait()
-    stations = joined.shape[1]
+    stations = base_re.shape[0]
     steps, lanes = spread_re.shape[0], spread_re.shape[2]
-    taps = table.shape[1]
-    variants = table.shape[0] // taps
     first_row = place[1].astype(jnp.float32)
     first_col = place[2].astype(jnp.float32)
-    code = joined[...].astype(jnp.float32)
+    kinds = variants * taps
+    kernels = joined[:kinds, :taps].astype(jnp.bfloat16)
+    code = jnp.concatenate([joined[kinds + n:kinds + n + 1, :] for n in range(stations // 128)], axis=1)
     rows = jnp.floor((code + 0.5) * (1.0 / (cells * variants)))
     code = code - rows * float(cells * variants)
     cols = jnp.floor((code + 0.5) * (1.0 / variants))
@@ -99,7 +100,6 @@
 
     down, across = down_across((taps, lanes), 0)
     tap = whole_of((taps, lanes), 0).astype(jnp.float32)
-    kernels = table[...]
 
     def over_columns(value):
         high, low = split(value)
@@ -109,22 +109,37 @@
 
     half_re, half_im = [over_columns(value) for value in wave(tap * across, cells)]
     turn_re, turn_im = wave(tap * down, cells)
-    tall = -(-steps // 16) * 16
-    lane = whole_of((tall, 6 * taps), 1)
-    start = first_row + float(STEP) * whole_of((tall, 6 * taps), 0).astype(jnp.float32)
-    left_re, left_im = wave(start * (lane % taps).astype(jnp.float32), cells)
-    value = jnp.where(lane // taps % 2 == 0, left_re, -left_im)
+    stride = 128
+    tall = -(-steps * 8 // 16) * 16
+    shape = (tall, stride)
+    row, lane = whole_of(shape, 0), whole_of(shape, 1)
+    start = first_row + float(STEP) * (row >> 3).astype(jnp.float32)
+    left_re, left_im = wave(start * (lane & (taps - 1)).astype(jnp.float32), cells)
+    value = jnp.where((lane & taps) == 0, left_re, -left_im)
     high, low = split(value)
-    left = jnp.where(lane // (2 * taps) == 1, low.astype(jnp.float32), high.astype(jnp.float32)).astype(jnp.bfloat16)
+    second = (lane >= 2 * taps) & (lane < 4 * taps)
+    value = jnp.where(second, low.astype(jnp.float32), high.astype(jnp.float32))
+    left = jnp.concatenate(
+        [jnp.where(((row & 7) == o) & (lane < 6 * taps), value, 0.0) for o in range(variants)], axis=1
+    ).astype(jnp.bfloat16)
+    rest = jnp.zeros((stride - 6 * taps, lanes), jnp.bfloat16)
     for o in range(variants):
         rows_o = slice(o * taps, (o + 1) * taps)
         real = turn_re * half_re[rows_o] - turn_im * half_im[rows_o]
         imag = turn_re * half_im[rows_o] + turn_im * half_re[rows_o]
-        for target, one, two in ((spread_re, real, imag), (spread_im, imag, -real)):
-            one_high, one_low = split(one)
-            two_high, two_low = split(two)
-            right = jnp.concatenate([one_high, two_high, one_high, two_high, one_low, two_low], axis=0)
-            target[:, o, :] = jnp.dot(left, right, preferred_element_type=jnp.float32)[:steps]
+        real_high, real_low = split(real)
+        imag_high, imag_low = split(imag)
+        for target, parts in (
+            (right_re, (real_high, imag_high, real_high, imag_high, real_low, imag_low)),
+            (right_im, (imag_high, -real_high, imag_high, -real_high, imag_low, -real_low)),
+        ):
+            for n, part in enumerate(parts):
+                target[o * stride + n * taps:o * stride + (n + 1) * taps, :] = part
+            target[o * stride + 6 * taps:(o + 1) * stride, :] = rest
+    for target, right in ((spread_re, right_re), (spread_im, right_im)):
+        spectra = jnp.dot(left, right[...], preferred_element_type=jnp.float32)
+        for q in range(steps):
+            target[q] = spectra[q * 8:q * 8 + 8]
 
 
 def response_kernel(first, held, base_re, base_im, pick, spread_re, spread_im, response, kept):
@@ -204,16 +219,20 @@
     top = chans // 8
     step_of = top + (2.0 * whole_of((8, TILE), 0).astype(jnp.float32) + 1.0 - chans) * 0.0625
 
-    def collect(q, tile, field):
-        s0, s1, s2 = None, None, None
-        for g in range(top):
+    def gather_sums(field, totals):
+        s0, s1, s2 = totals
+        for g in range(field.shape[0] // (2 * span)):
             for t in range(2 * times):
                 line = (g * 2 * times + t) * 8
                 part = field[line:line + 8, :]
                 total = part * part if t == 0 else total + part * part
-            s0 = total if g == 0 else s0 + total
-            s1 = s0 if g == 0 else s1 + s0
-            s2 = s1 if g == 0 else s2 + s1
+            s0 = s0 + total
+            s1 = s1 + s0
+            s2 = s2 + s1
+        return s0, s1, s2
+
+    def collect(q, tile, totals):
+        s0, s1, s2 = totals
         first = step_of * s0 - s1
         second = step_of * (step_of * s0 - 2.0 * s1) + (2.0 * s2 - s1)
         for k, value in enumerate((s0, first, second)):
@@ -225,12 +244,16 @@
 
     def chunk(q, turn, response, index):
         for n in range(tiles):
-            field = jnp.dot(
-                xs[turn][...], response[index, :, n * TILE:(n + 1) * TILE], preferred_element_type=jnp.float32
-            )
-            if n == 0:
-                prepare(jnp.minimum(q + 1, steps - 1), xs[1 - turn])
-            collect(q, n, field)
+            totals = (jnp.zeros((8, TILE), jnp.float32),) * 3
+            for m in range(planes * 2 // ROWS):
+                field = jnp.dot(
+                    xs[turn][m * ROWS:(m + 1) * ROWS, :], response[index, :, n * TILE:(n + 1) * TILE],
+                    preferred_element_type=jnp.float32,
+                )
+                if n == 0 and m == 0:
+                    prepare(jnp.minimum(q + 1, steps - 1), xs[1 - turn])
+                totals = gather_sums(field, totals)
+            collect(q, n, totals)
 
     base, turn = 0, 0
     for response in responses:
@@ -276,10 +299,12 @@
     while (1 << len(bits)) < count:
         bits.append(count >> (len(bits) + 1))
     hbm = pl.BlockSpec(memory_space=pltpu.HBM)
-    joined = ((station_rows * cells + station_cols) * variants + kernel_offset).reshape(1, stations)
+    code = ((station_rows * cells + station_cols) * variants + kernel_offset).astype(f32).reshape(stations // 128, 128)
+    shapes = kernel_table.reshape(variants * taps, taps).astype(f32)
+    joined = jnp.concatenate([jnp.pad(shapes, ((0, 0), (0, 128 - taps))), code])
     own = voltages.transpose(0, 1, 3, 2).reshape(2 * times * voltages.shape[3], chans)
     make_tables = lambda: pl.pallas_call(
-        lambda *refs: table_kernel(cells, width, *refs),
+        lambda *refs: table_kernel(cells, taps, variants, width, *refs),
         out_shape=[
             jax.ShapeDtypeStruct((stations, lanes), f32),
             jax.ShapeDtypeStruct((stations, lanes), f32),
@@ -290,16 +315,17 @@
             jax.ShapeDtypeStruct((steps, stations), f32),
             jax.ShapeDtypeStruct(own.shape, bf16),
         ],
-        in_specs=[smem] + [hbm] * 3,
+        in_specs=[smem] + [hbm] * 2,
         out_specs=[vmem] * 8,
         scratch_shapes=[
-            pltpu.VMEM((1, stations), jnp.int32),
-            pltpu.VMEM((variants * taps, taps), bf16),
-            pltpu.SemaphoreType.DMA((3,)),
+            pltpu.VMEM(joined.shape, f32),
+            pltpu.VMEM((variants * 128, lanes), bf16),
+            pltpu.VMEM((variants * 128, lanes), bf16),
+            pltpu.SemaphoreType.DMA((2,)),
         ],
         compiler_params=pltpu.CompilerParams(vmem_limit_bytes=16 * mib),
         cost_estimate=pl.CostEstimate(flops=100 * stations * lanes, bytes_accessed=16 * stations * lanes, transcendentals=0),
-    )(place, own, joined, kernel_table.reshape(variants * taps, taps))
+    )(place, own, joined)
 
     ahead = steps // 2
     shares = [(0, steps - ahead), (steps - ahead, ahead)]

time: 32.7 us -> 32.9 us (level)
  other arithmetic: 0.79 us -> 1.52 us
  local copies, waits for them, and re-layouts: 1.51 us -> 0.79 us
    pad x0 -> x1, other arithmetic: none -> 0.72 us  [local(): joined = jnp.concatenate([jnp.pad(shapes, ((0, 0), (0, 128 - taps))), code])]
    add x1 -> x0, other arithmetic: 0.72 us -> none  [local(): (station_rows * cells + station_cols) * variants + kernel_offset]
    reshape x0 -> x1, other arithmetic: none -> 0.72 us  [local(): ((station_rows * cells + station_cols) * variants + kernel_offset).astype...]
    unnamed x6 -> x4, local copies, waits for them, and re-layouts: 1.48 us -> 0.77 us
  transfers between devices with their start and end apart: 3 -> 3, of which waited for: 0 -> 0; matrix products, arithmetic and copies ran while one was open for 2% -> 5% of each run, Pallas kernels for 31% -> 31%
where the time goes in v8:
time: 32.9 us; the launch traced here: 32.7 us
  Pallas kernels  23 us (70%)
  starting transfers between devices  7.26 us (22%)
  other arithmetic  1.52 us (5%)
  local copies, waits for them, and re-layouts  0.79 us (2%)
    pallas_call x1, Pallas kernels, local(): pl.pallas_call(lambda *refs: image_kernel(chans, width, norm, masks, grou...  12.7 us
    pallas_call x2, Pallas kernels, local(): pl.pallas_call(lambda *refs, first=first: response_kernel(first, *refs),...  7.34 us
    ppermute x3, starting transfers between devices, local(): came = lax.ppermute(held, 'chan', [(j, j ^ bit) for j in range(count)])  7.26 us
    pallas_call x1, Pallas kernels, local(): pl.pallas_call(lambda *refs: table_kernel(cells, taps, variants, width, *...  2.93 us
    unnamed x4, local copies, waits for them, and re-layouts  0.77 us
    pad x1, other arithmetic, local(): joined = jnp.concatenate([jnp.pad(shapes, ((0, 0), (0, 128 - taps))), code])  0.72 us
    reshape x1, other arithmetic, local(): ((station_rows * cells + station_cols) * variants + kernel_offset).astype...  0.72 us
  transfers between devices with their start and end apart: 3, of which 0 were waited for; matrix products, arithmetic and copies ran while one was open for 5% of the time, Pallas kernels for 31%

profile of v8, /device:TPU:0, one launch (start us, length us, event | category | flops | bytes accessed | tf_op | source)
XLA Modules:
  0.0 32.7 jit_solution(12456434044346290520)
XLA Ops:
  0.0 4.0 %collective-permute-start = (bf16[128,128]{1,0:T(8,128)(2,1)}, bf16[128,128]{1,0:T(8,128)(2,1)S(1)}, u32[]{:S(2)}, u32[]{:S(2)}) collective-permute-start(bf16[128,128]{1,0:T(8,128)(2,1)} %bitcast.9), channel_id=1, source_target_pairs={{0,16},{4,20},{8,24},{12,28},{16,0},{20,4},{24,8},{28,12},{1,17},{... | collective-permute-start | bytes 98312 | tf_op jit(solution)/shard_map/ppermute | solution.py:334
  4.0 0.7 %pad_convert_fusion = f32[64,128]{1,0:T(8,128)S(1)} fusion(bf16[64,16]{1,0:T(8,128)(2,1)} %bitcast.11), kind=kLoop, calls=%fused_computation.1 | loop fusion | flops 8192 | bytes 34816 | tf_op jit(solution)/shard_map/jit(_pad)/pad | solution.py:304
  4.8 0.7 %convert_bitcast_fusion = f32[2,128]{1,0:T(2,128)S(1)} fusion(s32[256]{0:T(256)} %param.9, s32[256]{0:T(256)} %param.8, s32[256]{0:T(256)} %param.7), kind=kLoop, calls=%fused_computation.6 | loop fusion | flops 1280 | bytes 4096 | tf_op jit(solution)/shard_map/reshape | solution.py:302
  5.5 0.1 pad_add_fusion.refs_0_
  5.6 0.0 copy-start
  5.6 0.8 %copy-done = bf16[2,2,128,32]{2,3,1,0:T(8,128)(2,1)S(1)} copy-done((bf16[2,2,128,32]{2,3,1,0:T(8,128)(2,1)S(1)}, bf16[2,2,128,32]{2,3,1,0:T(8,128)(2,1)}, u32[]{:S(2)}) %copy-start) | copy-done | bytes 32792
  6.3 2.9 %shard_map.55 = (f32[256,1536]{1,0:T(8,128)S(1)}, f32[256,1536]{1,0:T(8,128)S(1)}, s32[256,128]{1,0:T(8,128)S(1)}, f32[12,8,1536]{2,1,0:T(8,128)S(1)}, f32[12,8,...) custom-call(s32[3]{0:T(128)S(1)} %pad_add_fusion.refs_0_, ...), custom_call_target="tpu_custom_call" | custom-call | flops 39321600 | bytes 6291456 | tf_op jit(solution)/shard_map/pallas_call | solution.py:306
  9.3 0.0 collective-permute-done
  9.3 1.6 %collective-permute-start.1 = (bf16[256,128]{1,0:T(8,128)(2,1)S(1)}, bf16[256,128]{1,0:T(8,128)(2,1)S(1)}, u32[]{:S(2)}, u32[]{:S(2)}) collective-permute-start(bf16[256,128]{1,0:T(8,128)(2,1)S(1)} %constant_dynamic-update-slice_fusion.refs_0_), channel_id=1, source_target_pairs={{0,8},{4,12},{8,0},{12,4},{16,24},{20,28},{24,16},{28,20},{1,9},{5... | collective-permute-start | bytes 196616 | tf_op jit(solution)/shard_map/ppermute | solution.py:334
  10.9 3.7 %shard_map.56 = (bf16[6,512,1536]{2,1,0:T(8,128)(2,1)S(1)}, bf16[256,128]{1,0:T(8,128)(2,1)S(1)}) custom-call(bf16[256,128]{1,0:T(8,128)(2,1)S(1)} %constant_dynamic-update-slice_fusion.refs_0_, f32[256,1536]{1,0:T(8,128)S(1)} %get-tuple-element.20.refs_1_, f32[256,1536]{1,0:T(8,128)S(1)} %get-tuple-element.21.refs_2_, ...), custom_call_target="tpu_custom_call" | custom-call | flops 37748736 | bytes 9437184 | tf_op jit(solution)/shard_map/pallas_call | solution.py:339
  14.6 0.0 collective-permute-done.1
  14.6 1.6 %collective-permute-start.2 = (bf16[512,128]{1,0:T(8,128)(2,1)S(1)}, bf16[512,128]{1,0:T(8,128)(2,1)S(1)}, u32[]{:S(2)}, u32[]{:S(2)}) collective-permute-start(bf16[512,128]{1,0:T(8,128)(2,1)S(1)} %constant_dynamic-update-slice_fusion.2.refs_0_), channel_id=1, source_target_pairs={{0,4},{4,0},{8,12},{12,8},{16,20},{20,16},{24,28},{28,24},{1,5},{5... | collective-permute-start | bytes 393224 | tf_op jit(solution)/shard_map/ppermute | solution.py:334
  16.2 3.7 %shard_map.57 = (bf16[6,512,1536]{2,1,0:T(8,128)(2,1)S(1)}, bf16[512,128]{1,0:T(8,128)(2,1)S(1)}) custom-call(bf16[512,128]{1,0:T(8,128)(2,1)S(1)} %constant_dynamic-update-slice_fusion.2.refs_0_, f32[256,1536]{1,0:T(8,128)S(1)} %get-tuple-element.20.refs_1_, f32[256,1536]{1,0:T(8,128)S(1)} %get-tuple-element.21.refs_2_, ...), custom_call_target="tpu_custom_call" | custom-call | flops 37748736 | bytes 9437184 | tf_op jit(solution)/shard_map/pallas_call | solution.py:339
  19.9 0.0 collective-permute-done.2.refs_4_
  19.9 12.7 %shard_map.58 = f32[3,96,192]{2,1,0:T(8,128)} custom-call(s32[3]{0:T(128)S(1)} %pad_add_fusion.refs_0_, f32[12,256]{1,0:T(8,128)S(1)} %get-tuple-element.17.refs_1_, f32[12,256]{1,0:T(8,128)S(1)} %get-tuple-element.18.refs_2_, bf16[512,128]{1,0:T(8,128)(2,1)S(1)} %get-tuple-element.26.refs_3_, bf16[512,128]{1,0:T(8,128)(2,1)S(1)} %collective-permute-done.2.refs_4_, ...), custom_call_target="tpu_custom_call" | custom-call | flops 9663676416 | bytes 18874368 | tf_op jit(solution)/shard_map/pallas_call | solution.py:364
  (5 shorter events, 0.0 us)
Async XLA Ops:
  0.0 9.3 %collective-permute-start = (bf16[128,128]{1,0:T(8,128)(2,1)}, bf16[128,128]{1,0:T(8,128)(2,1)S(1)}, u32[]{:S(2)}, u32[]{:S(2)}) collective-permute-start(bf16[128,128]{1,0:T(8,128)(2,1)} %bitcast.9), channel_id=1, source_target_pairs={{0,16},{4,20},{8,24},{12,28},{16,0},{20,4},{24,8},{28,12},{1,17},{... | collective-permute-start | bytes 98312 | tf_op jit(solution)/shard_map/ppermute | solution.py:334
  5.6 0.8 %copy-start = (bf16[2,2,128,32]{2,3,1,0:T(8,128)(2,1)S(1)}, bf16[2,2,128,32]{2,3,1,0:T(8,128)(2,1)}, u32[]{:S(2)}) copy-start(bf16[2,2,128,32]{2,3,1,0:T(8,128)(2,1)} %param.5) | copy-start | bytes 98308
  9.3 5.3 %collective-permute-start.1 = (bf16[256,128]{1,0:T(8,128)(2,1)S(1)}, bf16[256,128]{1,0:T(8,128)(2,1)S(1)}, u32[]{:S(2)}, u32[]{:S(2)}) collective-permute-start(bf16[256,128]{1,0:T(8,128)(2,1)S(1)} %constant_dynamic-update-slice_fusion.refs_0_), channel_id=1, source_target_pairs={{0,8},{4,12},{8,0},{12,4},{16,24},{20,28},{24,16},{28,20},{1,9},{5... | collective-permute-start | bytes 196616 | tf_op jit(solution)/shard_map/ppermute | solution.py:334
  14.6 5.3 %collective-permute-start.2 = (bf16[512,128]{1,0:T(8,128)(2,1)S(1)}, bf16[512,128]{1,0:T(8,128)(2,1)S(1)}, u32[]{:S(2)}, u32[]{:S(2)}) collective-permute-start(bf16[512,128]{1,0:T(8,128)(2,1)S(1)} %constant_dynamic-update-slice_fusion.2.refs_0_), channel_id=1, source_target_pairs={{0,4},{4,0},{8,12},{12,8},{16,20},{20,16},{24,28},{28,24},{1,5},{5... | collective-permute-start | bytes 393224 | tf_op jit(solution)/shard_map/ppermute | solution.py:334

commit v9 on v8

--- a/solution.py
+++ b/solution.py
@@ -7,7 +7,7 @@
 from jax.sharding import PartitionSpec as P
 
 TILE = 512
-ROWS = 256
+ROWS = 512
 STEP = 8
 
 
@@ -50,27 +50,31 @@
     return jnp.broadcast_to(values, (128, stations)).T
 
 
+def down_across(shape, start, width, first_col):
+    lane = whole_of(shape, 1) + start
+    down = jnp.zeros(shape, jnp.float32)
+    for p in range(1, STEP):
+        down = jnp.where(lane >= p * width, float(p), down)
+    return down, lane.astype(jnp.float32) - down * width + first_col
+
+
 def table_kernel(
-    cells, taps, variants, width, place, held_in, joined_in,
-    base_re, base_im, pick, spread_re, spread_im, phase_re, phase_im, held, joined, right_re, right_im, arrived
+    cells, variants, width, place, held_in, joined_in,
+    base_re, base_im, pick, phase_re, phase_im, held, joined, arrived
 ):
     copies = [
         pltpu.make_async_copy(source, target, arrived.at[n])
-        for n, (source, target) in enumerate((
-            (joined_in, joined), (held_in, held),
-        ))
+        for n, (source, target) in enumerate(((joined_in, joined), (held_in, held)))
     ]
     for copy in copies:
         copy.start()
     for copy in copies:
         copy.wait()
-    stations = base_re.shape[0]
-    steps, lanes = spread_re.shape[0], spread_re.shape[2]
+    stations, lanes = base_re.shape
+    steps = phase_re.shape[0]
     first_row = place[1].astype(jnp.float32)
     first_col = place[2].astype(jnp.float32)
-    kinds = variants * taps
-    kernels = joined[:kinds, :taps].astype(jnp.bfloat16)
-    code = jnp.concatenate([joined[kinds + n:kinds + n + 1, :] for n in range(stations // 128)], axis=1)
+    code = jnp.concatenate([joined[n:n + 1, :] for n in range(stations // 128)], axis=1)
     rows = jnp.floor((code + 0.5) * (1.0 / (cells * variants)))
     code = code - rows * float(cells * variants)
     cols = jnp.floor((code + 0.5) * (1.0 / variants))
@@ -79,26 +83,23 @@
     col_of = station_column(cols, stations)
     start = first_row + float(STEP) * whole_of((steps, stations), 0).astype(jnp.float32)
     phase_re[...], phase_im[...] = wave(start * rows, cells)
-
-    def down_across(shape, start):
-        lane = whole_of(shape, 1) + start
-        down = jnp.zeros(shape, jnp.float32)
-        for p in range(1, STEP):
-            down = jnp.where(lane >= p * width, float(p), down)
-        return down, lane.astype(jnp.float32) - down * width + first_col
-
     half = lanes // 2
     leap_re, leap_im = wave(row_of * float(STEP // 2), cells)
     for tile in range(half // 128):
         at = slice(tile * 128, (tile + 1) * 128)
         later = slice(half + tile * 128, half + (tile + 1) * 128)
-        down, across = down_across((stations, 128), tile * 128)
+        down, across = down_across((stations, 128), tile * 128, width, first_col)
         real, imag = wave(row_of * down + col_of * across, cells)
         base_re[:, at], base_im[:, at] = real, imag
         base_re[:, later] = real * leap_re - imag * leap_im
         base_im[:, later] = real * leap_im + imag * leap_re
 
-    down, across = down_across((taps, lanes), 0)
+
+def make_spectra(cells, taps, variants, width, place, table, spread_re, spread_im, right_re, right_im):
+    steps, lanes = spread_re.shape[0], spread_re.shape[2]
+    kernels = table[...]
+    first_row = place[1].astype(jnp.float32)
+    down, across = down_across((taps, lanes), 0, width, place[2].astype(jnp.float32))
     tap = whole_of((taps, lanes), 0).astype(jnp.float32)
 
     def over_columns(value):
@@ -142,27 +143,31 @@
             target[q] = spectra[q * 8:q * 8 + 8]
 
 
-def response_kernel(first, held, base_re, base_im, pick, spread_re, spread_im, response, kept):
-    kept[...] = held[...]
+def respond(first, base_re, base_im, pick, spread_re, spread_im, response, variants):
     parts, stations, lanes = response.shape[0], base_re.shape[0], base_re.shape[1]
     joint = 2 if parts % 2 == 0 else 1
 
     def some(i, carry):
         for tile in range(lanes // 128):
             at = slice(tile * 128, (tile + 1) * 128)
-            tables = [
-                (spread_re[first + joint * i + j, :, at], spread_im[first + joint * i + j, :, at]) for j in range(joint)
+            here = [first + joint * i + j for j in range(joint)]
+            tables = [spread_re[q, :, at] for q in here]
+            choices = [
+                [jnp.broadcast_to(spread_im[q, o:o + 1, at], (8, 128)) for o in range(variants)] for q in here
             ]
             for group in range(stations // 16):
                 made = [([], []) for j in range(joint)]
                 for half in range(2):
                     sub = slice(group * 16 + half * 8, group * 16 + half * 8 + 8)
                     index = pick[sub, :]
+                    chosen = [index == o for o in range(1, variants)]
                     br = base_re[sub, at]
                     bi = base_im[sub, at]
                     for j in range(joint):
-                        sr = jnp.take_along_axis(tables[j][0], index, axis=0)
-                        si = jnp.take_along_axis(tables[j][1], index, axis=0)
+                        sr = jnp.take_along_axis(tables[j], index, axis=0)
+                        si = choices[j][0]
+                        for o in range(1, variants):
+                            si = jnp.where(chosen[o - 1], choices[j][o], si)
                         made[j][0].append(br * sr - bi * si)
                         made[j][1].append(br * si + bi * sr)
                 pair = slice(group * 16, group * 16 + 16)
@@ -173,6 +178,20 @@
         return carry
 
     lax.fori_loop(0, parts // joint, some, 0)
+
+
+def first_kernel(
+    cells, taps, variants, width, place, held, table, base_re, base_im, pick,
+    response, kept, spread_re, spread_im, right_re, right_im
+):
+    kept[...] = held[...]
+    make_spectra(cells, taps, variants, width, place, table, spread_re, spread_im, right_re, right_im)
+    respond(0, base_re, base_im, pick, spread_re, spread_im, response, variants)
+
+
+def second_kernel(first, variants, held, base_re, base_im, pick, spread_re, spread_im, response, kept):
+    kept[...] = held[...]
+    respond(first, base_re, base_im, pick, spread_re, spread_im, response, variants)
 
 
 def image_kernel(
@@ -300,55 +319,57 @@
         bits.append(count >> (len(bits) + 1))
     hbm = pl.BlockSpec(memory_space=pltpu.HBM)
     code = ((station_rows * cells + station_cols) * variants + kernel_offset).astype(f32).reshape(stations // 128, 128)
-    shapes = kernel_table.reshape(variants * taps, taps).astype(f32)
-    joined = jnp.concatenate([jnp.pad(shapes, ((0, 0), (0, 128 - taps))), code])
+    shapes = kernel_table.reshape(variants * taps, taps)
     own = voltages.transpose(0, 1, 3, 2).reshape(2 * times * voltages.shape[3], chans)
     make_tables = lambda: pl.pallas_call(
-        lambda *refs: table_kernel(cells, taps, variants, width, *refs),
+        lambda *refs: table_kernel(cells, variants, width, *refs),
         out_shape=[
             jax.ShapeDtypeStruct((stations, lanes), f32),
             jax.ShapeDtypeStruct((stations, lanes), f32),
             jax.ShapeDtypeStruct((stations, 128), jnp.int32),
-            jax.ShapeDtypeStruct((steps, 8, lanes), f32),
-            jax.ShapeDtypeStruct((steps, 8, lanes), f32),
             jax.ShapeDtypeStruct((steps, stations), f32),
             jax.ShapeDtypeStruct((steps, stations), f32),
             jax.ShapeDtypeStruct(own.shape, bf16),
         ],
         in_specs=[smem] + [hbm] * 2,
-        out_specs=[vmem] * 8,
-        scratch_shapes=[
-            pltpu.VMEM(joined.shape, f32),
-            pltpu.VMEM((variants * 128, lanes), bf16),
-            pltpu.VMEM((variants * 128, lanes), bf16),
-            pltpu.SemaphoreType.DMA((2,)),
-        ],
+        out_specs=[vmem] * 6,
+        scratch_shapes=[pltpu.VMEM(code.shape, f32), pltpu.SemaphoreType.DMA((2,))],
         compiler_params=pltpu.CompilerParams(vmem_limit_bytes=16 * mib),
         cost_estimate=pl.CostEstimate(flops=100 * stations * lanes, bytes_accessed=16 * stations * lanes, transcendentals=0),
-    )(place, own, joined)
-
-    ahead = steps // 2
-    shares = [(0, steps - ahead), (steps - ahead, ahead)]
+    )(place, own, code)
+
+    early = max(1, steps // 3)
+    cost = lambda part: pl.CostEstimate(
+        flops=16 * part * stations * lanes, bytes_accessed=4 * part * stations * lanes, transcendentals=0
+    )
+    limit = pltpu.CompilerParams(vmem_limit_bytes=16 * mib)
+    made = lambda part: jax.ShapeDtypeStruct((part, 2 * stations, lanes), bf16)
     held, reach, responses = own, (0,), []
     for cut, bit in enumerate(bits):
         came = lax.ppermute(held, "chan", [(j, j ^ bit) for j in range(count)])
+        kept = jax.ShapeDtypeStruct(held.shape, bf16)
         if cut == 0:
-            *tables, phase_re, phase_im, held = make_tables()
-        elif cut <= len(shares):
-            first, part = shares[cut - 1]
+            *base, phase_re, phase_im, held = make_tables()
+        elif cut == 1:
+            response, held, *spread = pl.pallas_call(
+                lambda *refs: first_kernel(cells, taps, variants, width, *refs),
+                out_shape=[made(early), kept] + [jax.ShapeDtypeStruct((steps, 8, lanes), f32)] * 2,
+                in_specs=[smem] + [vmem] * 5,
+                out_specs=[vmem] * 4,
+                scratch_shapes=[pltpu.VMEM((variants * 128, lanes), bf16)] * 2,
+                compiler_params=limit,
+                cost_estimate=cost(early),
+            )(place, held, shapes, *base)
+            responses.append(response)
+        elif cut == 2:
             response, held = pl.pallas_call(
-                lambda *refs, first=first: response_kernel(first, *refs),
-                out_shape=[
-                    jax.ShapeDtypeStruct((part, 2 * stations, lanes), bf16),
-                    jax.ShapeDtypeStruct(held.shape, bf16),
-                ],
+                lambda *refs: second_kernel(early, variants, *refs),
+                out_shape=[made(steps - early), kept],
                 in_specs=[vmem] * 6,
                 out_specs=[vmem] * 2,
-                compiler_params=pltpu.CompilerParams(vmem_limit_bytes=16 * mib),
-                cost_estimate=pl.CostEstimate(
-                    flops=16 * part * stations * lanes, bytes_accessed=4 * part * stations * lanes, transcendentals=0
-                ),
-            )(held, *tables)
+                compiler_params=limit,
+                cost_estimate=cost(steps - early),
+            )(held, *base, *spread)
             responses.append(response)
         masks = [reach, tuple(m ^ bit for m in reach)]
         reach = sum(masks, ())

time: 32.9 us -> 35.9 us (1.091)
  Pallas kernels: 23 us -> 26 us
  other arithmetic: 1.52 us -> 0.79 us
  local copies, waits for them, and re-layouts: 0.79 us -> 1.51 us
    pallas_call x3, Pallas kernels: 10.3 us -> 13.2 us  [the longest x1 6.3 us: local(): pl.pallas_call(lambda *refs: second_kernel(early, variants, *refs), out_s...]
    pad x1 -> x0, other arithmetic: 0.72 us -> none  [local(): joined = jnp.concatenate([jnp.pad(shapes, ((0, 0), (0, 128 - taps))), code])]
    unnamed x4 -> x6, local copies, waits for them, and re-layouts: 0.77 us -> 1.48 us
  transfers between devices with their start and end apart: 3 -> 3, of which waited for: 0 -> 0; matrix products, arithmetic and copies ran while one was open for 5% -> 2% of each run, Pallas kernels for 31% -> 37%
where the time goes in v9:
time: 35.9 us; the launch traced here: 35.7 us
  Pallas kernels  26 us (72%)
  starting transfers between devices  7.26 us (20%)
  local copies, waits for them, and re-layouts  1.51 us (4%)
  other arithmetic  0.79 us (2%)
    pallas_call x1, Pallas kernels, local(): pl.pallas_call(lambda *refs: image_kernel(chans, width, norm, masks, grou...  12.9 us
    ppermute x3, starting transfers between devices, local(): came = lax.ppermute(held, 'chan', [(j, j ^ bit) for j in range(count)])  7.26 us
    pallas_call x1, Pallas kernels, local(): pl.pallas_call(lambda *refs: second_kernel(early, variants, *refs), out_s...  6.3 us
    pallas_call x1, Pallas kernels, local(): pl.pallas_call(lambda *refs: first_kernel(cells, taps, variants, width, *...  4.9 us
    pallas_call x1, Pallas kernels, local(): pl.pallas_call(lambda *refs: table_kernel(cells, variants, width, *refs),...  1.96 us
    unnamed x6, local copies, waits for them, and re-layouts  1.48 us
    reshape x1, other arithmetic, local(): ((station_rows * cells + station_cols) * variants + kernel_offset).astype...  0.72 us
  transfers between devices with their start and end apart: 3, of which 0 were waited for; matrix products, arithmetic and copies ran while one was open for 2% of the time, Pallas kernels for 37%

profile of v9, /device:TPU:0, one launch (start us, length us, event | category | flops | bytes accessed | tf_op | source)
XLA Modules:
  0.0 35.7 jit_solution(13464655077851409094)
XLA Ops:
  0.0 4.0 %collective-permute-start = (bf16[128,128]{1,0:T(8,128)(2,1)}, bf16[128,128]{1,0:T(8,128)(2,1)S(1)}, u32[]{:S(2)}, u32[]{:S(2)}) collective-permute-start(bf16[128,128]{1,0:T(8,128)(2,1)} %bitcast.10), channel_id=1, source_target_pairs={{0,16},{4,20},{8,24},{12,28},{16,0},{20,4},{24,8},{28,12},{1,17},{... | collective-permute-start | bytes 98312 | tf_op jit(solution)/shard_map/ppermute | solution.py:349
  4.0 0.1 pad_add_fusion.refs_0_
  4.1 0.7 %convert_bitcast_fusion.refs_2_ = f32[2,128]{1,0:T(2,128)S(1)} fusion(s32[256]{0:T(256)} %param.9, s32[256]{0:T(256)} %param.8, s32[256]{0:T(256)} %param.7), kind=kLoop, calls=%fused_computation.4 | loop fusion | flops 1280 | bytes 4096 | tf_op jit(solution)/shard_map/reshape | solution.py:321
  4.8 0.0 copy-start.1
  4.8 0.8 %copy-done.1 = bf16[2,2,128,32]{2,3,1,0:T(8,128)(2,1)S(1)} copy-done((bf16[2,2,128,32]{2,3,1,0:T(8,128)(2,1)S(1)}, bf16[2,2,128,32]{2,3,1,0:T(8,128)(2,1)}, u32[]{:S(2)}) %copy-start.1) | copy-done | bytes 32792
  5.6 2.0 %shard_map.55 = (f32[256,1536]{1,0:T(8,128)S(1)}, f32[256,1536]{1,0:T(8,128)S(1)}, s32[256,128]{1,0:T(8,128)S(1)}, f32[12,256]{1,0:T(8,128)S(1)}, f32[12,256]{1,0:T(8,128)S(1)}, /*index=5*/bf16[128,128]{1,0:T(8,128)(2,1)S(1)}) custom-call(s32[3]{0:T(128)S(1)} %pad_add_fusion.refs_0_, bf16[128,128]{1,0:T(8,128)(2,1)S(1)} %bitcast.11, ...), custom_call_target="tpu_custom_call" | custom-call | flops 39321600 | bytes 6291456 | tf_op jit(solution)/shard_map/pallas_call | solution.py:324
  7.6 0.0 collective-permute-done
  7.6 1.6 %collective-permute-start.1 = (bf16[256,128]{1,0:T(8,128)(2,1)S(1)}, bf16[256,128]{1,0:T(8,128)(2,1)S(1)}, u32[]{:S(2)}, u32[]{:S(2)}) collective-permute-start(bf16[256,128]{1,0:T(8,128)(2,1)S(1)} %constant_dynamic-update-slice_fusion.refs_1_), channel_id=1, source_target_pairs={{0,8},{4,12},{8,0},{12,4},{16,24},{20,28},{24,16},{28,20},{1,9},{5... | collective-permute-start | bytes 196616 | tf_op jit(solution)/shard_map/ppermute | solution.py:349
  9.2 0.0 copy-start
  9.2 0.7 %copy-done = bf16[4,16,16]{2,1,0:T(8,128)(2,1)S(1)} copy-done((bf16[4,16,16]{2,1,0:T(8,128)(2,1)S(1)}, bf16[4,16,16]{2,1,0:T(8,128)(2,1)}, u32[]{:S(2)}) %copy-start) | copy-done | bytes 2072
  10.0 4.9 %shard_map.56 = (bf16[4,512,1536]{2,1,0:T(8,128)(2,1)S(1)}, bf16[256,128]{1,0:T(8,128)(2,1)S(1)}, f32[12,8,1536]{2,1,0:T(8,128)S(1)}, f32[12,8,1536]{2,1,0:T(8,128)S(1)}) custom-call(s32[3]{0:T(128)S(1)} %pad_add_fusion.refs_0_, bf16[256,128]{1,0:T(8,128)(2,1)S(1)} %constant_dynamic-update-slice_fusion.refs_1_, bf16[64,16]{1,0:T(8,128)(2,1)S(1)} %bitcast.9, ...), custom_call_target="tpu_custom_call" | custom-call | flops 25165824 | bytes 6291456 | tf_op jit(solution)/shard_map/pallas_call | solution.py:354
  14.9 0.0 collective-permute-done.1
  14.9 1.6 %collective-permute-start.2 = (bf16[512,128]{1,0:T(8,128)(2,1)S(1)}, bf16[512,128]{1,0:T(8,128)(2,1)S(1)}, u32[]{:S(2)}, u32[]{:S(2)}) collective-permute-start(bf16[512,128]{1,0:T(8,128)(2,1)S(1)} %constant_dynamic-update-slice_fusion.2.refs_0_), channel_id=1, source_target_pairs={{0,4},{4,0},{8,12},{12,8},{16,20},{20,16},{24,28},{28,24},{1,5},{5... | collective-permute-start | bytes 393224 | tf_op jit(solution)/shard_map/ppermute | solution.py:349
  16.5 6.3 %shard_map.57 = (bf16[8,512,1536]{2,1,0:T(8,128)(2,1)S(1)}, bf16[512,128]{1,0:T(8,128)(2,1)S(1)}) custom-call(bf16[512,128]{1,0:T(8,128)(2,1)S(1)} %constant_dynamic-update-slice_fusion.2.refs_0_, f32[256,1536]{1,0:T(8,128)S(1)} %get-tuple-element.20.refs_3_.refs_1_, f32[256,1536]{1,0:T(8,128)S(1)} %get-tuple-element.21.refs_4_.refs_2_, ...), custom_call_target="tpu_custom_call" | custom-call | flops 50331648 | bytes 12582912 | tf_op jit(solution)/shard_map/pallas_call | solution.py:365
  22.8 0.0 collective-permute-done.2.refs_4_
  22.8 12.9 %shard_map.58 = f32[3,96,192]{2,1,0:T(8,128)} custom-call(s32[3]{0:T(128)S(1)} %pad_add_fusion.refs_0_, f32[12,256]{1,0:T(8,128)S(1)} %get-tuple-element.17.refs_1_, f32[12,256]{1,0:T(8,128)S(1)} %get-tuple-element.18.refs_2_, bf16[512,128]{1,0:T(8,128)(2,1)S(1)} %get-tuple-element.26.refs_3_, bf16[512,128]{1,0:T(8,128)(2,1)S(1)} %collective-permute-done.2.refs_4_, ...), custom_call_target="tpu_custom_call" | custom-call | flops 9663676416 | bytes 18874368 | tf_op jit(solution)/shard_map/pallas_call | solution.py:385
  (4 shorter events, 0.0 us)
Async XLA Ops:
  0.0 7.6 %collective-permute-start = (bf16[128,128]{1,0:T(8,128)(2,1)}, bf16[128,128]{1,0:T(8,128)(2,1)S(1)}, u32[]{:S(2)}, u32[]{:S(2)}) collective-permute-start(bf16[128,128]{1,0:T(8,128)(2,1)} %bitcast.10), channel_id=1, source_target_pairs={{0,16},{4,20},{8,24},{12,28},{16,0},{20,4},{24,8},{28,12},{1,17},{... | collective-permute-start | bytes 98312 | tf_op jit(solution)/shard_map/ppermute | solution.py:349
  4.8 0.8 %copy-start.1 = (bf16[2,2,128,32]{2,3,1,0:T(8,128)(2,1)S(1)}, bf16[2,2,128,32]{2,3,1,0:T(8,128)(2,1)}, u32[]{:S(2)}) copy-start(bf16[2,2,128,32]{2,3,1,0:T(8,128)(2,1)} %param.5) | copy-start | bytes 98308
  7.6 7.3 %collective-permute-start.1 = (bf16[256,128]{1,0:T(8,128)(2,1)S(1)}, bf16[256,128]{1,0:T(8,128)(2,1)S(1)}, u32[]{:S(2)}, u32[]{:S(2)}) collective-permute-start(bf16[256,128]{1,0:T(8,128)(2,1)S(1)} %constant_dynamic-update-slice_fusion.refs_1_), channel_id=1, source_target_pairs={{0,8},{4,12},{8,0},{12,4},{16,24},{20,28},{24,16},{28,20},{1,9},{5... | collective-permute-start | bytes 196616 | tf_op jit(solution)/shard_map/ppermute | solution.py:349
  9.2 0.7 %copy-start = (bf16[4,16,16]{2,1,0:T(8,128)(2,1)S(1)}, bf16[4,16,16]{2,1,0:T(8,128)(2,1)}, u32[]{:S(2)}) copy-start(bf16[4,16,16]{2,1,0:T(8,128)(2,1)} %param.6) | copy-start | bytes 6148
  14.9 7.9 %collective-permute-start.2 = (bf16[512,128]{1,0:T(8,128)(2,1)S(1)}, bf16[512,128]{1,0:T(8,128)(2,1)S(1)}, u32[]{:S(2)}, u32[]{:S(2)}) collective-permute-start(bf16[512,128]{1,0:T(8,128)(2,1)S(1)} %constant_dynamic-update-slice_fusion.2.refs_0_), channel_id=1, source_target_pairs={{0,4},{4,0},{8,12},{12,8},{16,20},{20,16},{24,28},{28,24},{1,5},{5... | collective-permute-start | bytes 393224 | tf_op jit(solution)/shard_map/ppermute | solution.py:349

commit v10 on v6

--- a/solution.py
+++ b/solution.py
@@ -10,7 +10,7 @@
 STEP = 8
 
 
-def wave_fit(terms=7):
+def wave_fit(terms=6):
     nodes = 0.125 + 0.125 * np.cos(np.pi * (np.arange(200) + 0.5) / 200)
     root = np.sqrt(nodes)
     fit = np.polynomial.polynomial.polyfit
@@ -86,16 +86,16 @@
             down = jnp.where(lane >= p * width, float(p), down)
         return down, lane.astype(jnp.float32) - down * width + first_col
 
-    half = lanes // 2
-    leap_re, leap_im = wave(row_of * float(STEP // 2), cells)
-    for tile in range(half // 128):
-        at = slice(tile * 128, (tile + 1) * 128)
-        later = slice(half + tile * 128, half + (tile + 1) * 128)
+    pace = lanes // STEP * 2
+    leaps = [wave(row_of * float(p), cells) for p in (2, 4)]
+    for tile in range(pace // 128):
         down, across = down_across((stations, 128), tile * 128)
-        real, imag = wave(row_of * down + col_of * across, cells)
-        base_re[:, at], base_im[:, at] = real, imag
-        base_re[:, later] = real * leap_re - imag * leap_im
-        base_im[:, later] = real * leap_im + imag * leap_re
+        near = [wave(row_of * down + col_of * across, cells)]
+        for leap_re, leap_im in leaps:
+            near += [(re * leap_re - im * leap_im, re * leap_im + im * leap_re) for re, im in near]
+        for p, (real, imag) in enumerate(near):
+            at = slice(p * pace + tile * 128, p * pace + (tile + 1) * 128)
+            base_re[:, at], base_im[:, at] = real, imag
 
     down, across = down_across((taps, lanes), 0)
     tap = whole_of((taps, lanes), 0).astype(jnp.float32)
@@ -180,7 +180,7 @@
     times = sheets // 2
     for sheet in range(sheets):
         target = volt_re if sheet < times else volt_im
-        facing = turned[sheet].T
+        facing = turned[sheet].astype(jnp.bfloat16).T.astype(jnp.float32)
         for g in range(chans // 8):
             at = (g * times + sheet % times) * 8
             target[at:at + 8, :] = facing[g * 8:g * 8 + 8]

time: 32.7 us -> 32.3 us (0.988)
  Pallas kernels: 22.8 us -> 22.4 us
  transfers between devices with their start and end apart: 3 -> 3, of which waited for: 0 -> 0; matrix products, arithmetic and copies ran while one was open for 2% -> 3% of each run, Pallas kernels for 31% -> 30%
where the time goes in v10:
time: 32.3 us; the launch traced here: 32.1 us
  Pallas kernels  22.4 us (69%)
  starting transfers between devices  7.26 us (22%)
  local copies, waits for them, and re-layouts  1.51 us (5%)
  other arithmetic  0.79 us (2%)
    pallas_call x1, Pallas kernels, local(): pl.pallas_call(lambda *refs: image_kernel(chans, width, norm, masks, grou...  12.7 us
    pallas_call x2, Pallas kernels, local(): pl.pallas_call(lambda *refs, first=first: response_kernel(first, *refs),...  7.34 us
    ppermute x3, starting transfers between devices, local(): came = lax.ppermute(held, 'chan', [(j, j ^ bit) for j in range(count)])  7.26 us
    pallas_call x1, Pallas kernels, local(): pl.pallas_call(lambda *refs: table_kernel(cells, width, *refs), out_shape...  2.42 us
    unnamed x6, local copies, waits for them, and re-layouts  1.48 us
    add x1, other arithmetic, local(): (station_rows * cells + station_cols) * variants + kernel_offset  0.72 us
  transfers between devices with their start and end apart: 3, of which 0 were waited for; matrix products, arithmetic and copies ran while one was open for 3% of the time, Pallas kernels for 30%

profile of v10, /device:TPU:0, one launch (start us, length us, event | category | flops | bytes accessed | tf_op | source)
XLA Modules:
  0.0 32.1 jit_solution(15998534138485124514)
XLA Ops:
  0.0 4.0 %collective-permute-start = (bf16[128,128]{1,0:T(8,128)(2,1)}, bf16[128,128]{1,0:T(8,128)(2,1)S(1)}, u32[]{:S(2)}, u32[]{:S(2)}) collective-permute-start(bf16[128,128]{1,0:T(8,128)(2,1)} %bitcast.9), channel_id=1, source_target_pairs={{0,16},{4,20},{8,24},{12,28},{16,0},{20,4},{24,8},{28,12},{1,17},{... | collective-permute-start | bytes 98312 | tf_op jit(solution)/shard_map/ppermute | solution.py:308
  4.0 0.1 pad_add_fusion.refs_0_
  4.1 0.7 %multiply_add_fusion = s32[256]{0:T(256)S(1)} fusion(s32[256]{0:T(256)} %param.9, s32[256]{0:T(256)} %param.8, s32[256]{0:T(256)} %param.7), kind=kLoop, calls=%fused_computation.4 | loop fusion | flops 1024 | bytes 4096 | tf_op jit(solution)/shard_map/add | solution.py:279
  4.8 0.0 copy-start
  4.8 0.8 %copy-done = bf16[2,2,128,32]{2,3,1,0:T(8,128)(2,1)S(1)} copy-done((bf16[2,2,128,32]{2,3,1,0:T(8,128)(2,1)S(1)}, bf16[2,2,128,32]{2,3,1,0:T(8,128)(2,1)}, u32[]{:S(2)}) %copy-start) | copy-done | bytes 32792
  5.6 0.0 copy-start.1
  5.6 0.7 %copy-done.1 = bf16[4,16,16]{2,1,0:T(8,128)(2,1)S(1)} copy-done((bf16[4,16,16]{2,1,0:T(8,128)(2,1)S(1)}, bf16[4,16,16]{2,1,0:T(8,128)(2,1)}, u32[]{:S(2)}) %copy-start.1) | copy-done | bytes 2072
  6.3 2.4 %shard_map.55 = (f32[256,1536]{1,0:T(8,128)S(1)}, f32[256,1536]{1,0:T(8,128)S(1)}, s32[256,128]{1,0:T(8,128)S(1)}, f32[12,8,1536]{2,1,0:T(8,128)S(1)}, f32[12,8,...) custom-call(s32[3]{0:T(128)S(1)} %pad_add_fusion.refs_0_, ...), custom_call_target="tpu_custom_call" | custom-call | flops 39321600 | bytes 6291456 | tf_op jit(solution)/shard_map/pallas_call | solution.py:281
  8.8 0.0 collective-permute-done
  8.8 1.6 %collective-permute-start.1 = (bf16[256,128]{1,0:T(8,128)(2,1)S(1)}, bf16[256,128]{1,0:T(8,128)(2,1)S(1)}, u32[]{:S(2)}, u32[]{:S(2)}) collective-permute-start(bf16[256,128]{1,0:T(8,128)(2,1)S(1)} %constant_dynamic-update-slice_fusion.refs_0_), channel_id=1, source_target_pairs={{0,8},{4,12},{8,0},{12,4},{16,24},{20,28},{24,16},{28,20},{1,9},{5... | collective-permute-start | bytes 196616 | tf_op jit(solution)/shard_map/ppermute | solution.py:308
  10.4 3.7 %shard_map.56 = (bf16[6,512,1536]{2,1,0:T(8,128)(2,1)S(1)}, bf16[256,128]{1,0:T(8,128)(2,1)S(1)}) custom-call(bf16[256,128]{1,0:T(8,128)(2,1)S(1)} %constant_dynamic-update-slice_fusion.refs_0_, f32[256,1536]{1,0:T(8,128)S(1)} %get-tuple-element.20.refs_1_, f32[256,1536]{1,0:T(8,128)S(1)} %get-tuple-element.21.refs_2_, ...), custom_call_target="tpu_custom_call" | custom-call | flops 37748736 | bytes 9437184 | tf_op jit(solution)/shard_map/pallas_call | solution.py:313
  14.1 0.0 collective-permute-done.1
  14.1 1.6 %collective-permute-start.2 = (bf16[512,128]{1,0:T(8,128)(2,1)S(1)}, bf16[512,128]{1,0:T(8,128)(2,1)S(1)}, u32[]{:S(2)}, u32[]{:S(2)}) collective-permute-start(bf16[512,128]{1,0:T(8,128)(2,1)S(1)} %constant_dynamic-update-slice_fusion.2.refs_0_), channel_id=1, source_target_pairs={{0,4},{4,0},{8,12},{12,8},{16,20},{20,16},{24,28},{28,24},{1,5},{5... | collective-permute-start | bytes 393224 | tf_op jit(solution)/shard_map/ppermute | solution.py:308
  15.7 3.7 %shard_map.57 = (bf16[6,512,1536]{2,1,0:T(8,128)(2,1)S(1)}, bf16[512,128]{1,0:T(8,128)(2,1)S(1)}) custom-call(bf16[512,128]{1,0:T(8,128)(2,1)S(1)} %constant_dynamic-update-slice_fusion.2.refs_0_, f32[256,1536]{1,0:T(8,128)S(1)} %get-tuple-element.20.refs_1_, f32[256,1536]{1,0:T(8,128)S(1)} %get-tuple-element.21.refs_2_, ...), custom_call_target="tpu_custom_call" | custom-call | flops 37748736 | bytes 9437184 | tf_op jit(solution)/shard_map/pallas_call | solution.py:313
  19.4 0.0 collective-permute-done.2.refs_4_
  19.4 12.7 %shard_map.58 = f32[3,96,192]{2,1,0:T(8,128)} custom-call(s32[3]{0:T(128)S(1)} %pad_add_fusion.refs_0_, f32[12,256]{1,0:T(8,128)S(1)} %get-tuple-element.17.refs_1_, f32[12,256]{1,0:T(8,128)S(1)} %get-tuple-element.18.refs_2_, bf16[512,128]{1,0:T(8,128)(2,1)S(1)} %get-tuple-element.26.refs_3_, bf16[512,128]{1,0:T(8,128)(2,1)S(1)} %collective-permute-done.2.refs_4_, ...), custom_call_target="tpu_custom_call" | custom-call | flops 9663676416 | bytes 18874368 | tf_op jit(solution)/shard_map/pallas_call | solution.py:338
  (4 shorter events, 0.0 us)
Async XLA Ops:
  0.0 8.8 %collective-permute-start = (bf16[128,128]{1,0:T(8,128)(2,1)}, bf16[128,128]{1,0:T(8,128)(2,1)S(1)}, u32[]{:S(2)}, u32[]{:S(2)}) collective-permute-start(bf16[128,128]{1,0:T(8,128)(2,1)} %bitcast.9), channel_id=1, source_target_pairs={{0,16},{4,20},{8,24},{12,28},{16,0},{20,4},{24,8},{28,12},{1,17},{... | collective-permute-start | bytes 98312 | tf_op jit(solution)/shard_map/ppermute | solution.py:308
  4.8 0.8 %copy-start = (bf16[2,2,128,32]{2,3,1,0:T(8,128)(2,1)S(1)}, bf16[2,2,128,32]{2,3,1,0:T(8,128)(2,1)}, u32[]{:S(2)}) copy-start(bf16[2,2,128,32]{2,3,1,0:T(8,128)(2,1)} %param.5) | copy-start | bytes 98308
  5.6 0.7 %copy-start.1 = (bf16[4,16,16]{2,1,0:T(8,128)(2,1)S(1)}, bf16[4,16,16]{2,1,0:T(8,128)(2,1)}, u32[]{:S(2)}) copy-start(bf16[4,16,16]{2,1,0:T(8,128)(2,1)} %param.6) | copy-start | bytes 6148
  8.8 5.3 %collective-permute-start.1 = (bf16[256,128]{1,0:T(8,128)(2,1)S(1)}, bf16[256,128]{1,0:T(8,128)(2,1)S(1)}, u32[]{:S(2)}, u32[]{:S(2)}) collective-permute-start(bf16[256,128]{1,0:T(8,128)(2,1)S(1)} %constant_dynamic-update-slice_fusion.refs_0_), channel_id=1, source_target_pairs={{0,8},{4,12},{8,0},{12,4},{16,24},{20,28},{24,16},{28,20},{1,9},{5... | collective-permute-start | bytes 196616 | tf_op jit(solution)/shard_map/ppermute | solution.py:308
  14.1 5.3 %collective-permute-start.2 = (bf16[512,128]{1,0:T(8,128)(2,1)S(1)}, bf16[512,128]{1,0:T(8,128)(2,1)S(1)}, u32[]{:S(2)}, u32[]{:S(2)}) collective-permute-start(bf16[512,128]{1,0:T(8,128)(2,1)S(1)} %constant_dynamic-update-slice_fusion.2.refs_0_), channel_id=1, source_target_pairs={{0,4},{4,0},{8,12},{12,8},{16,20},{20,16},{24,28},{28,24},{1,5},{5... | collective-permute-start | bytes 393224 | tf_op jit(solution)/shard_map/ppermute | solution.py:308

commit v11 on v10

--- a/solution.py
+++ b/solution.py
@@ -130,7 +130,7 @@
 def response_kernel(first, held, base_re, base_im, pick, spread_re, spread_im, response, kept):
     kept[...] = held[...]
     parts, stations, lanes = response.shape[0], base_re.shape[0], base_re.shape[1]
-    joint = 2 if parts % 2 == 0 else 1
+    joint = next(n for n in (3, 2, 1) if parts % n == 0)
 
     def some(i, carry):
         for tile in range(lanes // 128):

time: 32.3 us -> 31.9 us (0.988)
  Pallas kernels: 22.4 us -> 22 us
    pallas_call x2, Pallas kernels: 7.34 us -> 6.91 us  [local(): pl.pallas_call(lambda *refs, first=first: response_kernel(first, *refs),...]
  transfers between devices with their start and end apart: 3 -> 3, of which waited for: 0 -> 0; matrix products, arithmetic and copies ran while one was open for 3% -> 3% of each run, Pallas kernels for 30% -> 29%
where the time goes in v11:
time: 31.9 us; the launch traced here: 31.7 us
  Pallas kernels  22 us (69%)
  starting transfers between devices  7.26 us (23%)
  local copies, waits for them, and re-layouts  1.51 us (5%)
  other arithmetic  0.79 us (2%)
    pallas_call x1, Pallas kernels, local(): pl.pallas_call(lambda *refs: image_kernel(chans, width, norm, masks, grou...  12.7 us
    ppermute x3, starting transfers between devices, local(): came = lax.ppermute(held, 'chan', [(j, j ^ bit) for j in range(count)])  7.26 us
    pallas_call x2, Pallas kernels, local(): pl.pallas_call(lambda *refs, first=first: response_kernel(first, *refs),...  6.91 us
    pallas_call x1, Pallas kernels, local(): pl.pallas_call(lambda *refs: table_kernel(cells, width, *refs), out_shape...  2.42 us
    unnamed x6, local copies, waits for them, and re-layouts  1.48 us
    add x1, other arithmetic, local(): (station_rows * cells + station_cols) * variants + kernel_offset  0.72 us
  transfers between devices with their start and end apart: 3, of which 0 were waited for; matrix products, arithmetic and copies ran while one was open for 3% of the time, Pallas kernels for 29%

profile of v11, /device:TPU:0, one launch (start us, length us, event | category | flops | bytes accessed | tf_op | source)
XLA Modules:
  0.0 31.7 jit_solution(17881371794314608276)
XLA Ops:
  0.0 4.0 %collective-permute-start = (bf16[128,128]{1,0:T(8,128)(2,1)}, bf16[128,128]{1,0:T(8,128)(2,1)S(1)}, u32[]{:S(2)}, u32[]{:S(2)}) collective-permute-start(bf16[128,128]{1,0:T(8,128)(2,1)} %bitcast.9), channel_id=1, source_target_pairs={{0,16},{4,20},{8,24},{12,28},{16,0},{20,4},{24,8},{28,12},{1,17},{... | collective-permute-start | bytes 98312 | tf_op jit(solution)/shard_map/ppermute | solution.py:308
  4.0 0.1 pad_add_fusion.refs_0_
  4.1 0.7 %multiply_add_fusion = s32[256]{0:T(256)S(1)} fusion(s32[256]{0:T(256)} %param.9, s32[256]{0:T(256)} %param.8, s32[256]{0:T(256)} %param.7), kind=kLoop, calls=%fused_computation.4 | loop fusion | flops 1024 | bytes 4096 | tf_op jit(solution)/shard_map/add | solution.py:279
  4.8 0.0 copy-start
  4.8 0.8 %copy-done = bf16[2,2,128,32]{2,3,1,0:T(8,128)(2,1)S(1)} copy-done((bf16[2,2,128,32]{2,3,1,0:T(8,128)(2,1)S(1)}, bf16[2,2,128,32]{2,3,1,0:T(8,128)(2,1)}, u32[]{:S(2)}) %copy-start) | copy-done | bytes 32792
  5.6 0.0 copy-start.1
  5.6 0.7 %copy-done.1 = bf16[4,16,16]{2,1,0:T(8,128)(2,1)S(1)} copy-done((bf16[4,16,16]{2,1,0:T(8,128)(2,1)S(1)}, bf16[4,16,16]{2,1,0:T(8,128)(2,1)}, u32[]{:S(2)}) %copy-start.1) | copy-done | bytes 2072
  6.3 2.4 %shard_map.55 = (f32[256,1536]{1,0:T(8,128)S(1)}, f32[256,1536]{1,0:T(8,128)S(1)}, s32[256,128]{1,0:T(8,128)S(1)}, f32[12,8,1536]{2,1,0:T(8,128)S(1)}, f32[12,8,...) custom-call(s32[3]{0:T(128)S(1)} %pad_add_fusion.refs_0_, ...), custom_call_target="tpu_custom_call" | custom-call | flops 39321600 | bytes 6291456 | tf_op jit(solution)/shard_map/pallas_call | solution.py:281
  8.8 0.0 collective-permute-done
  8.8 1.6 %collective-permute-start.1 = (bf16[256,128]{1,0:T(8,128)(2,1)S(1)}, bf16[256,128]{1,0:T(8,128)(2,1)S(1)}, u32[]{:S(2)}, u32[]{:S(2)}) collective-permute-start(bf16[256,128]{1,0:T(8,128)(2,1)S(1)} %constant_dynamic-update-slice_fusion.refs_0_), channel_id=1, source_target_pairs={{0,8},{4,12},{8,0},{12,4},{16,24},{20,28},{24,16},{28,20},{1,9},{5... | collective-permute-start | bytes 196616 | tf_op jit(solution)/shard_map/ppermute | solution.py:308
  10.4 3.5 %shard_map.56 = (bf16[6,512,1536]{2,1,0:T(8,128)(2,1)S(1)}, bf16[256,128]{1,0:T(8,128)(2,1)S(1)}) custom-call(bf16[256,128]{1,0:T(8,128)(2,1)S(1)} %constant_dynamic-update-slice_fusion.refs_0_, f32[256,1536]{1,0:T(8,128)S(1)} %get-tuple-element.20.refs_1_, f32[256,1536]{1,0:T(8,128)S(1)} %get-tuple-element.21.refs_2_, ...), custom_call_target="tpu_custom_call" | custom-call | flops 37748736 | bytes 9437184 | tf_op jit(solution)/shard_map/pallas_call | solution.py:313
  13.9 0.0 collective-permute-done.1
  13.9 1.6 %collective-permute-start.2 = (bf16[512,128]{1,0:T(8,128)(2,1)S(1)}, bf16[512,128]{1,0:T(8,128)(2,1)S(1)}, u32[]{:S(2)}, u32[]{:S(2)}) collective-permute-start(bf16[512,128]{1,0:T(8,128)(2,1)S(1)} %constant_dynamic-update-slice_fusion.2.refs_0_), channel_id=1, source_target_pairs={{0,4},{4,0},{8,12},{12,8},{16,20},{20,16},{24,28},{28,24},{1,5},{5... | collective-permute-start | bytes 393224 | tf_op jit(solution)/shard_map/ppermute | solution.py:308
  15.5 3.5 %shard_map.57 = (bf16[6,512,1536]{2,1,0:T(8,128)(2,1)S(1)}, bf16[512,128]{1,0:T(8,128)(2,1)S(1)}) custom-call(bf16[512,128]{1,0:T(8,128)(2,1)S(1)} %constant_dynamic-update-slice_fusion.2.refs_0_, f32[256,1536]{1,0:T(8,128)S(1)} %get-tuple-element.20.refs_1_, f32[256,1536]{1,0:T(8,128)S(1)} %get-tuple-element.21.refs_2_, ...), custom_call_target="tpu_custom_call" | custom-call | flops 37748736 | bytes 9437184 | tf_op jit(solution)/shard_map/pallas_call | solution.py:313
  19.0 0.0 collective-permute-done.2.refs_4_
  19.0 12.7 %shard_map.58 = f32[3,96,192]{2,1,0:T(8,128)} custom-call(s32[3]{0:T(128)S(1)} %pad_add_fusion.refs_0_, f32[12,256]{1,0:T(8,128)S(1)} %get-tuple-element.17.refs_1_, f32[12,256]{1,0:T(8,128)S(1)} %get-tuple-element.18.refs_2_, bf16[512,128]{1,0:T(8,128)(2,1)S(1)} %get-tuple-element.26.refs_3_, bf16[512,128]{1,0:T(8,128)(2,1)S(1)} %collective-permute-done.2.refs_4_, ...), custom_call_target="tpu_custom_call" | custom-call | flops 9663676416 | bytes 18874368 | tf_op jit(solution)/shard_map/pallas_call | solution.py:338
  (4 shorter events, 0.0 us)
Async XLA Ops:
  0.0 8.8 %collective-permute-start = (bf16[128,128]{1,0:T(8,128)(2,1)}, bf16[128,128]{1,0:T(8,128)(2,1)S(1)}, u32[]{:S(2)}, u32[]{:S(2)}) collective-permute-start(bf16[128,128]{1,0:T(8,128)(2,1)} %bitcast.9), channel_id=1, source_target_pairs={{0,16},{4,20},{8,24},{12,28},{16,0},{20,4},{24,8},{28,12},{1,17},{... | collective-permute-start | bytes 98312 | tf_op jit(solution)/shard_map/ppermute | solution.py:308
  4.8 0.8 %copy-start = (bf16[2,2,128,32]{2,3,1,0:T(8,128)(2,1)S(1)}, bf16[2,2,128,32]{2,3,1,0:T(8,128)(2,1)}, u32[]{:S(2)}) copy-start(bf16[2,2,128,32]{2,3,1,0:T(8,128)(2,1)} %param.5) | copy-start | bytes 98308
  5.6 0.7 %copy-start.1 = (bf16[4,16,16]{2,1,0:T(8,128)(2,1)S(1)}, bf16[4,16,16]{2,1,0:T(8,128)(2,1)}, u32[]{:S(2)}) copy-start(bf16[4,16,16]{2,1,0:T(8,128)(2,1)} %param.6) | copy-start | bytes 6148
  8.8 5.1 %collective-permute-start.1 = (bf16[256,128]{1,0:T(8,128)(2,1)S(1)}, bf16[256,128]{1,0:T(8,128)(2,1)S(1)}, u32[]{:S(2)}, u32[]{:S(2)}) collective-permute-start(bf16[256,128]{1,0:T(8,128)(2,1)S(1)} %constant_dynamic-update-slice_fusion.refs_0_), channel_id=1, source_target_pairs={{0,8},{4,12},{8,0},{12,4},{16,24},{20,28},{24,16},{28,20},{1,9},{5... | collective-permute-start | bytes 196616 | tf_op jit(solution)/shard_map/ppermute | solution.py:308
  13.9 5.0 %collective-permute-start.2 = (bf16[512,128]{1,0:T(8,128)(2,1)S(1)}, bf16[512,128]{1,0:T(8,128)(2,1)S(1)}, u32[]{:S(2)}, u32[]{:S(2)}) collective-permute-start(bf16[512,128]{1,0:T(8,128)(2,1)S(1)} %constant_dynamic-update-slice_fusion.2.refs_0_), channel_id=1, source_target_pairs={{0,4},{4,0},{8,12},{12,8},{16,20},{20,16},{24,28},{28,24},{1,5},{5... | collective-permute-start | bytes 393224 | tf_op jit(solution)/shard_map/ppermute | solution.py:308
